TPU v7x, 32 devices: a whole 2x2x4 slice. The times are simulated.
32 devices in a mesh: pix: 8 (over z, y), ch: 4 (over x, core).
Axes of the slice: x: 2, y: 2, z: 4, core: 2. Of those that a mesh axis runs over, the one named last changes fastest.
Arguments:
- features: bfloat16 [25088, 1024], P('pix', 'ch'), may hold values from -6 to 6
- pad_mask: int32 [25088], P('pix'), may hold values from 0 to 1, as said below
- reduce_weight: bfloat16 [1024, 256], P(None, 'ch'), may hold values from -0.1875 to 0.1875
- spatial_weight: bfloat16 [3, 3, 256, 256], P(None, None, None, 'ch'), may hold values from -0.125 to 0.125
- expand_weight: bfloat16 [256, 1024], P('ch'), may hold values from -0.375 to 0.375
- gain_first: bfloat16 [256], P('ch'), may hold values from 0.25 to 1.75
- shift_first: bfloat16 [256], P('ch'), may hold values from -3 to 3
- gain_second: bfloat16 [256], P('ch'), may hold values from 0.25 to 1.75
- shift_second: bfloat16 [256], P('ch'), may hold values from -3 to 3
- gain_third: bfloat16 [1024], P('ch'), may hold values from 0.25 to 1.75
- shift_third: bfloat16 [1024], P('ch'), may hold values from -3 to 3
- out_cotangent: bfloat16 [25088, 1024], P('pix', 'ch'), may hold values from -6 to 6
Outputs:
- result: bfloat16 [25088, 1024], P('pix', 'ch')
- input_grad: bfloat16 [25088, 1024], P('pix', 'ch')
- reduce_grad: float32 [1024, 256], P(None, 'ch')
- spatial_grad: float32 [3, 3, 256, 256], P(None, None, None, 'ch')
- expand_grad: float32 [256, 1024], P('ch')
- gain_first_grad: float32 [256], P('ch')
- shift_first_grad: float32 [256], P('ch')
- gain_second_grad: float32 [256], P('ch')
- shift_second_grad: float32 [256], P('ch')
- gain_third_grad: float32 [1024], P('ch')
- shift_third_grad: float32 [1024], P('ch')
Inputs may be any that keep to these rules, and one draw needn't show every extreme that they name: `pad_mask`: 1 marks a pixel that holds picture, 0 one of padding; the share of padding differs from image to image.
All inputs are finite; a program needn't handle non-finite values.
Results may differ from a plain program's by a relative error of at most 0.0081.
Values may be sent and summed in bfloat16 or wider, within the bound.
A program may use at most 128 MiB of HBM per device.

v0:
```python
import jax
import jax.numpy as jnp
from jax import lax
from jax.sharding import PartitionSpec as P

SIDE = 14


EPS = 1e-05


def smooth_slope(values):
    logistic = jax.nn.sigmoid(values)
    return logistic * (1.0 + values * (1.0 - logistic))


def as_grid(row_data):
    images = row_data.shape[0] // (SIDE * SIDE)
    return row_data.reshape(images, SIDE, SIDE, row_data.shape[1])


def conv_forward(activations, kernel):
    output = lax.conv_general_dilated(
        as_grid(activations),
        kernel,
        (1, 1),
        "SAME",
        dimension_numbers=("NHWC", "HWIO", "NHWC"),
        preferred_element_type=jnp.float32,
    )
    return output.reshape(activations.shape[0], kernel.shape[3])


def conv_input_grad(gradient, kernel):
    flipped = jnp.flip(kernel, (0, 1)).transpose(0, 1, 3, 2)
    return conv_forward(gradient, flipped)


def row_contract(left, right):
    return lax.dot_general(
        left, right, (((0,), (0,)), ((), ())), preferred_element_type=jnp.float32
    )


def col_contract(left, right):
    return lax.dot_general(
        left, right, (((1,), (1,)), ((), ())), preferred_element_type=jnp.float32
    )


def conv_weight_grad(activations, gradient):
    padded = jnp.pad(as_grid(activations), ((0, 0), (1, 1), (1, 1), (0, 0)))
    kernel_taps = []
    for row_shift in range(3):
        for col_shift in range(3):
            window = padded[
                :, row_shift : row_shift + SIDE, col_shift : col_shift + SIDE, :
            ].reshape(activations.shape)
            kernel_taps.append(row_contract(window, gradient))
    return jnp.stack(kernel_taps).reshape(3, 3, activations.shape[1], gradient.shape[1])


def norm_forward(hidden, valid, gain, shift, local_count):
    totals = jnp.sum(valid * hidden, axis=0)
    squares = jnp.sum(valid * hidden * hidden, axis=0)
    totals, squares, counted = lax.psum((totals, squares, local_count), "pix")
    average = totals / counted
    scale = lax.rsqrt(squares / counted - average * average + EPS)
    normed = (hidden - average) * scale
    return (normed, valid * (gain * normed + shift), scale, counted)


def norm_backward(incoming, valid, normed, scale, gain, counted):
    shift_grad = jnp.sum(valid * incoming, axis=0)
    gain_grad = jnp.sum(valid * incoming * normed, axis=0)
    shift_grad, gain_grad = lax.psum((shift_grad, gain_grad), "pix")
    hidden_grad = valid * scale * gain * (incoming - (shift_grad + normed * gain_grad) / counted)
    return (hidden_grad.astype(jnp.bfloat16), gain_grad, shift_grad)


def body(
    features,
    pad_mask,
    reduce_weight,
    spatial_weight,
    expand_weight,
    gain_first,
    shift_first,
    gain_second,
    shift_second,
    gain_third,
    shift_third,
    out_cotangent,
):
    own_rows, own_cotangent, own_mask = (features, out_cotangent, pad_mask)
    params = (
        reduce_weight,
        spatial_weight,
        expand_weight,
        gain_first,
        shift_first,
        gain_second,
        shift_second,
        gain_third,
        shift_third,
    )
    full_input = lax.all_gather(features, "ch", axis=1, tiled=True)
    reducer, spatial, expander = (params[0], params[1], params[2])
    norm_params = [entry.astype(jnp.float32) for entry in params[3:]]
    valid = own_mask.astype(jnp.float32)[:, None]
    local_count = jnp.sum(valid)
    hidden_one = jnp.dot(full_input, reducer, preferred_element_type=jnp.float32)
    normed_one, affine_one, scale_one, counted = norm_forward(
        hidden_one, valid, norm_params[0], norm_params[1], local_count
    )
    active_one = jax.nn.silu(affine_one).astype(jnp.bfloat16)
    mid_input = lax.all_gather(active_one, "ch", axis=1, tiled=True)
    hidden_two = conv_forward(mid_input, spatial)
    normed_two, affine_two, scale_two, counted = norm_forward(
        hidden_two, valid, norm_params[2], norm_params[3], local_count
    )
    active_two = jax.nn.silu(affine_two).astype(jnp.bfloat16)
    hidden_three = lax.psum_scatter(
        jnp.dot(active_two, expander, preferred_element_type=jnp.float32),
        "ch",
        scatter_dimension=1,
        tiled=True,
    )
    normed_three, affine_three, scale_three, counted = norm_forward(
        hidden_three, valid, norm_params[4], norm_params[5], local_count
    )
    summed = affine_three + own_rows.astype(jnp.float32)
    output = jax.nn.silu(summed).astype(jnp.bfloat16)
    grad_sum = own_cotangent.astype(jnp.float32) * smooth_slope(summed)
    grad_three, third_gains, third_shifts = norm_backward(
        grad_sum, valid, normed_three, scale_three, norm_params[4], counted
    )
    grad_wide = lax.all_gather(grad_three, "ch", axis=1, tiled=True)
    expand_grad = row_contract(active_two, grad_wide)
    grad_active_two = col_contract(grad_wide, expander)
    grad_two, second_gains, second_shifts = norm_backward(
        grad_active_two * smooth_slope(affine_two),
        valid,
        normed_two,
        scale_two,
        norm_params[2],
        counted,
    )
    spatial_grad = conv_weight_grad(mid_input, grad_two)
    grad_active_one = lax.psum_scatter(
        conv_input_grad(grad_two, spatial), "ch", scatter_dimension=1, tiled=True
    )
    grad_one, first_gains, first_shifts = norm_backward(
        grad_active_one * smooth_slope(affine_one),
        valid,
        normed_one,
        scale_one,
        norm_params[0],
        counted,
    )
    reduce_grad = row_contract(full_input, grad_one)
    stat_grads = (first_gains, first_shifts, second_gains, second_shifts, third_gains, third_shifts)
    input_term = lax.psum_scatter(
        col_contract(grad_one, reducer), "ch", scatter_dimension=1, tiled=True
    )
    input_grad = (input_term + grad_sum).astype(jnp.bfloat16)
    reduce_grad, spatial_grad, expand_grad = lax.psum(
        (reduce_grad, spatial_grad, expand_grad), "pix"
    )
    return (output, input_grad, reduce_grad, spatial_grad, expand_grad) + stat_grads


def solution(mesh):
    placed = (
        P("pix", "ch"),
        P("pix"),
        P(None, "ch"),
        P(None, None, None, "ch"),
        P("ch", None),
        P("ch"),
        P("ch"),
        P("ch"),
        P("ch"),
        P("ch"),
        P("ch"),
        P("pix", "ch"),
    )
    return jax.shard_map(
        body,
        mesh=mesh,
        in_specs=placed,
        out_specs=(
            P("pix", "ch"),
            P("pix", "ch"),
            P(None, "ch"),
            P(None, None, None, "ch"),
            P("ch", None),
            P("ch"),
            P("ch"),
            P("ch"),
            P("ch"),
            P("ch"),
            P("ch"),
        ),
        check_vma=False,
    )
```

profile of v0, /device:TPU:0, one launch (start us, length us, event | category | flops | bytes accessed | tf_op | source)
XLA Modules:
  0.0 649.8 jit_solution(11745651363895318443)
XLA Ops:
  11.3 48.9 %all-gather.4.cloned.1.call-done = bf16[3136,1024]{1,0:T(8,128)(2,1)} async-done(((bf16[3136,256]{1,0:T(8,128)(2,1)}), bf16[3136,1024]{1,0:T(8,128)(2,1)}) %all-gather.4.cloned.1.call-update) | async-done | bytes 6422544 | tf_op jit(solution)/shard_map/all_gather | solution.py:107
  60.3 5.0 fusion.13
  65.3 22.1 %all-reduce.6 = (f32[64]{0:T(128)S(1)}, f32[]{:T(128)}, f32[64]{0:T(128)S(1)}) all-reduce(f32[64]{0:T(128)S(1)} %get-tuple-element.22, f32[]{:T(128)} %convert_reduce_fusion, f32[64]{0:T(128)S(1)} %get-tuple-element.21), channel_id=1, replica_groups=mesh['pix'=8,'ch'=4] {'pix'}, use_global_device_ids=true, to_apply=%region_1.0 | all-reduce | flops 129 | bytes 1032 | tf_op jit(solution)/shard_map/psum | solution.py:66
  89.7 16.1 %all-gather.6.cloned.1.call-done = bf16[3136,256]{0,1:T(8,128)(2,1)} async-done(((bf16[3136,64]{0,1:T(8,128)(2,1)}), bf16[3136,256]{0,1:T(8,128)(2,1)}) %all-gather.6.cloned.1.call-update) | async-done | bytes 1605648 | tf_op jit(solution)/shard_map/all_gather | solution.py:117
  105.8 3.7 copy.27
  111.9 4.3 fusion.1
  119.9 21.4 %all-reduce.5 = (f32[64]{0:T(128)S(1)}, f32[64]{0:T(128)S(1)}) all-reduce(f32[64]{0:T(128)S(1)} %get-tuple-element.16, f32[64]{0:T(128)S(1)} %get-tuple-element.15), channel_id=1, replica_groups=mesh['pix'=8,'ch'=4] {'pix'}, use_global_device_ids=true, to_apply=%region_7.8 | all-reduce | flops 128 | bytes 1024 | tf_op jit(solution)/shard_map/psum | solution.py:66
  142.0 6.6 %fusion.17 = f32[3136,1024]{1,0:T(8,128)} fusion(bf16[64,1024]{1,0:T(8,128)(2,1)S(1)} %copy-done.21, f32[3136,64]{0,1:T(8,128)S(1)} %copy.31, f32[64]{0:T(128)S(1)} %convert_element_type.56, f32[64]{0:T(128)S(1)} %get-tuple-element.43, f32[64]{0:T(128)S(1)} %get-tuple-element.44, f32[64]{0:T(128)S(1)} %convert_element_type.52, ...), kind=kOutput, calls=%fused_computation.76 | convolution fusion | flops 413048832 | bytes 13792512 | tf_op jit(solution)/shard_map/dot_general | solution.py:124
  150.4 95.5 %reduce-scatter.4.cloned.1.call-done = f32[3136,256]{1,0:T(8,128)} async-done(((f32[3136,1024]{1,0:T(8,128)}), f32[3136,256]{1,0:T(8,128)}) %reduce-scatter.4.cloned.1.call-update) | async-done | bytes 3211280 | tf_op jit(solution)/shard_map/reduce_scatter | solution.py:123
  248.8 22.1 %all-reduce.4 = (f32[256]{0:T(256)}, f32[256]{0:T(256)}) all-reduce(f32[256]{0:T(256)S(1)} %get-tuple-element.14, f32[256]{0:T(256)S(1)} %get-tuple-element.13), channel_id=1, replica_groups=mesh['pix'=8,'ch'=4] {'pix'}, use_global_device_ids=true, to_apply=%region_12.13 | all-reduce | flops 512 | bytes 4096 | tf_op jit(solution)/shard_map/psum | solution.py:66
  272.3 6.2 multiply_reduce_fusion.2
  278.5 17.8 %all-reduce.3 = (f32[256]{0:T(256)}, f32[256]{0:T(256)}) all-reduce(f32[256]{0:T(256)} %get-tuple-element.12, f32[256]{0:T(256)} %get-tuple-element.11), channel_id=1, replica_groups=mesh['pix'=8,'ch'=4] {'pix'}, use_global_device_ids=true, to_apply=%region_18.19 | all-reduce | flops 512 | bytes 4096 | tf_op jit(solution)/shard_map/psum | solution.py:76
  296.3 4.5 multiply_convert_fusion
  300.9 45.9 %all-gather.8.cloned.1.call-done = bf16[3136,1024]{1,0:T(8,128)(2,1)} async-done(((bf16[3136,256]{1,0:T(8,128)(2,1)}), bf16[3136,1024]{1,0:T(8,128)(2,1)}) %all-gather.8.cloned.1.call-update) | async-done | bytes 6422544 | tf_op jit(solution)/shard_map/all_gather | solution.py:138
  346.7 5.3 multiply_reduce_fusion.8
  352.0 21.4 %all-reduce.2 = (f32[64]{0:T(128)S(1)}, f32[64]{0:T(128)S(1)}) all-reduce(f32[64]{0:T(128)S(1)} %get-tuple-element.20, f32[64]{0:T(128)S(1)} %get-tuple-element.19), channel_id=1, replica_groups=mesh['pix'=8,'ch'=4] {'pix'}, use_global_device_ids=true, to_apply=%region_22.23 | all-reduce | flops 128 | bytes 1024 | tf_op jit(solution)/shard_map/psum | solution.py:76
  376.6 3.7 copy.34
  380.3 4.6 reshape.94
  384.9 4.7 copy.35
  389.8 35.2 %reduce-scatter.6.cloned.1.call-done = f32[3136,64]{0,1:T(8,128)} async-done(((f32[3136,256]{0,1:T(8,128)}), f32[3136,64]{0,1:T(8,128)}) %reduce-scatter.6.cloned.1.call-update) | async-done | bytes 802832 | tf_op jit(solution)/shard_map/reduce_scatter | solution.py:150
  426.8 21.6 %all-reduce.1 = (f32[64]{0:T(128)S(1)}, f32[64]{0:T(128)S(1)}) all-reduce(f32[64]{0:T(128)S(1)} %get-tuple-element.18, f32[64]{0:T(128)S(1)} %get-tuple-element.17), channel_id=1, replica_groups=mesh['pix'=8,'ch'=4] {'pix'}, use_global_device_ids=true, to_apply=%region_27.28 | all-reduce | flops 128 | bytes 1024 | tf_op jit(solution)/shard_map/psum | solution.py:76
  448.4 7.3 %fusion.18 = f32[3136,1024]{1,0:T(8,128)} fusion(bf16[1024,64]{0,1:T(8,128)(2,1)S(1)} %copy-done.20, f32[3136,64]{0,1:T(8,128)S(1)} %get-tuple-element.39, f32[3136,64]{0,1:T(8,128)S(1)} %copy-done.5, f32[64]{0:T(128)S(1)} %get-tuple-element.64, f32[64]{0:T(128)S(1)} %get-tuple-element.65, f32[]{:T(128)} %get-tuple-element.34, ...), kind=kOutput, calls=%fused_computation.77 | convolution fusion | flops 413048832 | bytes 14595588 | tf_op jit(solution)/shard_map/dot_general | solution.py:46
  455.7 14.6 %pad_slice_fusion = (bf16[16,14,14,256]{3,2,1,0:T(8,128)(2,1)}, bf16[16,14,14,256]{3,2,1,0:T(8,128)(2,1)}, bf16[16,14,14,256]{3,2,1,0:T(8,128)(2,1)}, bf16[16,14...) fusion(bf16[16,14,14,256]{3,2,1,0:T(8,128)(2,1)} %copy-done.9), kind=kLoop, calls=%fused_computation.18 | loop fusion | bytes 14450688 | tf_op jit(solution)/shard_map/slice | solution.py:56
  470.3 3.7 reshape.102
  474.1 3.6 reshape.96
  477.7 3.7 reshape.97
  481.4 3.7 reshape.98
  485.1 3.6 reshape.99
  492.4 3.7 reshape.101
  508.7 5.5 fusion.16
  517.4 35.6 %reduce-scatter.8.cloned.1.call-done = f32[3136,256]{1,0:T(8,128)} async-done(((f32[3136,1024]{1,0:T(8,128)}), f32[3136,256]{1,0:T(8,128)}) %reduce-scatter.8.cloned.1.call-update) | async-done | bytes 3211280 | tf_op jit(solution)/shard_map/reduce_scatter | solution.py:163
  556.4 81.3 %all-reduce.10.cloned.1.call-done = (f32[1024,64]{0,1:T(8,128)}, f32[3,3,256,64]{2,3,1,0:T(8,128)}, f32[64,1024]{1,0:T(8,128)}) async-done(((f32[1024,64]{0,1:T(8,128)}, f32[3,3,256,64]{2,3,1,0:T(8,128)}, f32[64,1024]{1,0:T(8,128)}), (f32[1024,64]{0,1:T(8,128)}, f32[3,3,256,64]{2,3,1,0:T(8,128)}, f32[64,1024]{1,0:T(8,128)})) %all-reduce.10.cloned.1.call-update) | async-done | bytes 1114128 | tf_op jit(solution)/shard_map/psum | solution.py:167
  (127 shorter events, 52.4 us)
Async XLA Ops:
  7.2 104.7 %copy-start = (bf16[3,3,256,64]{2,3,1,0:T(8,128)(2,1)S(1)}, bf16[3,3,256,64]{2,3,1,0:T(8,128)(2,1)}, u32[]{:S(2)}) copy-start(bf16[3,3,256,64]{2,3,1,0:T(8,128)(2,1)} %param.15) | copy-start | bytes 884740
  7.2 53.1 %all-gather.4.cloned.1.call-start = ((), (), s32[]{:S(2)}) async-start(), calls=%async_computation.3 | async-start | bytes 8028160 | tf_op jit(solution)/shard_map/all_gather | solution.py:107
  7.9 97.8 %all-gather.6.cloned.1.call-start = ((), (), s32[]{:S(2)}) async-start(), calls=%async_computation.4 | async-start | bytes 2048000 | tf_op jit(solution)/shard_map/all_gather | solution.py:117
  9.3 78.8 %copy-start.26 = (f32[64]{0:T(128)}, f32[64]{0:T(128)S(1)}, u32[]{:S(2)}) copy-start(f32[64]{0:T(128)S(1)} %convert_element_type.54) | copy-start | bytes 772
  11.3 78.1 %copy-start.30 = (bf16[64]{0:T(256)(128)(2,1)S(1)}, bf16[64]{0:T(256)(128)(2,1)}, u32[]{:S(2)}) copy-start(bf16[64]{0:T(256)(128)(2,1)} %param.19) | copy-start | bytes 388
  11.3 78.1 %copy-start.31 = (bf16[64]{0:T(256)(128)(2,1)S(1)}, bf16[64]{0:T(256)(128)(2,1)}, u32[]{:S(2)}) copy-start(bf16[64]{0:T(256)(128)(2,1)} %param.20) | copy-start | bytes 388
  65.3 44.1 %copy-start.4 = (f32[3136,64]{0,1:T(8,128)}, f32[3136,64]{0,1:T(8,128)S(1)}, u32[]{:S(2)}) copy-start(f32[3136,64]{0,1:T(8,128)S(1)} %get-tuple-element.56) | copy-start | bytes 2408452
  89.2 156.6 %reduce-scatter.4.cloned.1.call-start = ((), (), s32[]{:S(2)}) async-start(), calls=%async_computation.5 | async-start | bytes 16056320 | tf_op jit(solution)/shard_map/reduce_scatter | solution.py:123
  89.5 52.5 %copy-start.22 = (f32[64]{0:T(128)}, f32[64]{0:T(128)S(1)}, u32[]{:S(2)}) copy-start(f32[64]{0:T(128)S(1)} %convert_element_type.56) | copy-start | bytes 772
  111.9 4.3 copy-start.9
  116.7 25.3 %copy-start.21 = (bf16[64,1024]{1,0:T(8,128)(2,1)S(1)}, bf16[64,1024]{1,0:T(8,128)(2,1)}, u32[]{:S(2)}) copy-start(bf16[64,1024]{1,0:T(8,128)(2,1)} %param.16) | copy-start | bytes 393220
  119.9 28.7 %copy-start.7 = (f32[3136,64]{0,1:T(8,128)}, f32[3136,64]{0,1:T(8,128)S(1)}, u32[]{:S(2)}) copy-start(f32[3136,64]{0,1:T(8,128)S(1)} %copy.31) | copy-start | bytes 2408452
  148.6 198.1 %all-gather.8.cloned.1.call-start = ((), (), s32[]{:S(2)}) async-start(), calls=%async_computation.6 | async-start | bytes 8028160 | tf_op jit(solution)/shard_map/all_gather | solution.py:138
  245.9 26.4 %copy-start.2 = (f32[3136,256]{1,0:T(8,128)S(1)}, f32[3136,256]{1,0:T(8,128)}, u32[]{:S(2)}) copy-start(f32[3136,256]{1,0:T(8,128)} %reduce-scatter.4.cloned.1.call-done) | copy-start | bytes 9633796
  300.8 72.6 %copy-start.8 = (f32[3136,64]{0,1:T(8,128)S(1)}, f32[3136,64]{0,1:T(8,128)}, u32[]{:S(2)}) copy-start(f32[3136,64]{0,1:T(8,128)} %copy-done.7) | copy-start | bytes 2408452
  300.8 124.1 %reduce-scatter.6.cloned.1.call-start = ((), (), s32[]{:S(2)}) async-start(), calls=%async_computation.7 | async-start | bytes 4096000 | tf_op jit(solution)/shard_map/reduce_scatter | solution.py:150
  389.7 35.3 %copy-start.5 = (f32[3136,64]{0,1:T(8,128)S(1)}, f32[3136,64]{0,1:T(8,128)}, u32[]{:S(2)}) copy-start(f32[3136,64]{0,1:T(8,128)} %copy-done.4) | copy-start | bytes 2408452
  389.7 35.3 %copy-start.27 = (f32[64]{0:T(128)S(1)}, f32[64]{0:T(128)}, u32[]{:S(2)}) copy-start(f32[64]{0:T(128)} %copy-done.26) | copy-start | bytes 772
  389.7 58.7 %copy-start.20 = (bf16[1024,64]{0,1:T(8,128)(2,1)S(1)}, bf16[1024,64]{0,1:T(8,128)(2,1)}, u32[]{:S(2)}) copy-start(bf16[1024,64]{0,1:T(8,128)(2,1)} %param.14) | copy-start | bytes 393220
  389.7 163.2 %reduce-scatter.8.cloned.1.call-start = ((), (), s32[]{:S(2)}) async-start(), calls=%async_computation.8 | async-start | bytes 16056320 | tf_op jit(solution)/shard_map/reduce_scatter | solution.py:163
  426.8 28.9 %copy-start.17 = (f32[3136,64]{0,1:T(8,128)}, f32[3136,64]{0,1:T(8,128)S(1)}, u32[]{:S(2)}) copy-start(f32[3136,64]{0,1:T(8,128)S(1)} %get-tuple-element.39) | copy-start | bytes 2408452
  448.4 65.8 %copy-start.24 = (f32[64]{0:T(128)}, f32[64]{0:T(128)S(1)}, u32[]{:S(2)}) copy-start(f32[64]{0:T(128)S(1)} %get-tuple-element.64) | copy-start | bytes 772
  448.4 65.8 %copy-start.25 = (f32[64]{0:T(128)}, f32[64]{0:T(128)S(1)}, u32[]{:S(2)}) copy-start(f32[64]{0:T(128)S(1)} %get-tuple-element.65) | copy-start | bytes 772
  455.7 182.0 %all-reduce.10.cloned.1.call-start = ((), (), s32[]{:S(2)}) async-start(), calls=%async_computation.9 | async-start | bytes 2228224 | tf_op jit(solution)/shard_map/psum | solution.py:167
  499.8 3.9 copy-start.16
  507.3 6.9 %slice-start = ((s8[6422528]{0:T(1024)(128)(4,1)}), s8[4194304]{0:T(1024)(128)(4,1)S(1)}, s32[]{:S(2)}) async-start(s8[6422528]{0:T(1024)(128)(4,1)} %bitcast.67), calls=%async_computation.10 | async-start | bytes 8388608
  508.6 5.6 copy-start.19
  508.7 5.6 copy-start.6
  508.7 5.6 slice-start.1
  508.7 5.6 copy-start.18
  514.2 38.7 %copy-start.3 = (f32[3136,256]{1,0:T(8,128)S(1)}, f32[3136,256]{1,0:T(8,128)}, u32[]{:S(2)}) copy-start(f32[3136,256]{1,0:T(8,128)} %get-tuple-element.40) | copy-start | bytes 9633796
  552.9 90.0 %copy-start.1 = (bf16[3,3,256,64]{2,3,1,0:T(8,128)(2,1)S(1)}, bf16[3,3,256,64]{2,3,1,0:T(8,128)(2,1)}, u32[]{:S(2)}) copy-start(bf16[3,3,256,64]{2,3,1,0:T(8,128)(2,1)} %param.15) | copy-start | bytes 884740
  (11 other events, 17.3 us)
Sparse Core Ops, SparseCore 0:
  9.6 50.6 all-gather.3
  89.4 16.3 all-gather.5
  148.8 97.0 reduce-scatter.3
  300.9 45.7 all-gather.7
  389.8 35.0 reduce-scatter.5
  455.8 97.0 reduce-scatter.7
  557.8 79.8 all-reduce.9
where the time goes:
time: 651 us; the launch traced here: 650 us
  waiting for transfers between devices  359 us (55%)
  blocking collectives  126 us (19%)
  local copies, waits for them, and re-layouts  75.6 us (12%)
  matrix products  45.5 us (7%)
  other arithmetic  28.3 us (4%)
  between operations  14.6 us (2%)
    reduce_scatter x1, waiting for transfers between devices, body(): lax.psum_scatter(jnp.dot(active_two, expander, preferred_element_type=jnp...  95.5 us
    psum x1, waiting for transfers between devices, body(): lax.psum((reduce_grad, spatial_grad, expand_grad), 'pix')  81.3 us
    psum x3, blocking collectives, norm_forward(): totals, squares, counted = lax.psum((totals, squares, local_count), 'pix')  65.5 us
    psum x3, blocking collectives, norm_backward(): shift_grad, gain_grad = lax.psum((shift_grad, gain_grad), 'pix')  60.8 us
    all_gather x1, waiting for transfers between devices, body(): full_input = lax.all_gather(features, 'ch', axis=1, tiled=True)  48.9 us
    all_gather x1, waiting for transfers between devices, body(): grad_wide = lax.all_gather(grad_three, 'ch', axis=1, tiled=True)  45.9 us
    reduce_scatter x1, waiting for transfers between devices, body(): lax.psum_scatter(col_contract(grad_one, reducer), 'ch', scatter_dimension...  35.6 us
    reduce_scatter x1, waiting for transfers between devices, body(): lax.psum_scatter(conv_input_grad(grad_two, spatial), 'ch', scatter_dimens...  35.2 us
  transfers between devices with their start and end apart: 7, of which 7 were waited for; matrix products, arithmetic and copies ran while one was open for 10% of the time, Pallas kernels for 0%

commit v1 on v0

v1 whole, which is shorter than its diff:
```python
import functools

import jax
import jax.numpy as jnp
from jax import lax
from jax.experimental import pallas as pl
from jax.experimental.pallas import tpu as pltpu
from jax.sharding import PartitionSpec as P

SIDE = 14
EPS = 1e-05
MESH = pl.DeviceIdType.MESH
F32 = jnp.float32
BF16 = jnp.bfloat16

ROWS = 112
OWN = 7
BOTH = 14
IMAGES = 4
PAD = 16
FLAT = IMAGES * PAD * PAD
EDGE = 8


def mm(a, b):
    return jnp.dot(a, b, preferred_element_type=F32)


def mm_nt(a, b):
    return lax.dot_general(a, b, (((1,), (1,)), ((), ())), preferred_element_type=F32)


def mm_tn(a, b):
    return lax.dot_general(a, b, (((0,), (0,)), ((), ())), preferred_element_type=F32)


def logistic(v):
    return 0.5 * jnp.tanh(0.5 * v) + 0.5


def fold8(v):
    return jnp.sum(v.reshape(v.shape[0] // 8, 8, v.shape[1]), axis=0)


def fold1(v):
    return jnp.sum(v, axis=0, keepdims=True)


def spread(v, lanes):
    return jnp.concatenate([v] * (lanes // 128), axis=1)


def kernel(
    n_pix,
    n_ch,
    feat,
    cot,
    mask,
    w1_in,
    w2_in,
    w3_in,
    params,
    res_out,
    ig_out,
    rg_out,
    sg_out,
    eg_out,
    st_out,
    F,
    C,
    V,
    w1v,
    w2v,
    w1t_own,
    W1T,
    W2T,
    W3,
    pk,
    sbuf,
    rbuf,
    h1s,
    h1r,
    H1,
    h1b,
    h1o,
    D1,
    comp,
    P0,
    PC,
    Q,
    padded,
    H2,
    h2s,
    h2r,
    A2,
    D2,
    H3,
    GS,
    RES,
    G3,
    E2,
    e2s,
    e2r,
    E1,
    e1s,
    e1r,
    G1,
    acc_w,
    acc_s,
    wp,
    wc,
    wa,
    wr,
    wh,
    wf,
    wfin,
    sp,
    sc,
    sa,
    sr,
    sh,
    sf,
    sx,
    sfin,
    ld_sem,
    fx_send,
    fx_recv,
    w_send,
    w_recv,
    ar_send,
    ar_recv,
    x_send,
    x_recv,
    out_sem,
    o_send,
    o_recv,
    g_send,
    g_recv,
):
    me_p, me_c = lax.axis_index("pix"), lax.axis_index("ch")
    hi, lo = me_c // 2, lax.rem(me_c, 2)
    n_lo = min(n_pix, 8)
    n_hi = n_pix // n_lo
    g_hi, g_lo = me_p // n_lo, lax.rem(me_p, n_lo)
    across = (me_p, (1 - hi) * 2 + lo)
    beside = (me_p, hi * 2 + 1 - lo)
    n_all = n_pix * n_ch

    def remote(src, dst, send, recv, device):
        return pltpu.make_async_remote_copy(
            src_ref=src, dst_ref=dst, send_sem=send, recv_sem=recv, device_id=device, device_id_type=MESH
        )

    def local(src, dst, sem):
        return pltpu.make_async_copy(src, dst, sem)

    mine, theirs = lo * BOTH, (1 - lo) * BOTH
    part0, part1 = hi * OWN, (1 - hi) * OWN

    w1_load = local(w1_in, w1v, ld_sem.at[0])
    w2_load = local(w2_in, w2v, ld_sem.at[1])
    f_load = [
        local(feat.at[pl.ds(mine + part, OWN)], F.at[lo, pl.ds(OWN * s, OWN)], ld_sem.at[2 + s])
        for s, part in enumerate((part0, part1))
    ]
    c_load = [
        local(cot.at[pl.ds(mine + part, OWN)], C.at[lo, pl.ds(OWN * s, OWN)], ld_sem.at[4 + s])
        for s, part in enumerate((part0, part1))
    ]
    w3_load = local(w3_in.at[:, pl.ds(pl.multiple_of(hi * 512, 512), 512)], W3.at[me_c], ld_sem.at[6])
    w1_load.start()
    f_load[1].start()
    f_load[0].start()
    w2_load.start()
    w3_load.start()
    c_load[0].start()
    c_load[1].start()

    barrier = pltpu.get_barrier_semaphore()

    def greet(t, carry):
        q = lax.rem(me_p * n_ch + me_c + t, n_all)
        pl.semaphore_signal(barrier, inc=1, device_id=(q // n_ch, lax.rem(q, n_ch)), device_id_type=MESH)
        return carry

    lax.fori_loop(1, n_all, greet, 0)

    eye = (
        lax.broadcasted_iota(jnp.int32, (64, 64), 0) == lax.broadcasted_iota(jnp.int32, (64, 64), 1)
    ).astype(BF16)
    w1_load.wait()
    w1t = mm_nt(eye, w1v[...]).astype(BF16)
    w1t_own[0] = w1t[:, 0:512]
    w1t_own[1] = w1t[:, 512:1024]
    W1T[me_c] = w1t_own[hi]

    vec = params[...]
    vec8 = jnp.broadcast_to(vec[:, 0:256], (8, 256)).astype(BF16)
    row_i = lax.broadcasted_iota(jnp.int32, (256, 256), 0)
    col_i = lax.broadcasted_iota(jnp.int32, (256, 256), 1)
    pk_rows = []
    for k in range(4):
        sel = (row_i - 64 * k == col_i - 64 * me_c) & (row_i >= 64 * k) & (row_i < 64 * k + 64)
        pk_rows.append(mm(vec8, sel.astype(BF16))[0:1])
    pk_rows += [vec[:, 256:512], vec[:, 512:768], jnp.zeros((2, 256), F32)]
    pk[me_c] = jnp.concatenate(pk_rows, axis=0)

    pl.semaphore_wait(barrier, n_all - 1)

    fx = [
        remote(
            feat.at[pl.ds(theirs + part, OWN)], F.at[lo, pl.ds(OWN * s, OWN)], fx_send.at[s], fx_recv.at[s], beside
        )
        for s, part in enumerate((part0, part1))
    ]
    cx = [
        remote(
            cot.at[pl.ds(theirs + part, OWN)], C.at[lo, pl.ds(OWN * s, OWN)], fx_send.at[2 + s], fx_recv.at[2 + s], beside
        )
        for s, part in enumerate((part0, part1))
    ]
    others = []
    for t in range(1, n_ch):
        q = lax.rem(me_c + t, n_ch)
        others.append((t - 1, (me_p, q), q // 2))
    w1x = [remote(w1t_own.at[h], W1T.at[me_c], w_send.at[t], w_recv.at[me_c], dev) for t, dev, h in others]
    pkx = [remote(pk.at[me_c], pk.at[me_c], w_send.at[4 + t], w_recv.at[4 + me_c], dev) for t, dev, h in others]
    w3x = [
        remote(
            w3_in.at[:, pl.ds(pl.multiple_of(h * 512, 512), 512)],
            W3.at[me_c],
            w_send.at[8 + t],
            w_recv.at[8 + me_c],
            dev,
        )
        for t, dev, h in others
    ]
    for cp in w1x:
        cp.start()
    fx[1].start()
    fx[0].start()
    for cp in pkx:
        cp.start()

    diag = lax.broadcasted_iota(jnp.int32, (ROWS, ROWS), 0) == lax.broadcasted_iota(jnp.int32, (ROWS, ROWS), 1)
    ones = jnp.ones((ROWS, 128), BF16)

    def put_mask(t, carry):
        at = mine + jnp.where(t < OWN, part0 + t, part1 + t - OWN)
        row = mask[pl.ds(at, 1), :]
        V[t] = mm(jnp.where(diag, row, 0.0).astype(BF16), ones)
        return carry

    lax.fori_loop(0, BOTH, put_mask, 0)

    w2_load.wait()
    for r in range(3):
        W2T[me_c, :, 768 * r : 768 * (r + 1)] = mm_nt(eye, w2v[768 * r : 768 * (r + 1), :]).astype(BF16)
    P0[...] = jnp.zeros_like(P0)

    def arrived(dst, sem):
        local(dst, dst, sem).wait()

    for t, dev, h in others:
        q = dev[1]
        arrived(W1T.at[q], w_recv.at[q])

    f_load[1].wait()
    fx[1].wait_recv()
    w1_all = W1T[...].reshape(256, 512)

    def first(t):
        wide = jnp.concatenate([F[0, t], F[1, t]], axis=1)
        return mm_nt(wide, w1_all)

    def xcopy(kind, src, dst, t):
        return remote(src.at[t], dst.at[t], x_send.at[kind, t], x_recv.at[kind, t], across)

    def send_first(t, carry):
        h1s[t] = first(t + OWN).astype(BF16)
        xcopy(0, h1s, h1r, t).start()
        return carry

    lax.fori_loop(0, OWN, send_first, 0)
    f_load[0].wait()
    fx[0].wait_recv()

    def keep_first(t, carry):
        H1[t] = first(t)
        return carry

    lax.fori_loop(0, OWN, keep_first, 0)

    w2x_across = remote(W2T.at[me_c], W2T.at[me_c], w_send.at[12], w_recv.at[12], across)
    w2x_beside = remote(W2T.at[me_c], W2T.at[me_c], w_send.at[13], w_recv.at[13], beside)
    far = (1 - hi) * 2 + lo
    w2x_pass = remote(W2T.at[far], W2T.at[far], w_send.at[14], w_recv.at[14], beside)
    w2x_beside.start()
    w2x_across.start()
    cx[0].start()
    cx[1].start()
    for t, dev, h in others:
        arrived(pk.at[dev[1]], w_recv.at[4 + dev[1]])
    gains = pk[0] + pk[1] + pk[2] + pk[3]
    g1, b1, g2, b2 = (gains[k : k + 1] for k in range(4))
    pair0, pair1 = pk[2 * hi], pk[2 * hi + 1]
    g3 = jnp.concatenate([pair0[4:5], pair1[4:5]], axis=1)
    b3 = jnp.concatenate([pair0[5:6], pair1[5:6]], axis=1)

    def ar_start(k, val, half):
        n = n_pix * 2 if half else n_all
        me = me_p * 2 + lo if half else me_p * n_ch + me_c
        sbuf[k] = val
        rbuf[k, me] = val

        def send(t, carry):
            q = lax.rem(me + t, n)
            dev = (q // 2, hi * 2 + lax.rem(q, 2)) if half else (q // n_ch, lax.rem(q, n_ch))
            remote(sbuf.at[k], rbuf.at[k, me], ar_send.at[k], ar_recv.at[k], dev).start()
            return carry

        lax.fori_loop(1, n, send, 0)

    def ar_finish(k, half):
        n = n_pix * 2 if half else n_all
        span = rbuf.at[k, pl.ds(0, n - 1)]
        arrived(span, ar_recv.at[k])
        total = jnp.sum(rbuf[k, 0:n], axis=0)
        return total

    def ar_close(k, half):
        n = n_pix * 2 if half else n_all
        span = rbuf.at[k, pl.ds(0, n - 1)]
        arrived(span, ar_send.at[k])

    def pack2(a, b, extra=None):
        tail = jnp.zeros((1, 128), F32) if extra is None else extra
        return jnp.concatenate(
            [a[:, 0:128], a[:, 128:256], b[:, 0:128], b[:, 128:256], tail, jnp.zeros((3, 128), F32)], axis=0
        )

    def unpack2(v):
        return (
            jnp.concatenate([v[0:1], v[1:2]], axis=1),
            jnp.concatenate([v[2:3], v[3:4]], axis=1),
        )

    def pack3(a, b):
        return jnp.concatenate([a[:, 128 * i : 128 * (i + 1)] for i in range(4)] + [b[:, 128 * i : 128 * (i + 1)] for i in range(4)], axis=0)

    def unpack3(v):
        return (
            jnp.concatenate([v[i : i + 1] for i in range(4)], axis=1),
            jnp.concatenate([v[i : i + 1] for i in range(4, 8)], axis=1),
        )

    zero = jnp.zeros((8, 256), F32)

    def sum_first(t, carry):
        s, q, n = carry
        xcopy(0, h1s, h1r, t).wait_recv()
        h = H1[t] + h1r[t].astype(F32)
        H1[t] = h
        h1b[t] = h.astype(BF16)
        v = V[t]
        vh = spread(v, 256) * h
        return s + fold8(vh), q + fold8(vh * h), n + fold8(v)

    s, q, n = lax.fori_loop(0, OWN, sum_first, (zero, zero, jnp.zeros((8, 128), F32)))
    ar_start(0, pack2(fold1(s), fold1(q), fold1(n)), False)
    arrived(W2T.at[far], w_recv.at[12])
    w2x_pass.start()
    total = ar_finish(0, False)
    s, q = unpack2(total)
    inv_n = 1.0 / spread(total[4:5], 512)
    inv_n2 = inv_n[:, 0:256]
    avg1 = s * inv_n2
    scale1 = lax.rsqrt(q * inv_n2 - avg1 * avg1 + EPS)
    a1_gain = g1 * scale1
    a1_shift = b1 - avg1 * a1_gain

    def act_first(t, carry):
        v = spread(V[t], 256)
        aff = v * (H1[t] * a1_gain + a1_shift)
        sig = logistic(aff)
        act = aff * sig
        comp[pl.ds(pl.multiple_of(t * ROWS, 16), ROWS), :] = act
        D1[t] = v * (sig + act * (1.0 - sig))
        return carry

    lax.fori_loop(0, OWN, act_first, 0)

    def to_padded():
        for i in range(IMAGES):
            for y in range(SIDE):
                P0[EDGE + (i * PAD + y + 1) * PAD : EDGE + (i * PAD + y + 1) * PAD + SIDE, :] = comp[
                    (i * SIDE + y) * SIDE : (i * SIDE + y + 1) * SIDE, :
                ]

    def from_padded(dst):
        for i in range(IMAGES):
            for y in range(SIDE):
                dst[(i * SIDE + y) * SIDE : (i * SIDE + y + 1) * SIDE, :] = padded[
                    (i * SIDE + y) * PAD : (i * SIDE + y) * PAD + SIDE, :
                ]

    to_padded()
    for i in range(IMAGES):
        for c in range(3):
            at = EDGE + i * 256 + c - 1
            PC[i * 256 : (i + 1) * 256, 256 * c : 256 * (c + 1)] = P0[at : at + 256, :].astype(BF16)

    arrived(W2T.at[hi * 2 + 1 - lo], w_recv.at[13])
    arrived(W2T.at[(1 - hi) * 2 + 1 - lo], w_recv.at[14])
    for cp in w3x:
        cp.start()
    h1x = [remote(h1b, h1o, x_send.at[4, 0], x_recv.at[4, 0], across)]

    def conv(i, carry):
        total = None
        for r in range(3):
            rows = PC[pl.ds(pl.multiple_of(i * 256 + 16 * r, 16), SIDE * PAD), :]
            part = mm_nt(rows, W2T[:, :, 768 * r : 768 * (r + 1)].reshape(256, 768))
            total = part if total is None else total + part
        padded[pl.ds(pl.multiple_of(i * SIDE * PAD, 16), SIDE * PAD), :] = total
        return carry

    lax.fori_loop(0, IMAGES, conv, 0)
    from_padded(H2)

    def sum_second(t, carry):
        s, q = carry
        h = H2[pl.ds(pl.multiple_of(t * ROWS, 16), ROWS), :]
        h2s[t] = h.astype(BF16)
        xcopy(1, h2s, h2r, t).start()
        vh = spread(V[t], 256) * h
        return s + fold8(vh), q + fold8(vh * h)

    s, q = lax.fori_loop(0, OWN, sum_second, (zero, zero))
    ar_start(1, pack2(fold1(s), fold1(q)), False)
    s, q = unpack2(ar_finish(1, False))
    avg2 = s * inv_n2
    scale2 = lax.rsqrt(q * inv_n2 - avg2 * avg2 + EPS)
    a2_gain = g2 * scale2
    a2_shift = b2 - avg2 * a2_gain

    w3_load.wait()
    for t, dev, h in others:
        arrived(W3.at[dev[1]], w_recv.at[8 + dev[1]])

    def act_second(t, h, carry):
        s, q = carry
        v = spread(V[t], 256)
        aff = v * (h * a2_gain + a2_shift)
        sig = logistic(aff)
        act = aff * sig
        D2[t] = v * (sig + act * (1.0 - sig))
        act = act.astype(BF16)
        A2[t] = act
        h3 = mm(act, W3[...].reshape(256, 512))
        H3[t] = h3
        return s + fold8(h3), q + fold8(h3 * h3)

    def own_second(t, carry):
        return act_second(t, H2[pl.ds(pl.multiple_of(t * ROWS, 16), ROWS), :], carry)

    def other_second(t, carry):
        xcopy(1, h2s, h2r, t).wait_recv()
        return act_second(t + OWN, h2r[t].astype(F32), carry)

    wide_zero = jnp.zeros((8, 512), F32)
    carry = lax.fori_loop(0, OWN, own_second, (wide_zero, wide_zero))
    s, q = lax.fori_loop(0, OWN, other_second, carry)
    ar_start(2, pack3(fold1(s), fold1(q)), True)
    for cp in h1x:
        cp.start()
    for cp in c_load:
        cp.wait()
    for cp in cx:
        cp.wait_recv()
    s, q = unpack3(ar_finish(2, True))
    avg3 = s * inv_n
    scale3 = lax.rsqrt(q * inv_n - avg3 * avg3 + EPS)
    a3_gain = g3 * scale3
    a3_shift = b3 - avg3 * a3_gain

    def last(t, carry):
        s, q = carry
        v = spread(V[t], 512)
        h3 = H3[t]
        wide = jnp.concatenate([F[0, t], F[1, t]], axis=1).astype(F32)
        total = v * (h3 * a3_gain + a3_shift) + wide
        sig = logistic(total)
        out = total * sig
        RES[0, t] = out[:, 0:256].astype(BF16)
        RES[1, t] = out[:, 256:512].astype(BF16)
        given = jnp.concatenate([C[0, t], C[1, t]], axis=1).astype(F32)
        gs = given * (sig + out * (1.0 - sig))
        GS[t] = gs
        vg = v * gs
        return s + fold8(vg), q + fold8(vg * (h3 - avg3))

    s, q = lax.fori_loop(0, BOTH, last, (wide_zero, wide_zero))
    ar_start(3, pack3(fold1(s), fold1(q * scale3)), True)
    parts = ((0, part0), (1, part1))
    res_here = [
        local(RES.at[lo, pl.ds(OWN * s, OWN)], res_out.at[pl.ds(mine + part, OWN)], out_sem.at[s]) for s, part in parts
    ]
    res_there = [
        remote(RES.at[1 - lo, pl.ds(OWN * s, OWN)], res_out.at[pl.ds(mine + part, OWN)], o_send.at[s], o_recv.at[s], beside)
        for s, part in parts
    ]
    for cp in res_here + res_there:
        cp.start()
    shift3, gain3 = unpack3(ar_finish(3, True))
    k3_h = -a3_gain * gain3 * scale3 * inv_n
    k3_0 = -a3_gain * shift3 * inv_n - k3_h * avg3

    def back_third(t, carry):
        s, q, h2 = carry[0], carry[1], carry[2]
        v = spread(V[t], 512)
        g = (v * (a3_gain * GS[t] + k3_h * H3[t] + k3_0)).astype(BF16)
        G3[t] = g
        e = mm_nt(g, W3[...].reshape(256, 512)) * D2[t]
        return e, s + fold8(e), q + fold8(e * (h2 - avg2))

    def other_third(t, carry):
        e, s, q = back_third(t + OWN, (carry[0], carry[1], h2r[t].astype(F32)))
        e2s[t] = e.astype(BF16)
        xcopy(2, e2s, e2r, t).start()
        return s, q

    def own_third(t, carry):
        e, s, q = back_third(t, (carry[0], carry[1], H2[pl.ds(pl.multiple_of(t * ROWS, 16), ROWS), :]))
        E2[t] = e
        return s, q

    carry = lax.fori_loop(0, OWN, other_third, (zero, zero))
    s, q = lax.fori_loop(0, OWN, own_third, carry)
    ar_start(4, pack2(fold1(s), fold1(q * scale2)), False)

    piece = 128 // n_lo
    n_sub = n_lo // 2

    def pair_copies(k, part, got):
        return [
            remote(part.at[h, 1 - lo], got.at[h], g_send.at[k, h], g_recv.at[k, h], beside) for h in range(2)
        ]

    def pair_add(k, part, got, acc):
        for h, cp in enumerate(pair_copies(k, part, got)):
            cp.wait_recv()
            both = part[h, lo].astype(F32) + got[h].astype(F32)
            acc[h] = both.astype(BF16).reshape(acc.shape[1:])

    def spread_copies(k, acc, got):
        copies = []
        for t in range(1, n_lo):
            q = lax.rem(g_lo + t, n_lo)
            copies.append(
                remote(
                    acc.at[lax.rem(q, 2), q // 2],
                    got.at[g_lo],
                    g_send.at[k, 2 + t],
                    g_recv.at[k, 2 + t],
                    (g_hi * n_lo + q, me_c),
                )
            )
        return copies

    def spread_add(k, acc, got, level):
        for cp in spread_copies(k, acc, got):
            cp.wait_recv()
        total = acc[lax.rem(g_lo, 2), g_lo // 2].astype(F32)
        for t in range(1, n_lo):
            total = total + got[lax.rem(g_lo + t, n_lo)].astype(F32)
        if n_hi > 1:
            level[g_hi] = total.astype(BF16)

            def swap(t):
                q = lax.rem(g_hi + t, n_hi)
                return remote(
                    level.at[g_hi], level.at[g_hi], g_send.at[k, 27 + t], g_recv.at[k, 27 + t], (q * n_lo + g_lo, me_c)
                )

            for t in range(1, n_hi):
                swap(t).start()
            for t in range(1, n_hi):
                swap(t).wait()
            total = level[0].astype(F32)
            for t in range(1, n_hi):
                total = total + level[t].astype(F32)
        return total

    def give_copies(k, done, fin, to_hi, first=0):
        copies = []
        for t in range(first, n_lo):
            q = lax.rem(g_lo + t, n_lo)
            copies.append(
                remote(
                    done, fin, g_send.at[k, 10 + t], g_recv.at[k, 10 + 8 * hi + t], (g_hi * n_lo + q, to_hi * 2 + lo)
                )
            )
        return copies

    owner_hi = lax.rem(g_lo, 2)
    own_sub = g_lo // 2
    keeps = owner_hi == hi

    def wide_give(k, slot):
        copies = give_copies(k, wf.at[slot], wfin.at[slot, hi, own_sub], owner_hi)
        for t, cp in enumerate(copies):
            if t == 0:

                @pl.when(jnp.logical_not(keeps))
                def _():
                    cp.start()

                @pl.when(keeps)
                def _():
                    wfin[slot, hi, own_sub] = wf[slot]

            else:
                cp.start()

    def wide_take(k, slot, out):
        for sub in range(n_sub):
            q = sub * 2 + hi
            t = lax.rem(g_lo - q + n_lo, n_lo)
            for h in range(2):

                @pl.when(jnp.logical_not((q == g_lo) & (hi == h)))
                def _():
                    arrived(wfin.at[slot, h, sub], g_recv.at[k, 10 + 8 * h + t])

        for h in range(2):
            out[:, 512 * h : 512 * (h + 1)] = wfin[slot, h].astype(F32).reshape(64, 512)

    def wide_close(k, slot):
        for cp in pair_copies(k, wp.at[slot], wc.at[slot]):
            cp.wait_send()
        for cp in spread_copies(k, wa.at[slot], wr.at[slot]):
            cp.wait_send()
        for t, cp in enumerate(give_copies(k, wf.at[slot], wfin.at[slot, hi, own_sub], owner_hi)):
            if t == 0:

                @pl.when(jnp.logical_not(keeps))
                def _():
                    cp.wait_send()

            else:
                cp.wait_send()

    def wide_part(slot, left, right_of):
        acc_w[...] = jnp.zeros_like(acc_w)

        def add(t, carry):
            a = left[pl.ds(2 * t, 2)].reshape(2 * ROWS, 256)
            acc_w[...] += mm_tn(a, right_of(t))
            return carry

        lax.fori_loop(0, OWN, add, 0)
        wp[slot] = acc_w[...].astype(BF16).reshape(2, 2, 64, 512)

    wide_part(0, A2, lambda t: G3[pl.ds(2 * t, 2)].reshape(2 * ROWS, 512))
    for cp in pair_copies(0, wp.at[0], wc.at[0]):
        cp.start()

    shift2, gain2 = unpack2(ar_finish(4, False))
    k2_h = -a2_gain * gain2 * scale2 * inv_n2
    k2_0 = -a2_gain * shift2 * inv_n2 - k2_h * avg2

    def back_second(t, carry):
        xcopy(2, e2s, e2r, t).wait_recv()
        at = pl.ds(pl.multiple_of(t * ROWS, 16), ROWS)
        e = E2[t] + e2r[t].astype(F32)
        comp[at, :] = spread(V[t], 256) * (a2_gain * e + k2_h * H2[at, :] + k2_0)
        return carry

    lax.fori_loop(0, OWN, back_second, 0)
    to_padded()
    for i in range(IMAGES):
        for c in range(3):
            at = EDGE + i * 256 - (c - 1)
            Q[c, i * 256 : (i + 1) * 256, :] = P0[at : at + 256, :].astype(BF16)

    pair_add(0, wp.at[0], wc.at[0], wa.at[0])
    for cp in spread_copies(0, wa.at[0], wr.at[0]):
        cp.start()

    def conv_back(i, carry):
        total = None
        for r in range(3):
            at = pl.ds(pl.multiple_of(i * 256 + 16 * (2 - r), 16), SIDE * PAD)
            for c in range(3):
                w = W2T[:, :, 768 * r + 256 * c : 768 * r + 256 * (c + 1)].reshape(256, 256)
                part = mm(Q[c, at, :], w)
                total = part if total is None else total + part
        padded[pl.ds(pl.multiple_of(i * SIDE * PAD, 16), SIDE * PAD), :] = total
        return carry

    lax.fori_loop(0, IMAGES, conv_back, 0)
    from_padded(comp)

    def sum_back_first(t, carry):
        s, q = carry
        e = comp[pl.ds(pl.multiple_of(t * ROWS, 16), ROWS), :] * D1[t]
        E1[t] = e
        e1s[t] = e.astype(BF16)
        xcopy(3, e1s, e1r, t).start()
        return s + fold8(e), q + fold8(e * (H1[t] - avg1))

    s, q = lax.fori_loop(0, OWN, sum_back_first, (zero, zero))
    ar_start(5, pack2(fold1(s), fold1(q * scale1)), False)

    wf[0] = spread_add(0, wa.at[0], wr.at[0], wh.at[0]).astype(BF16)
    wide_give(0, 0)

    acc_s[...] = jnp.zeros_like(acc_s)

    def taps(i, carry):
        left = Q[1, pl.ds(pl.multiple_of(i * 256 + 16, 16), SIDE * PAD), :]
        for r in range(3):
            right = PC[pl.ds(pl.multiple_of(i * 256 + 16 * r, 16), SIDE * PAD), :]
            acc_s[:, 768 * r : 768 * (r + 1)] += mm_tn(left, right)
        return carry

    lax.fori_loop(0, IMAGES, taps, 0)
    sp[...] = acc_s[...].astype(BF16).reshape(2, 2, 64, 2304)
    for cp in pair_copies(2, sp, sc):
        cp.start()

    shift1, gain1 = unpack2(ar_finish(5, False))
    k1_h = -a1_gain * gain1 * scale1 * inv_n2
    k1_0 = -a1_gain * shift1 * inv_n2 - k1_h * avg1

    def back_first(t, e, h):
        g = (spread(V[t], 256) * (a1_gain * e + k1_h * h + k1_0)).astype(BF16)
        G1[t] = g
        out = (mm(g, W1T[...].reshape(256, 512)) + GS[t]).astype(BF16)
        RES[0, t] = out[:, 0:256]
        RES[1, t] = out[:, 256:512]

    ig_here = [
        local(RES.at[lo, pl.ds(OWN * s, OWN)], ig_out.at[pl.ds(mine + part, OWN)], out_sem.at[2 + s])
        for s, part in parts
    ]
    ig_there = [
        remote(
            RES.at[1 - lo, pl.ds(OWN * s, OWN)], ig_out.at[pl.ds(mine + part, OWN)], o_send.at[2 + s], o_recv.at[2 + s], beside
        )
        for s, part in parts
    ]
    for cp in res_here:
        cp.wait()
    for cp in res_there:
        cp.wait_send()

    def own_back_first(t, carry):
        back_first(t, E1[t], H1[t])
        return carry

    lax.fori_loop(0, OWN, own_back_first, 0)
    ig_here[0].start()
    ig_there[0].start()
    pair_add(2, sp, sc, sa)
    for cp in spread_copies(2, sa, sr):
        cp.start()
    for cp in h1x:
        cp.wait_recv()

    def other_back_first(t, carry):
        xcopy(3, e1s, e1r, t).wait_recv()
        back_first(t + OWN, e1r[t].astype(F32), h1o[t].astype(F32))
        return carry

    lax.fori_loop(0, OWN, other_back_first, 0)
    ig_here[1].start()
    ig_there[1].start()

    def features_of(t):
        left = F[0, pl.ds(2 * t, 2)].reshape(2 * ROWS, 256)
        right = F[1, pl.ds(2 * t, 2)].reshape(2 * ROWS, 256)
        return jnp.concatenate([left, right], axis=1)

    wide_part(1, G1, features_of)
    for cp in pair_copies(1, wp.at[1], wc.at[1]):
        cp.start()

    pair_add(1, wp.at[1], wc.at[1], wa.at[1])
    for cp in spread_copies(1, wa.at[1], wr.at[1]):
        cp.start()
    sf[...] = spread_add(2, sa, sr, sh).astype(BF16)
    cross = remote(sf, sx, g_send.at[2, 26], g_recv.at[2, 26], across)

    @pl.when(jnp.logical_not(keeps))
    def _():
        cross.start()

    wf[1] = spread_add(1, wa.at[1], wr.at[1], wh.at[1]).astype(BF16)
    wide_give(1, 1)

    def s_copies():
        return give_copies(2, sf, sfin.at[own_sub], hi, 1)

    @pl.when(keeps)
    def _():
        cross.wait_recv()
        total = (sf[...].astype(F32) + sx[...].astype(F32)).astype(BF16)
        sf[...] = total
        sfin[own_sub] = total
        for cp in s_copies():
            cp.start()

    def own64(v):
        half = jnp.where(hi == 0, v[:, 0:128], v[:, 128:256])
        swapped = jnp.concatenate([half[:, 64:128], half[:, 0:64]], axis=1)
        return jnp.concatenate([jnp.where(lo == 0, half, swapped), jnp.zeros((1, 128), F32)], axis=1)

    def own256(v):
        return jnp.where(lo == 0, v[:, 0:256], v[:, 256:512])

    st_out[...] = jnp.concatenate(
        [
            own64(gain1),
            own64(shift1),
            own64(gain2),
            own64(shift2),
            own256(gain3),
            own256(shift3),
            jnp.zeros((2, 256), F32),
        ],
        axis=0,
    )

    wide_take(0, 0, eg_out)
    wide_take(1, 1, rg_out)
    for sub in range(n_sub):
        q = sub * 2 + hi
        t = lax.rem(g_lo - q + n_lo, n_lo)

        @pl.when(q != g_lo)
        def _():
            arrived(sfin.at[sub], g_recv.at[2, 10 + 8 * hi + t])

    sg_out[...] = sfin[...].astype(F32).reshape(64, 2304)

    wide_close(0, 0)
    wide_close(1, 1)
    for cp in pair_copies(2, sp, sc) + spread_copies(2, sa, sr):
        cp.wait_send()

    @pl.when(keeps)
    def _():
        for cp in s_copies():
            cp.wait_send()

    @pl.when(jnp.logical_not(keeps))
    def _():
        cross.wait_send()

    for cp in ig_here:
        cp.wait()
    for cp in ig_there:
        cp.wait()
    for cp in res_there:
        cp.wait_recv()
    for cp in fx + cx + w1x + pkx + w3x + h1x + [w2x_across, w2x_beside, w2x_pass]:
        cp.wait_send()
    for kind, src, dst in ((0, h1s, h1r), (1, h2s, h2r), (2, e2s, e2r), (3, e1s, e1r)):
        for t in range(OWN):
            xcopy(kind, src, dst, t).wait_send()
    for k, half in ((0, False), (1, False), (2, True), (3, True), (4, False), (5, False)):
        ar_close(k, half)


def block(n_pix, n_ch, *args):
    (feat, cot, mask, w1, w2, w3, params) = args
    rows, lanes = feat.shape
    n_lo = min(n_pix, 8)
    n_hi = n_pix // n_lo
    piece = 128 // n_lo
    n_sub = n_lo // 2
    chunks = rows // ROWS
    any_space = pl.BlockSpec(memory_space=pl.ANY)
    vmem = pl.BlockSpec(memory_space=pltpu.VMEM)
    V = pltpu.VMEM
    DMA = pltpu.SemaphoreType.DMA
    scratch = [
        V((2, BOTH, ROWS, 256), BF16),
        V((2, BOTH, ROWS, 256), BF16),
        V((BOTH, ROWS, 128), F32),
        V((1024, 64), BF16),
        V((2304, 64), BF16),
        V((2, 64, 512), BF16),
        V((4, 64, 512), BF16),
        V((4, 64, 2304), BF16),
        V((4, 64, 512), BF16),
        V((4, 8, 256), F32),
        V((6, 8, 128), F32),
        V((6, n_pix * n_ch, 8, 128), F32),
        V((OWN, ROWS, 256), BF16),
        V((OWN, ROWS, 256), BF16),
        V((OWN, ROWS, 256), F32),
        V((OWN, ROWS, 256), BF16),
        V((OWN, ROWS, 256), BF16),
        V((OWN, ROWS, 256), F32),
        V((OWN * ROWS, 256), F32),
        V((FLAT + 2 * EDGE, 256), F32),
        V((FLAT, 768), BF16),
        V((3, FLAT, 256), BF16),
        V((IMAGES * SIDE * PAD, 256), F32),
        V((OWN * ROWS, 256), F32),
        V((OWN, ROWS, 256), BF16),
        V((OWN, ROWS, 256), BF16),
        V((BOTH, ROWS, 256), BF16),
        V((BOTH, ROWS, 256), F32),
        V((BOTH, ROWS, 512), F32),
        V((BOTH, ROWS, 512), F32),
        V((2, BOTH, ROWS, 256), BF16),
        V((BOTH, ROWS, 512), BF16),
        V((OWN, ROWS, 256), F32),
        V((OWN, ROWS, 256), BF16),
        V((OWN, ROWS, 256), BF16),
        V((OWN, ROWS, 256), F32),
        V((OWN, ROWS, 256), BF16),
        V((OWN, ROWS, 256), BF16),
        V((BOTH, ROWS, 256), BF16),
        V((256, 512), F32),
        V((256, 2304), F32),
        V((2, 2, 2, 64, 512), BF16),
        V((2, 2, 64, 512), BF16),
        V((2, 2, n_sub, piece, 512), BF16),
        V((2, n_lo, piece, 512), BF16),
        V((2, n_hi, piece, 512), BF16),
        V((2, piece, 512), BF16),
        V((2, 2, n_sub, piece, 512), BF16),
        V((2, 2, 64, 2304), BF16),
        V((2, 64, 2304), BF16),
        V((2, n_sub, piece, 2304), BF16),
        V((n_lo, piece, 2304), BF16),
        V((n_hi, piece, 2304), BF16),
        V((piece, 2304), BF16),
        V((piece, 2304), BF16),
        V((n_sub, piece, 2304), BF16),
        DMA((8,)),
        DMA((4,)),
        DMA((4,)),
        DMA((16,)),
        DMA((16,)),
        DMA((6,)),
        DMA((6,)),
        DMA((5, OWN)),
        DMA((5, OWN)),
        DMA((4,)),
        DMA((4,)),
        DMA((4,)),
        DMA((3, 28 + n_hi)),
        DMA((3, 28 + n_hi)),
    ]
    wide = jax.ShapeDtypeStruct((chunks, ROWS, lanes), BF16)
    return pl.pallas_call(
        functools.partial(kernel, n_pix, n_ch),
        out_shape=(
            wide,
            wide,
            jax.ShapeDtypeStruct((64, 1024), F32),
            jax.ShapeDtypeStruct((64, 2304), F32),
            jax.ShapeDtypeStruct((64, 1024), F32),
            jax.ShapeDtypeStruct((8, 256), F32),
        ),
        in_specs=[any_space, any_space, vmem, any_space, any_space, any_space, vmem],
        out_specs=(any_space, any_space, vmem, vmem, vmem, vmem),
        scratch_shapes=scratch,
        compiler_params=pltpu.CompilerParams(
            collective_id=0, has_side_effects=True, vmem_limit_bytes=56 * 2**20
        ),
        name="bottleneck",
    )(
        feat.reshape(chunks, ROWS, lanes),
        cot.reshape(chunks, ROWS, lanes),
        mask.astype(F32).reshape(chunks, ROWS),
        w1,
        w2.reshape(2304, 64),
        w3,
        params,
    )


def solution(mesh):
    n_pix, n_ch = mesh.shape["pix"], mesh.shape["ch"]

    def body(feat, mask, w1, w2, w3, g1, b1, g2, b2, g3, b3, cot):
        params = jnp.concatenate([v.astype(F32) for v in (g1, b1, g2, b2, g3, b3)]).reshape(1, 768)
        res, ig, rg, sg, eg, st = block(n_pix, n_ch, feat, cot, mask, w1, w2, w3, params)
        return (
            res.reshape(feat.shape),
            ig.reshape(feat.shape),
            rg.T,
            sg.T.reshape(3, 3, 256, 64),
            eg,
            st[0, 0:64],
            st[1, 0:64],
            st[2, 0:64],
            st[3, 0:64],
            st[4],
            st[5],
        )

    wide = P("pix", "ch")
    return jax.shard_map(
        body,
        mesh=mesh,
        in_specs=(wide, P("pix"), P(None, "ch"), P(None, None, None, "ch"), P("ch", None)) + (P("ch"),) * 6 + (wide,),
        out_specs=(wide, wide, P(None, "ch"), P(None, None, None, "ch"), P("ch", None)) + (P("ch"),) * 6,
        check_vma=False,
    )
```

time: 651 us -> 148 us (0.23)
  waiting for transfers between devices: 359 us -> 0 us
  Pallas kernels: 0 us -> 127 us
  blocking collectives: 126 us -> 0 us
  local copies, waits for them, and re-layouts: 75.6 us -> 18.6 us
  matrix products: 45.5 us -> 0 us
  other arithmetic: 28.3 us -> 0.72 us
  between operations: 14.6 us -> 0.67 us
    reduce_scatter x3 -> x0, waiting for transfers between devices: 166 us -> none  [the longest x1 95.5 us: body(): lax.psum_scatter(jnp.dot(active_two, expander, preferred_element_type=jnp...]
    pallas_call x0 -> x1, Pallas kernels: none -> 127 us  [block(): pl.pallas_call(functools.partial(kernel, n_pix, n_ch), out_shape=(wide, w...]
    psum x6 -> x0, blocking collectives: 126 us -> none  [the longest x3 65.5 us: norm_forward(): totals, squares, counted = lax.psum((totals, squares, local_count), 'pix')]
    all_gather x3 -> x0, waiting for transfers between devices: 111 us -> none  [the longest x1 48.9 us: body(): full_input = lax.all_gather(features, 'ch', axis=1, tiled=True)]
    psum x1 -> x0, waiting for transfers between devices: 81.3 us -> none  [body(): lax.psum((reduce_grad, spatial_grad, expand_grad), 'pix')]
    reshape x14 -> x3, local copies, waits for them, and re-layouts: 44.7 us -> 2.63 us  [the longest x1 1.36 us: body(): sg.T.reshape(3, 3, 256, 64)]
    dot_general x15 -> x0, matrix products: 39.7 us -> none  [the longest x11 15.5 us: row_contract(): lax.dot_general(left, right, (((0,), (0,)), ((), ())), preferred_element_...]
    slice x1, local copies, waits for them, and re-layouts: 14.6 us -> 1.34 us  [body(): st[5]]
  transfers between devices with their start and end apart: 7 -> 0, of which waited for: 7 -> 0; matrix products, arithmetic and copies ran while one was open for 10% -> 0% of each run, Pallas kernels for 0% -> 0%
where the time goes in v1:
time: 148 us; the launch traced here: 147 us
  Pallas kernels  127 us (86%)
  local copies, waits for them, and re-layouts  18.6 us (13%)
    pallas_call x1, Pallas kernels, block(): pl.pallas_call(functools.partial(kernel, n_pix, n_ch), out_shape=(wide, w...  127 us
    unnamed x15, local copies, waits for them, and re-layouts  9.25 us
    concatenate x1, local copies, waits for them, and re-layouts, body(): jnp.concatenate([v.astype(F32) for v in (g1, b1, g2, b2, g3, b3)])  4.08 us

profile of v1, /device:TPU:0, one launch (start us, length us, event | category | flops | bytes accessed | tf_op | source)
XLA Modules:
  0.0 146.8 jit_solution(10093979451221086801)
XLA Ops:
  0.6 2.0 %copy.26 = bf16[3,3,256,64]{3,2,1,0:T(8,128)(2,1)} copy(bf16[3,3,256,64]{2,3,1,0:T(8,128)(2,1)} %param.15) | data formatting | bytes 589824 | tf_op args[3]
  2.7 1.7 %copy.27.w1_in = bf16[1024,64]{1,0:T(8,128)(2,1)} copy(bf16[1024,64]{0,1:T(8,128)(2,1)} %param.14) | data formatting | bytes 262144 | tf_op args[2]
  4.4 0.7 convert_element_type.2
  5.1 0.7 reshape.50.mask
  5.8 4.1 %concatenate.4 = bf16[768]{0:T(1024)(128)(2,1)S(1)} concatenate(bf16[64]{0:T(256)(128)(2,1)} %param.17, bf16[64]{0:T(256)(128)(2,1)} %param.18, bf16[64]{0:T(256)(128)(2,1)} %param.19, bf16[64]{0:T(256)(128)(2,1)} %param.20, bf16[256]{0:T(256)(128)(2,1)} %param.21, bf16[256]{0:T(256)(128)(2,1)} %param.22), dimensions={0} | concatenate | bytes 3072 | tf_op jit(solution)/shard_map/concatenate | solution.py:994
  9.9 0.6 reshape.58.params
  10.5 126.8 %bottleneck.1 = (bf16[28,112,256]{2,1,0:T(8,128)(2,1)}, bf16[28,112,256]{2,1,0:T(8,128)(2,1)}, f32[64,1024]{1,0:T(8,128)}, f32[64,2304]{1,0:T(8,128)}, f32[64,1024]{1,0:T(8,128)}, /*index=5*/f32[8,256]{1,0:T(8,128)}) custom-call(bf16[28,112,256]{2,1,0:T(8,128)(2,1)} %bitcast.20, bf16[28,112,256]{2,1,0:T(8,128)(2,1)} %bitcast.21, f32[28,112]{1,0:T(8,128)} %reshape.50.mask, ...), custom_call_target="tpu_custom_call" | custom-call | tf_op jit(solution)/shard_map/bottleneck/pallas_call | solution.py:962
  137.2 0.0 copy-start.1
  137.2 1.3 slice_bitcast_fusion
  138.6 1.3 fusion
  139.9 1.4 reshape.56
  141.3 0.9 copy.28
  142.2 0.0 copy-done.1
  142.2 0.0 copy-start
  142.2 1.2 copy.33
  143.4 0.8 copy-done
  144.2 0.0 copy-start.3
  144.2 0.0 copy-start.2
  144.2 1.2 copy.34
  145.4 0.0 copy-done.3
  145.4 0.7 copy.35
  146.1 0.0 copy-done.2
  146.1 0.7 copy.36
Async XLA Ops:
  137.2 5.0 %copy-start.1 = (bf16[28,112,256]{2,1,0:T(8,128)(2,1)S(1)}, bf16[28,112,256]{2,1,0:T(8,128)(2,1)}, u32[]{:S(2)}) copy-start(bf16[28,112,256]{2,1,0:T(8,128)(2,1)} %get-tuple-element.17) | copy-start | bytes 4816900
  142.2 2.0 %copy-start = (bf16[28,112,256]{2,1,0:T(8,128)(2,1)S(1)}, bf16[28,112,256]{2,1,0:T(8,128)(2,1)}, u32[]{:S(2)}) copy-start(bf16[28,112,256]{2,1,0:T(8,128)(2,1)} %get-tuple-element.18) | copy-start | bytes 4816900
  144.2 1.2 copy-start.3
  144.2 1.9 %copy-start.2 = (f32[64,1024]{1,0:T(8,128)S(1)}, f32[64,1024]{1,0:T(8,128)}, u32[]{:S(2)}) copy-start(f32[64,1024]{1,0:T(8,128)} %get-tuple-element.66) | copy-start | bytes 786436

commit v2 on v1

--- a/solution.py
+++ b/solution.py
@@ -59,7 +59,12 @@
     w1_in,
     w2_in,
     w3_in,
-    params,
+    g1_in,
+    b1_in,
+    g2_in,
+    b2_in,
+    g3_in,
+    b3_in,
     res_out,
     ig_out,
     rg_out,
@@ -69,9 +74,6 @@
     F,
     C,
     V,
-    w1v,
-    w2v,
-    w1t_own,
     W1T,
     W2T,
     W3,
@@ -157,8 +159,8 @@
     mine, theirs = lo * BOTH, (1 - lo) * BOTH
     part0, part1 = hi * OWN, (1 - hi) * OWN
 
-    w1_load = local(w1_in, w1v, ld_sem.at[0])
-    w2_load = local(w2_in, w2v, ld_sem.at[1])
+    w1_load = local(w1_in.at[:, pl.ds(pl.multiple_of(hi * 512, 512), 512)], W1T.at[me_c], ld_sem.at[0])
+    w2_load = local(w2_in, W2T.at[me_c], ld_sem.at[1])
     f_load = [
         local(feat.at[pl.ds(mine + part, OWN)], F.at[lo, pl.ds(OWN * s, OWN)], ld_sem.at[2 + s])
         for s, part in enumerate((part0, part1))
@@ -185,25 +187,13 @@
 
     lax.fori_loop(1, n_all, greet, 0)
 
-    eye = (
-        lax.broadcasted_iota(jnp.int32, (64, 64), 0) == lax.broadcasted_iota(jnp.int32, (64, 64), 1)
-    ).astype(BF16)
-    w1_load.wait()
-    w1t = mm_nt(eye, w1v[...]).astype(BF16)
-    w1t_own[0] = w1t[:, 0:512]
-    w1t_own[1] = w1t[:, 512:1024]
-    W1T[me_c] = w1t_own[hi]
-
-    vec = params[...]
-    vec8 = jnp.broadcast_to(vec[:, 0:256], (8, 256)).astype(BF16)
-    row_i = lax.broadcasted_iota(jnp.int32, (256, 256), 0)
-    col_i = lax.broadcasted_iota(jnp.int32, (256, 256), 1)
-    pk_rows = []
-    for k in range(4):
-        sel = (row_i - 64 * k == col_i - 64 * me_c) & (row_i >= 64 * k) & (row_i < 64 * k + 64)
-        pk_rows.append(mm(vec8, sel.astype(BF16))[0:1])
-    pk_rows += [vec[:, 256:512], vec[:, 512:768], jnp.zeros((2, 256), F32)]
-    pk[me_c] = jnp.concatenate(pk_rows, axis=0)
+    row_i = lax.broadcasted_iota(jnp.int32, (64, 256), 0)
+    col_i = lax.broadcasted_iota(jnp.int32, (64, 256), 1)
+    place = (row_i == col_i - 64 * me_c).astype(BF16)
+    narrow = jnp.concatenate([v[...].astype(F32).reshape(1, 64) for v in (g1_in, b1_in, g2_in, b2_in)] * 2, axis=0)
+    pk_rows = [mm(narrow.astype(BF16), place)[0:4]]
+    pk_rows += [v[...].astype(F32).reshape(1, 256) for v in (g3_in, b3_in)]
+    pk[me_c] = jnp.concatenate(pk_rows + [jnp.zeros((2, 256), F32)], axis=0)
 
     pl.semaphore_wait(barrier, n_all - 1)
 
@@ -223,7 +213,12 @@
     for t in range(1, n_ch):
         q = lax.rem(me_c + t, n_ch)
         others.append((t - 1, (me_p, q), q // 2))
-    w1x = [remote(w1t_own.at[h], W1T.at[me_c], w_send.at[t], w_recv.at[me_c], dev) for t, dev, h in others]
+    w1x = [
+        remote(
+            w1_in.at[:, pl.ds(pl.multiple_of(h * 512, 512), 512)], W1T.at[me_c], w_send.at[t], w_recv.at[me_c], dev
+        )
+        for t, dev, h in others
+    ]
     pkx = [remote(pk.at[me_c], pk.at[me_c], w_send.at[4 + t], w_recv.at[4 + me_c], dev) for t, dev, h in others]
     w3x = [
         remote(
@@ -247,15 +242,12 @@
 
     def put_mask(t, carry):
         at = mine + jnp.where(t < OWN, part0 + t, part1 + t - OWN)
-        row = mask[pl.ds(at, 1), :]
+        row = mask[pl.ds(at, 1), :].astype(F32)
         V[t] = mm(jnp.where(diag, row, 0.0).astype(BF16), ones)
         return carry
 
     lax.fori_loop(0, BOTH, put_mask, 0)
 
-    w2_load.wait()
-    for r in range(3):
-        W2T[me_c, :, 768 * r : 768 * (r + 1)] = mm_nt(eye, w2v[768 * r : 768 * (r + 1), :]).astype(BF16)
     P0[...] = jnp.zeros_like(P0)
 
     def arrived(dst, sem):
@@ -264,6 +256,8 @@
     for t, dev, h in others:
         q = dev[1]
         arrived(W1T.at[q], w_recv.at[q])
+
+    w1_load.wait()
 
     f_load[1].wait()
     fx[1].wait_recv()
@@ -295,6 +289,7 @@
     w2x_beside = remote(W2T.at[me_c], W2T.at[me_c], w_send.at[13], w_recv.at[13], beside)
     far = (1 - hi) * 2 + lo
     w2x_pass = remote(W2T.at[far], W2T.at[far], w_send.at[14], w_recv.at[14], beside)
+    w2_load.wait()
     w2x_beside.start()
     w2x_across.start()
     cx[0].start()
@@ -420,7 +415,7 @@
         total = None
         for r in range(3):
             rows = PC[pl.ds(pl.multiple_of(i * 256 + 16 * r, 16), SIDE * PAD), :]
-            part = mm_nt(rows, W2T[:, :, 768 * r : 768 * (r + 1)].reshape(256, 768))
+            part = mm_nt(rows, jnp.concatenate([W2T[:, 3 * r + c].reshape(256, 256) for c in range(3)], axis=1))
             total = part if total is None else total + part
         padded[pl.ds(pl.multiple_of(i * SIDE * PAD, 16), SIDE * PAD), :] = total
         return carry
@@ -693,7 +688,7 @@
         for r in range(3):
             at = pl.ds(pl.multiple_of(i * 256 + 16 * (2 - r), 16), SIDE * PAD)
             for c in range(3):
-                w = W2T[:, :, 768 * r + 256 * c : 768 * r + 256 * (c + 1)].reshape(256, 256)
+                w = W2T[:, 3 * r + c].reshape(256, 256)
                 part = mm(Q[c, at, :], w)
                 total = part if total is None else total + part
         padded[pl.ds(pl.multiple_of(i * SIDE * PAD, 16), SIDE * PAD), :] = total
@@ -843,7 +838,8 @@
         def _():
             arrived(sfin.at[sub], g_recv.at[2, 10 + 8 * hi + t])
 
-    sg_out[...] = sfin[...].astype(F32).reshape(64, 2304)
+    for k in range(9):
+        sg_out[k] = sfin[:, :, 256 * k : 256 * (k + 1)].astype(F32).reshape(64, 256)
 
     wide_close(0, 0)
     wide_close(1, 1)
@@ -875,7 +871,7 @@
 
 
 def block(n_pix, n_ch, *args):
-    (feat, cot, mask, w1, w2, w3, params) = args
+    feat, cot, mask, w1, w2, w3 = args[:6]
     rows, lanes = feat.shape
     n_lo = min(n_pix, 8)
     n_hi = n_pix // n_lo
@@ -890,11 +886,8 @@
         V((2, BOTH, ROWS, 256), BF16),
         V((2, BOTH, ROWS, 256), BF16),
         V((BOTH, ROWS, 128), F32),
-        V((1024, 64), BF16),
-        V((2304, 64), BF16),
-        V((2, 64, 512), BF16),
         V((4, 64, 512), BF16),
-        V((4, 64, 2304), BF16),
+        V((4, 9, 64, 256), BF16),
         V((4, 64, 512), BF16),
         V((4, 8, 256), F32),
         V((6, 8, 128), F32),
@@ -959,17 +952,17 @@
         DMA((3, 28 + n_hi)),
     ]
     wide = jax.ShapeDtypeStruct((chunks, ROWS, lanes), BF16)
-    return pl.pallas_call(
+    made = pl.pallas_call(
         functools.partial(kernel, n_pix, n_ch),
         out_shape=(
             wide,
             wide,
             jax.ShapeDtypeStruct((64, 1024), F32),
-            jax.ShapeDtypeStruct((64, 2304), F32),
+            jax.ShapeDtypeStruct((9, 64, 256), F32),
             jax.ShapeDtypeStruct((64, 1024), F32),
             jax.ShapeDtypeStruct((8, 256), F32),
         ),
-        in_specs=[any_space, any_space, vmem, any_space, any_space, any_space, vmem],
+        in_specs=[any_space, any_space, vmem, any_space, any_space, any_space] + [vmem] * 6,
         out_specs=(any_space, any_space, vmem, vmem, vmem, vmem),
         scratch_shapes=scratch,
         compiler_params=pltpu.CompilerParams(
@@ -979,33 +972,48 @@
     )(
         feat.reshape(chunks, ROWS, lanes),
         cot.reshape(chunks, ROWS, lanes),
-        mask.astype(F32).reshape(chunks, ROWS),
-        w1,
-        w2.reshape(2304, 64),
+        mask.reshape(chunks, ROWS),
+        w1.T,
+        w2.transpose(0, 1, 3, 2).reshape(9, 64, 256),
         w3,
-        params,
+        *args[6:],
     )
+    narrow = jax.ShapeDtypeStruct((64,), F32)
+    broad = jax.ShapeDtypeStruct((256,), F32)
+    return pl.pallas_call(
+        finish,
+        out_shape=tuple(jax.ShapeDtypeStruct(v.shape, v.dtype) for v in made[:5]) + (narrow,) * 4 + (broad,) * 2,
+        in_specs=[vmem] * 6,
+        out_specs=(any_space,) * 5 + (vmem,) * 6,
+        scratch_shapes=[DMA((5,))],
+        name="outputs",
+    )(*made)
+
+
+def finish(*refs):
+    made, stats, outs, small, sems = refs[:5], refs[5], refs[6:11], refs[11:17], refs[17]
+    copies = [pltpu.make_async_copy(a, b, sems.at[i]) for i, (a, b) in enumerate(zip(made, outs))]
+    for cp in copies:
+        cp.start()
+    for i, out in enumerate(small):
+        out[...] = stats[i : i + 1, 0 : out.shape[0]].reshape(out.shape)
+    for cp in copies:
+        cp.wait()
 
 
 def solution(mesh):
     n_pix, n_ch = mesh.shape["pix"], mesh.shape["ch"]
 
     def body(feat, mask, w1, w2, w3, g1, b1, g2, b2, g3, b3, cot):
-        params = jnp.concatenate([v.astype(F32) for v in (g1, b1, g2, b2, g3, b3)]).reshape(1, 768)
-        res, ig, rg, sg, eg, st = block(n_pix, n_ch, feat, cot, mask, w1, w2, w3, params)
+        made = block(n_pix, n_ch, feat, cot, mask, w1, w2, w3, g1, b1, g2, b2, g3, b3)
+        res, ig, rg, sg, eg = made[:5]
         return (
             res.reshape(feat.shape),
             ig.reshape(feat.shape),
             rg.T,
-            sg.T.reshape(3, 3, 256, 64),
+            sg.reshape(3, 3, 64, 256).transpose(0, 1, 3, 2),
             eg,
-            st[0, 0:64],
-            st[1, 0:64],
-            st[2, 0:64],
-            st[3, 0:64],
-            st[4],
-            st[5],
-        )
+        ) + tuple(made[5:])
 
     wide = P("pix", "ch")
     return jax.shard_map(

time: 148 us -> 135 us (0.912)
  local copies, waits for them, and re-layouts: 18.6 us -> 1.4 us
  Pallas kernels: 127 us -> 132 us
    unnamed x15 -> x0, local copies, waits for them, and re-layouts: 9.25 us -> none
    pallas_call x0 -> x1, Pallas kernels: none -> 4.92 us  [block(): pl.pallas_call(finish, out_shape=tuple((jax.ShapeDtypeStruct(v.shape, v.d...]
    concatenate x1 -> x0, local copies, waits for them, and re-layouts: 4.08 us -> none  [body(): jnp.concatenate([v.astype(F32) for v in (g1, b1, g2, b2, g3, b3)])]
where the time goes in v2:
time: 135 us; the launch traced here: 134 us
  Pallas kernels  132 us (98%)
  local copies, waits for them, and re-layouts  1.4 us (1%)
    pallas_call x1, Pallas kernels, block(): pl.pallas_call(functools.partial(kernel, n_pix, n_ch), out_shape=(wide, w...  127 us
    pallas_call x1, Pallas kernels, block(): pl.pallas_call(finish, out_shape=tuple((jax.ShapeDtypeStruct(v.shape, v.d...  4.92 us

profile of v2, /device:TPU:0, one launch (start us, length us, event | category | flops | bytes accessed | tf_op | source)
XLA Modules:
  0.0 134.0 jit_solution(15150676249008958293)
XLA Ops:
  0.6 1.4 %reshape.45.mask = s32[28,112]{1,0:T(8,128)} reshape(s32[3136]{0:T(1024)} %param.13) | data formatting | bytes 25088 | tf_op jit(solution)/shard_map/reshape | solution.py:975
  2.0 127.0 %bottleneck.1 = (bf16[28,112,256]{2,1,0:T(8,128)(2,1)}, bf16[28,112,256]{2,1,0:T(8,128)(2,1)}, f32[64,1024]{1,0:T(8,128)}, f32[9,64,256]{2,1,0:T(8,128)}, f32[64,1024]{1,0:T(8,128)}, /*index=5*/f32[8,256]{1,0:T(8,128)}) custom-call(bf16[28,112,256]{2,1,0:T(8,128)(2,1)} %bitcast.12, bf16[28,112,256]{2,1,0:T(8,128)(2,1)} %bitcast.13, s32[28,112]{1,0:T(8,128)} %reshape.45.mask, ...), custom_call_target="tpu_custom_call" | custom-call | tf_op jit(solution)/shard_map/bottleneck/pallas_call | solution.py:955
  129.1 4.9 %outputs.1 = (bf16[28,112,256]{2,1,0:T(8,128)(2,1)}, bf16[28,112,256]{2,1,0:T(8,128)(2,1)}, f32[64,1024]{1,0:T(8,128)}, f32[9,64,256]{2,1,0:T(8,128)}, f32[64,10...) custom-call(bf16[28,112,256]{2,1,0:T(8,128)(2,1)} %get-tuple-element, ...), custom_call_target="tpu_custom_call" | custom-call | tf_op jit(solution)/shard_map/outputs/pallas_call | solution.py:983

commit v3 on v2

--- a/solution.py
+++ b/solution.py
@@ -20,6 +20,7 @@
 PAD = 16
 FLAT = IMAGES * PAD * PAD
 EDGE = 8
+BLOCK = PAD * PAD
 
 
 def mm(a, b):
@@ -107,22 +108,30 @@
     e1s,
     e1r,
     G1,
+    QT,
+    rows28,
     acc_w,
-    acc_s,
     wp,
     wc,
     wa,
+    wb,
     wr,
     wh,
     wf,
     wfin,
+    acc_s,
     sp,
     sc,
-    sa,
-    sr,
+    s1,
+    ys,
+    yr,
+    s2,
+    zs,
+    zr,
+    s3,
+    xs,
+    xr,
     sh,
-    sf,
-    sx,
     sfin,
     ld_sem,
     fx_send,
@@ -138,10 +147,14 @@
     o_recv,
     g_send,
     g_recv,
+    s_send,
+    s_recv,
+    h_send,
+    h_recv,
 ):
     me_p, me_c = lax.axis_index("pix"), lax.axis_index("ch")
     hi, lo = me_c // 2, lax.rem(me_c, 2)
-    n_lo = min(n_pix, 8)
+    n_lo = 8
     n_hi = n_pix // n_lo
     g_hi, g_lo = me_p // n_lo, lax.rem(me_p, n_lo)
     across = (me_p, (1 - hi) * 2 + lo)
@@ -195,6 +208,25 @@
     pk_rows += [v[...].astype(F32).reshape(1, 256) for v in (g3_in, b3_in)]
     pk[me_c] = jnp.concatenate(pk_rows + [jnp.zeros((2, 256), F32)], axis=0)
 
+    flat = mask[...].astype(F32).reshape(1, rows28.shape[0] * ROWS)
+    for t in range(rows28.shape[0]):
+        rows28[t : t + 1, :] = flat[:, t * ROWS : (t + 1) * ROWS]
+    diag = lax.broadcasted_iota(jnp.int32, (ROWS, ROWS), 0) == lax.broadcasted_iota(jnp.int32, (ROWS, ROWS), 1)
+    ones = jnp.ones((ROWS, 128), BF16)
+
+    def put_mask(t, carry):
+        at = mine + jnp.where(t < OWN, part0 + t, part1 + t - OWN)
+        row = rows28[pl.ds(at, 1), :]
+        V[t] = mm(jnp.where(diag, row, 0.0).astype(BF16), ones)
+        return carry
+
+    lax.fori_loop(0, BOTH, put_mask, 0)
+    lanes = jnp.broadcast_to(jnp.sum(rows28[...], axis=0, keepdims=True), (8, ROWS))
+    local_count = mm(lanes.astype(BF16), ones)
+    P0[...] = jnp.zeros_like(P0)
+    PC[0:PAD, :] = jnp.zeros((PAD, 768), BF16)
+    PC[PAD + FLAT :, :] = jnp.zeros((PAD, 768), BF16)
+    w2_load.wait()
     pl.semaphore_wait(barrier, n_all - 1)
 
     fx = [
@@ -237,21 +269,76 @@
     for cp in pkx:
         cp.start()
 
-    diag = lax.broadcasted_iota(jnp.int32, (ROWS, ROWS), 0) == lax.broadcasted_iota(jnp.int32, (ROWS, ROWS), 1)
-    ones = jnp.ones((ROWS, 128), BF16)
-
-    def put_mask(t, carry):
-        at = mine + jnp.where(t < OWN, part0 + t, part1 + t - OWN)
-        row = mask[pl.ds(at, 1), :].astype(F32)
-        V[t] = mm(jnp.where(diag, row, 0.0).astype(BF16), ones)
-        return carry
-
-    lax.fori_loop(0, BOTH, put_mask, 0)
-
-    P0[...] = jnp.zeros_like(P0)
-
     def arrived(dst, sem):
         local(dst, dst, sem).wait()
+
+    def ar_group(kind):
+        if kind == "all":
+            return n_all, me_p * n_ch + me_c, lambda q: (q // n_ch, lax.rem(q, n_ch))
+        if kind == "half":
+            return n_pix * 2, me_p * 2 + lo, lambda q: (q // 2, hi * 2 + lax.rem(q, 2))
+        return n_pix, me_p, lambda q: (q, me_c)
+
+    def ar_start(k, val, kind):
+        n, me, device = ar_group(kind)
+        rows = val.shape[0]
+        sbuf[k, 0:rows] = val
+        rbuf[k, me, 0:rows] = val
+
+        def send(t, carry):
+            to = device(lax.rem(me + t, n))
+            cut = pl.ds(0, rows)
+            remote(sbuf.at[k, cut], rbuf.at[k, me, cut], ar_send.at[k], ar_recv.at[k], to).start()
+            return carry
+
+        lax.fori_loop(1, n, send, 0)
+
+    def ar_finish(k, kind, rows):
+        n = ar_group(kind)[0]
+        arrived(rbuf.at[k, pl.ds(0, n - 1), pl.ds(0, rows)], ar_recv.at[k])
+        return jnp.sum(rbuf[k, 0:n, 0:rows], axis=0)
+
+    def ar_close(k, kind, rows):
+        n = ar_group(kind)[0]
+        arrived(rbuf.at[k, pl.ds(0, n - 1), pl.ds(0, rows)], ar_send.at[k])
+
+    def pack2(a, b):
+        return jnp.concatenate([a[:, 0:128], a[:, 128:256], b[:, 0:128], b[:, 128:256]], axis=0)
+
+    def unpack2(v):
+        return (
+            jnp.concatenate([v[0:1], v[1:2]], axis=1),
+            jnp.concatenate([v[2:3], v[3:4]], axis=1),
+        )
+
+    def pack3(a, b):
+        return jnp.concatenate([a[:, 128 * i : 128 * (i + 1)] for i in range(4)] + [b[:, 128 * i : 128 * (i + 1)] for i in range(4)], axis=0)
+
+    def unpack3(v):
+        return (
+            jnp.concatenate([v[i : i + 1] for i in range(4)], axis=1),
+            jnp.concatenate([v[i : i + 1] for i in range(4, 8)], axis=1),
+        )
+
+    ar_start(6, local_count, "pix")
+
+    far = (1 - hi) * 2 + lo
+
+    def w2_piece(slot, q):
+        return W2T.at[slot, :, pl.ds(pl.multiple_of(q // 2 * 16, 16), 16), pl.ds(pl.multiple_of(lax.rem(q, 2) * 128, 128), 128)]
+
+    w2x_across = remote(w2_piece(me_c, g_lo), w2_piece(me_c, g_lo), w_send.at[12], w_recv.at[12], across)
+    w2x_across.start()
+    w2x_beside = remote(W2T.at[me_c], W2T.at[me_c], w_send.at[13], w_recv.at[13], beside)
+    w2x_pass = remote(W2T.at[far], W2T.at[far], w_send.at[14], w_recv.at[14], beside)
+    w2x_share = []
+    for t in range(1, n_lo):
+        q = lax.rem(g_lo + t, n_lo)
+        w2x_share.append(
+            remote(
+                w2_piece(far, g_lo), w2_piece(far, g_lo), w_send.at[15 + t], w_recv.at[15 + t], (g_hi * n_lo + q, me_c)
+            )
+        )
 
     for t, dev, h in others:
         q = dev[1]
@@ -285,13 +372,10 @@
 
     lax.fori_loop(0, OWN, keep_first, 0)
 
-    w2x_across = remote(W2T.at[me_c], W2T.at[me_c], w_send.at[12], w_recv.at[12], across)
-    w2x_beside = remote(W2T.at[me_c], W2T.at[me_c], w_send.at[13], w_recv.at[13], beside)
-    far = (1 - hi) * 2 + lo
-    w2x_pass = remote(W2T.at[far], W2T.at[far], w_send.at[14], w_recv.at[14], beside)
-    w2_load.wait()
+    arrived(w2_piece(far, g_lo), w_recv.at[12])
+    for cp in w2x_share:
+        cp.start()
     w2x_beside.start()
-    w2x_across.start()
     cx[0].start()
     cx[1].start()
     for t, dev, h in others:
@@ -302,73 +386,25 @@
     g3 = jnp.concatenate([pair0[4:5], pair1[4:5]], axis=1)
     b3 = jnp.concatenate([pair0[5:6], pair1[5:6]], axis=1)
 
-    def ar_start(k, val, half):
-        n = n_pix * 2 if half else n_all
-        me = me_p * 2 + lo if half else me_p * n_ch + me_c
-        sbuf[k] = val
-        rbuf[k, me] = val
-
-        def send(t, carry):
-            q = lax.rem(me + t, n)
-            dev = (q // 2, hi * 2 + lax.rem(q, 2)) if half else (q // n_ch, lax.rem(q, n_ch))
-            remote(sbuf.at[k], rbuf.at[k, me], ar_send.at[k], ar_recv.at[k], dev).start()
-            return carry
-
-        lax.fori_loop(1, n, send, 0)
-
-    def ar_finish(k, half):
-        n = n_pix * 2 if half else n_all
-        span = rbuf.at[k, pl.ds(0, n - 1)]
-        arrived(span, ar_recv.at[k])
-        total = jnp.sum(rbuf[k, 0:n], axis=0)
-        return total
-
-    def ar_close(k, half):
-        n = n_pix * 2 if half else n_all
-        span = rbuf.at[k, pl.ds(0, n - 1)]
-        arrived(span, ar_send.at[k])
-
-    def pack2(a, b, extra=None):
-        tail = jnp.zeros((1, 128), F32) if extra is None else extra
-        return jnp.concatenate(
-            [a[:, 0:128], a[:, 128:256], b[:, 0:128], b[:, 128:256], tail, jnp.zeros((3, 128), F32)], axis=0
-        )
-
-    def unpack2(v):
-        return (
-            jnp.concatenate([v[0:1], v[1:2]], axis=1),
-            jnp.concatenate([v[2:3], v[3:4]], axis=1),
-        )
-
-    def pack3(a, b):
-        return jnp.concatenate([a[:, 128 * i : 128 * (i + 1)] for i in range(4)] + [b[:, 128 * i : 128 * (i + 1)] for i in range(4)], axis=0)
-
-    def unpack3(v):
-        return (
-            jnp.concatenate([v[i : i + 1] for i in range(4)], axis=1),
-            jnp.concatenate([v[i : i + 1] for i in range(4, 8)], axis=1),
-        )
-
     zero = jnp.zeros((8, 256), F32)
 
     def sum_first(t, carry):
-        s, q, n = carry
+        s, q = carry
         xcopy(0, h1s, h1r, t).wait_recv()
         h = H1[t] + h1r[t].astype(F32)
         H1[t] = h
         h1b[t] = h.astype(BF16)
-        v = V[t]
-        vh = spread(v, 256) * h
-        return s + fold8(vh), q + fold8(vh * h), n + fold8(v)
-
-    s, q, n = lax.fori_loop(0, OWN, sum_first, (zero, zero, jnp.zeros((8, 128), F32)))
-    ar_start(0, pack2(fold1(s), fold1(q), fold1(n)), False)
-    arrived(W2T.at[far], w_recv.at[12])
+        vh = spread(V[t], 256) * h
+        return s + fold8(vh), q + fold8(vh * h)
+
+    s, q = lax.fori_loop(0, OWN, sum_first, (zero, zero))
+    ar_start(0, pack2(fold1(s), fold1(q)), "all")
+    for t in range(1, n_lo):
+        arrived(w2_piece(far, lax.rem(g_lo - t + n_lo, n_lo)), w_recv.at[15 + t])
     w2x_pass.start()
-    total = ar_finish(0, False)
-    s, q = unpack2(total)
-    inv_n = 1.0 / spread(total[4:5], 512)
+    inv_n = 1.0 / spread(ar_finish(6, "pix", 8)[0:1], 512)
     inv_n2 = inv_n[:, 0:256]
+    s, q = unpack2(ar_finish(0, "all", 4))
     avg1 = s * inv_n2
     scale1 = lax.rsqrt(q * inv_n2 - avg1 * avg1 + EPS)
     a1_gain = g1 * scale1
@@ -392,8 +428,8 @@
                     (i * SIDE + y) * SIDE : (i * SIDE + y + 1) * SIDE, :
                 ]
 
-    def from_padded(dst):
-        for i in range(IMAGES):
+    def from_padded(dst, images):
+        for i in images:
             for y in range(SIDE):
                 dst[(i * SIDE + y) * SIDE : (i * SIDE + y + 1) * SIDE, :] = padded[
                     (i * SIDE + y) * PAD : (i * SIDE + y) * PAD + SIDE, :
@@ -403,7 +439,7 @@
     for i in range(IMAGES):
         for c in range(3):
             at = EDGE + i * 256 + c - 1
-            PC[i * 256 : (i + 1) * 256, 256 * c : 256 * (c + 1)] = P0[at : at + 256, :].astype(BF16)
+            PC[PAD + i * BLOCK : PAD + (i + 1) * BLOCK, 256 * c : 256 * (c + 1)] = P0[at : at + BLOCK, :].astype(BF16)
 
     arrived(W2T.at[hi * 2 + 1 - lo], w_recv.at[13])
     arrived(W2T.at[(1 - hi) * 2 + 1 - lo], w_recv.at[14])
@@ -414,26 +450,34 @@
     def conv(i, carry):
         total = None
         for r in range(3):
-            rows = PC[pl.ds(pl.multiple_of(i * 256 + 16 * r, 16), SIDE * PAD), :]
+            rows = PC[pl.ds(pl.multiple_of(PAD + i * BLOCK + PAD * r, 16), SIDE * PAD), :]
             part = mm_nt(rows, jnp.concatenate([W2T[:, 3 * r + c].reshape(256, 256) for c in range(3)], axis=1))
             total = part if total is None else total + part
         padded[pl.ds(pl.multiple_of(i * SIDE * PAD, 16), SIDE * PAD), :] = total
         return carry
 
-    lax.fori_loop(0, IMAGES, conv, 0)
-    from_padded(H2)
-
     def sum_second(t, carry):
         s, q = carry
         h = H2[pl.ds(pl.multiple_of(t * ROWS, 16), ROWS), :]
         h2s[t] = h.astype(BF16)
-        xcopy(1, h2s, h2r, t).start()
         vh = spread(V[t], 256) * h
         return s + fold8(vh), q + fold8(vh * h)
 
-    s, q = lax.fori_loop(0, OWN, sum_second, (zero, zero))
-    ar_start(1, pack2(fold1(s), fold1(q)), False)
-    s, q = unpack2(ar_finish(1, False))
+    def start_all(kind, src, dst, first, last):
+        for t in range(first, last):
+            xcopy(kind, src, dst, t).start()
+
+    early = 2
+    lax.fori_loop(0, 2, conv, 0)
+    from_padded(H2, (0, 1))
+    carry = lax.fori_loop(0, 3, sum_second, (zero, zero))
+    start_all(1, h2s, h2r, 0, early)
+    lax.fori_loop(2, IMAGES, conv, 0)
+    from_padded(H2, (2, 3))
+    s, q = lax.fori_loop(3, OWN, sum_second, carry)
+    ar_start(1, pack2(fold1(s), fold1(q)), "all")
+    start_all(1, h2s, h2r, early, OWN)
+    s, q = unpack2(ar_finish(1, "all", 4))
     avg2 = s * inv_n2
     scale2 = lax.rsqrt(q * inv_n2 - avg2 * avg2 + EPS)
     a2_gain = g2 * scale2
@@ -466,14 +510,14 @@
     wide_zero = jnp.zeros((8, 512), F32)
     carry = lax.fori_loop(0, OWN, own_second, (wide_zero, wide_zero))
     s, q = lax.fori_loop(0, OWN, other_second, carry)
-    ar_start(2, pack3(fold1(s), fold1(q)), True)
+    ar_start(2, pack3(fold1(s), fold1(q)), "half")
     for cp in h1x:
         cp.start()
     for cp in c_load:
         cp.wait()
     for cp in cx:
         cp.wait_recv()
-    s, q = unpack3(ar_finish(2, True))
+    s, q = unpack3(ar_finish(2, "half", 8))
     avg3 = s * inv_n
     scale3 = lax.rsqrt(q * inv_n - avg3 * avg3 + EPS)
     a3_gain = g3 * scale3
@@ -496,7 +540,7 @@
         return s + fold8(vg), q + fold8(vg * (h3 - avg3))
 
     s, q = lax.fori_loop(0, BOTH, last, (wide_zero, wide_zero))
-    ar_start(3, pack3(fold1(s), fold1(q * scale3)), True)
+    ar_start(3, pack3(fold1(s), fold1(q * scale3)), "half")
     parts = ((0, part0), (1, part1))
     res_here = [
         local(RES.at[lo, pl.ds(OWN * s, OWN)], res_out.at[pl.ds(mine + part, OWN)], out_sem.at[s]) for s, part in parts
@@ -505,9 +549,9 @@
         remote(RES.at[1 - lo, pl.ds(OWN * s, OWN)], res_out.at[pl.ds(mine + part, OWN)], o_send.at[s], o_recv.at[s], beside)
         for s, part in parts
     ]
+    shift3, gain3 = unpack3(ar_finish(3, "half", 8))
     for cp in res_here + res_there:
         cp.start()
-    shift3, gain3 = unpack3(ar_finish(3, True))
     k3_h = -a3_gain * gain3 * scale3 * inv_n
     k3_0 = -a3_gain * shift3 * inv_n - k3_h * avg3
 
@@ -522,7 +566,11 @@
     def other_third(t, carry):
         e, s, q = back_third(t + OWN, (carry[0], carry[1], h2r[t].astype(F32)))
         e2s[t] = e.astype(BF16)
-        xcopy(2, e2s, e2r, t).start()
+
+        @pl.when(t < 4)
+        def _():
+            xcopy(2, e2s, e2r, t).start()
+
         return s, q
 
     def own_third(t, carry):
@@ -532,30 +580,38 @@
 
     carry = lax.fori_loop(0, OWN, other_third, (zero, zero))
     s, q = lax.fori_loop(0, OWN, own_third, carry)
-    ar_start(4, pack2(fold1(s), fold1(q * scale2)), False)
-
-    piece = 128 // n_lo
-    n_sub = n_lo // 2
-
-    def pair_copies(k, part, got):
-        return [
-            remote(part.at[h, 1 - lo], got.at[h], g_send.at[k, h], g_recv.at[k, h], beside) for h in range(2)
-        ]
-
-    def pair_add(k, part, got, acc):
-        for h, cp in enumerate(pair_copies(k, part, got)):
+    ar_start(4, pack2(fold1(s), fold1(q * scale2)), "all")
+    start_all(2, e2s, e2r, 4, OWN)
+
+    piece = 16
+    n_sub = 4
+
+    def pair_copies(k):
+        return [remote(wp.at[k, h], wc.at[k, h], g_send.at[k, h], g_recv.at[k, h], beside) for h in range(2)]
+
+    def pair_start(k):
+        for h in range(2):
+            wp[k, h] = acc_w[k, h, 1 - lo].astype(BF16)
+        for cp in pair_copies(k):
+            cp.start()
+
+    def pair_add(k):
+        for h, cp in enumerate(pair_copies(k)):
             cp.wait_recv()
-            both = part[h, lo].astype(F32) + got[h].astype(F32)
-            acc[h] = both.astype(BF16).reshape(acc.shape[1:])
-
-    def spread_copies(k, acc, got):
+            both = (acc_w[k, h, lo] + wc[k, h].astype(F32)).reshape(n_sub, piece, 512)
+            wa[k, h] = both
+            wb[k, h] = both.astype(BF16)
+        for cp in spread_copies(k):
+            cp.start()
+
+    def spread_copies(k):
         copies = []
         for t in range(1, n_lo):
             q = lax.rem(g_lo + t, n_lo)
             copies.append(
                 remote(
-                    acc.at[lax.rem(q, 2), q // 2],
-                    got.at[g_lo],
+                    wb.at[k, lax.rem(q, 2), q // 2],
+                    wr.at[k, g_lo],
                     g_send.at[k, 2 + t],
                     g_recv.at[k, 2 + t],
                     (g_hi * n_lo + q, me_c),
@@ -563,37 +619,45 @@
             )
         return copies
 
-    def spread_add(k, acc, got, level):
-        for cp in spread_copies(k, acc, got):
+    def over_groups(total, level, sems):
+        if n_hi == 1:
+            return total
+        level[g_hi] = total.astype(BF16)
+
+        def swap(t):
+            q = lax.rem(g_hi + t, n_hi)
+            return remote(
+                level.at[g_hi], level.at[g_hi], sems[0].at[t], sems[1].at[t], (q * n_lo + g_lo, me_c)
+            )
+
+        for t in range(1, n_hi):
+            swap(t).start()
+        for t in range(1, n_hi):
+            swap(t).wait()
+        total = level[0].astype(F32)
+        for t in range(1, n_hi):
+            total = total + level[t].astype(F32)
+        return total
+
+    def spread_add(k):
+        for cp in spread_copies(k):
             cp.wait_recv()
-        total = acc[lax.rem(g_lo, 2), g_lo // 2].astype(F32)
+        total = wa[k, lax.rem(g_lo, 2), g_lo // 2]
         for t in range(1, n_lo):
-            total = total + got[lax.rem(g_lo + t, n_lo)].astype(F32)
-        if n_hi > 1:
-            level[g_hi] = total.astype(BF16)
-
-            def swap(t):
-                q = lax.rem(g_hi + t, n_hi)
-                return remote(
-                    level.at[g_hi], level.at[g_hi], g_send.at[k, 27 + t], g_recv.at[k, 27 + t], (q * n_lo + g_lo, me_c)
-                )
-
-            for t in range(1, n_hi):
-                swap(t).start()
-            for t in range(1, n_hi):
-                swap(t).wait()
-            total = level[0].astype(F32)
-            for t in range(1, n_hi):
-                total = total + level[t].astype(F32)
-        return total
-
-    def give_copies(k, done, fin, to_hi, first=0):
+            total = total + wr[k, lax.rem(g_lo + t, n_lo)].astype(F32)
+        return over_groups(total, wh.at[k], (h_send.at[k], h_recv.at[k]))
+
+    def give_copies(k):
         copies = []
-        for t in range(first, n_lo):
+        for t in range(n_lo):
             q = lax.rem(g_lo + t, n_lo)
             copies.append(
                 remote(
-                    done, fin, g_send.at[k, 10 + t], g_recv.at[k, 10 + 8 * hi + t], (g_hi * n_lo + q, to_hi * 2 + lo)
+                    wf.at[k],
+                    wfin.at[k, hi, own_sub],
+                    g_send.at[k, 10 + t],
+                    g_recv.at[k, 10 + 8 * hi + t],
+                    (g_hi * n_lo + q, owner_hi * 2 + lo),
                 )
             )
         return copies
@@ -602,9 +666,9 @@
     own_sub = g_lo // 2
     keeps = owner_hi == hi
 
-    def wide_give(k, slot):
-        copies = give_copies(k, wf.at[slot], wfin.at[slot, hi, own_sub], owner_hi)
-        for t, cp in enumerate(copies):
+    def wide_give(k):
+        wf[k] = spread_add(k).astype(BF16)
+        for t, cp in enumerate(give_copies(k)):
             if t == 0:
 
                 @pl.when(jnp.logical_not(keeps))
@@ -613,12 +677,12 @@
 
                 @pl.when(keeps)
                 def _():
-                    wfin[slot, hi, own_sub] = wf[slot]
+                    wfin[k, hi, own_sub] = wf[k]
 
             else:
                 cp.start()
 
-    def wide_take(k, slot, out):
+    def wide_take(k, out):
         for sub in range(n_sub):
             q = sub * 2 + hi
             t = lax.rem(g_lo - q + n_lo, n_lo)
@@ -626,17 +690,15 @@
 
                 @pl.when(jnp.logical_not((q == g_lo) & (hi == h)))
                 def _():
-                    arrived(wfin.at[slot, h, sub], g_recv.at[k, 10 + 8 * h + t])
+                    arrived(wfin.at[k, h, sub], g_recv.at[k, 10 + 8 * h + t])
 
         for h in range(2):
-            out[:, 512 * h : 512 * (h + 1)] = wfin[slot, h].astype(F32).reshape(64, 512)
-
-    def wide_close(k, slot):
-        for cp in pair_copies(k, wp.at[slot], wc.at[slot]):
+            out[:, 512 * h : 512 * (h + 1)] = wfin[k, h].astype(F32).reshape(64, 512)
+
+    def wide_close(k):
+        for cp in pair_copies(k) + spread_copies(k):
             cp.wait_send()
-        for cp in spread_copies(k, wa.at[slot], wr.at[slot]):
-            cp.wait_send()
-        for t, cp in enumerate(give_copies(k, wf.at[slot], wfin.at[slot, hi, own_sub], owner_hi)):
+        for t, cp in enumerate(give_copies(k)):
             if t == 0:
 
                 @pl.when(jnp.logical_not(keeps))
@@ -646,22 +708,14 @@
             else:
                 cp.wait_send()
 
-    def wide_part(slot, left, right_of):
-        acc_w[...] = jnp.zeros_like(acc_w)
-
-        def add(t, carry):
-            a = left[pl.ds(2 * t, 2)].reshape(2 * ROWS, 256)
-            acc_w[...] += mm_tn(a, right_of(t))
-            return carry
-
-        lax.fori_loop(0, OWN, add, 0)
-        wp[slot] = acc_w[...].astype(BF16).reshape(2, 2, 64, 512)
-
-    wide_part(0, A2, lambda t: G3[pl.ds(2 * t, 2)].reshape(2 * ROWS, 512))
-    for cp in pair_copies(0, wp.at[0], wc.at[0]):
-        cp.start()
-
-    shift2, gain2 = unpack2(ar_finish(4, False))
+    def half_of(ref, part):
+        return ref[OWN * part : OWN * (part + 1)].reshape(OWN * ROWS, ref.shape[2])
+
+    acc_w[0] = (mm_tn(half_of(A2, 0), half_of(G3, 0)) + mm_tn(half_of(A2, 1), half_of(G3, 1))).reshape(2, 2, 64, 512)
+    pair_start(0)
+    pair_add(0)
+
+    shift2, gain2 = unpack2(ar_finish(4, "all", 4))
     k2_h = -a2_gain * gain2 * scale2 * inv_n2
     k2_0 = -a2_gain * shift2 * inv_n2 - k2_h * avg2
 
@@ -676,17 +730,13 @@
     to_padded()
     for i in range(IMAGES):
         for c in range(3):
-            at = EDGE + i * 256 - (c - 1)
-            Q[c, i * 256 : (i + 1) * 256, :] = P0[at : at + 256, :].astype(BF16)
-
-    pair_add(0, wp.at[0], wc.at[0], wa.at[0])
-    for cp in spread_copies(0, wa.at[0], wr.at[0]):
-        cp.start()
+            at = EDGE + i * BLOCK - (c - 1)
+            Q[c, i * BLOCK : (i + 1) * BLOCK, :] = P0[at : at + BLOCK, :].astype(BF16)
 
     def conv_back(i, carry):
         total = None
         for r in range(3):
-            at = pl.ds(pl.multiple_of(i * 256 + 16 * (2 - r), 16), SIDE * PAD)
+            at = pl.ds(pl.multiple_of(i * BLOCK + PAD * (2 - r), 16), SIDE * PAD)
             for c in range(3):
                 w = W2T[:, 3 * r + c].reshape(256, 256)
                 part = mm(Q[c, at, :], w)
@@ -694,38 +744,151 @@
         padded[pl.ds(pl.multiple_of(i * SIDE * PAD, 16), SIDE * PAD), :] = total
         return carry
 
-    lax.fori_loop(0, IMAGES, conv_back, 0)
-    from_padded(comp)
-
     def sum_back_first(t, carry):
         s, q = carry
         e = comp[pl.ds(pl.multiple_of(t * ROWS, 16), ROWS), :] * D1[t]
         E1[t] = e
         e1s[t] = e.astype(BF16)
-        xcopy(3, e1s, e1r, t).start()
         return s + fold8(e), q + fold8(e * (H1[t] - avg1))
 
-    s, q = lax.fori_loop(0, OWN, sum_back_first, (zero, zero))
-    ar_start(5, pack2(fold1(s), fold1(q * scale1)), False)
-
-    wf[0] = spread_add(0, wa.at[0], wr.at[0], wh.at[0]).astype(BF16)
-    wide_give(0, 0)
-
-    acc_s[...] = jnp.zeros_like(acc_s)
-
-    def taps(i, carry):
-        left = Q[1, pl.ds(pl.multiple_of(i * 256 + 16, 16), SIDE * PAD), :]
-        for r in range(3):
-            right = PC[pl.ds(pl.multiple_of(i * 256 + 16 * r, 16), SIDE * PAD), :]
-            acc_s[:, 768 * r : 768 * (r + 1)] += mm_tn(left, right)
-        return carry
-
-    lax.fori_loop(0, IMAGES, taps, 0)
-    sp[...] = acc_s[...].astype(BF16).reshape(2, 2, 64, 2304)
-    for cp in pair_copies(2, sp, sc):
-        cp.start()
-
-    shift1, gain1 = unpack2(ar_finish(5, False))
+    lax.fori_loop(0, 2, conv_back, 0)
+    from_padded(comp, (0, 1))
+    carry = lax.fori_loop(0, 3, sum_back_first, (zero, zero))
+    start_all(3, e1s, e1r, 0, early)
+    lax.fori_loop(2, IMAGES, conv_back, 0)
+    from_padded(comp, (2, 3))
+    s, q = lax.fori_loop(3, OWN, sum_back_first, carry)
+    ar_start(5, pack2(fold1(s), fold1(q * scale1)), "all")
+    start_all(3, e1s, e1r, early, OWN)
+
+    bit, quad = lax.rem(g_lo, 2), g_lo // 2
+    next_group = (g_hi * n_lo + quad * 2 + 1 - bit, me_c)
+    s_owner = lax.rem(quad, 2) == hi
+
+    def s_pair(r):
+        return [
+            remote(sp.at[r, h], sc.at[r, h], s_send.at[r, h], s_recv.at[r, h], beside) for h in range(2)
+        ]
+
+    def s_next(r):
+        return remote(ys.at[r], yr.at[r], s_send.at[r, 2], s_recv.at[r, 2], next_group)
+
+    def s_quad(r):
+        copies = []
+        for t in range(1, 4):
+            q = lax.rem(quad + t, 4)
+            copies.append(
+                remote(
+                    zs.at[r, lax.rem(q, 2), q // 2],
+                    zr.at[r, t - 1],
+                    s_send.at[r, 2 + t],
+                    s_recv.at[r, 2 + t],
+                    (g_hi * n_lo + q * 2 + bit, me_c),
+                )
+            )
+        return copies
+
+    def s_cross(r):
+        return remote(xs.at[r], xr.at[r], s_send.at[r, 6], s_recv.at[r, 6], across)
+
+    def s_give(r):
+        copies = []
+        for t in range(1, 4):
+            q = lax.rem(quad + t, 4)
+            spot = sfin.at[r, bit, quad // 2]
+            copies.append(
+                remote(
+                    spot, spot, s_send.at[r, 6 + t], s_recv.at[r, 7 + quad // 2], (g_hi * n_lo + q * 2 + bit, me_c)
+                )
+            )
+        return copies
+
+    def s_back(r):
+        return remote(sfin.at[r, bit], sfin.at[r, bit], s_send.at[r, 10], s_recv.at[r, 10], next_group)
+
+    def s_make(r):
+        taps = mm(QT[...], PC[PAD * r : PAD * r + FLAT, :])
+        acc_s[r] = taps.reshape(2, 2, 64, 768)
+        for h in range(2):
+            sp[r, h] = acc_s[r, h, 1 - lo].astype(BF16)
+        for cp in s_pair(r):
+            cp.start()
+
+    def s_pair_add(r):
+        for h, cp in enumerate(s_pair(r)):
+            cp.wait_recv()
+            s1[r, h] = (acc_s[r, h, lo] + sc[r, h].astype(F32)).reshape(2, 32, 768)
+            ys[r, h] = s1[r, h, 1 - bit].astype(BF16)
+        s_next(r).start()
+
+    def s_next_add(r):
+        s_next(r).wait_recv()
+        for h in range(2):
+            s2[r, h] = (s1[r, h, bit] + yr[r, h].astype(F32)).reshape(2, 16, 768)
+            zs[r, h] = s2[r, h].astype(BF16)
+        for cp in s_quad(r):
+            cp.start()
+
+    def s_quad_add(r):
+        for cp in s_quad(r):
+            cp.wait_recv()
+        total = s2[r, lax.rem(quad, 2), quad // 2]
+        for t in range(3):
+            total = total + zr[r, t].astype(F32)
+        s3[r] = total
+        xs[r] = total.astype(BF16)
+
+        @pl.when(jnp.logical_not(s_owner))
+        def _():
+            s_cross(r).start()
+
+    def s_cross_add(r):
+        @pl.when(s_owner)
+        def _():
+            s_cross(r).wait_recv()
+            total = s3[r] + xr[r].astype(F32)
+            sfin[r, bit, quad // 2] = over_groups(total, sh.at[r], (h_send.at[2 + r], h_recv.at[2 + r])).astype(BF16)
+            for cp in s_give(r):
+                cp.start()
+
+    def s_give_back(r):
+        for part in range(2):
+
+            @pl.when(quad != 2 * part + hi)
+            def _():
+                arrived(sfin.at[r, bit, part], s_recv.at[r, 7 + part])
+
+        s_back(r).start()
+
+    def s_take(r):
+        arrived(sfin.at[r, 1 - bit], s_recv.at[r, 10])
+        rows = sfin[r].astype(F32).reshape(64, 768)
+        for c in range(3):
+            sg_out[3 * r + c] = rows[:, 256 * c : 256 * (c + 1)]
+
+    def s_close(r):
+        for cp in s_pair(r) + [s_next(r)] + s_quad(r) + [s_back(r)]:
+            cp.wait_send()
+
+        @pl.when(s_owner)
+        def _():
+            for cp in s_give(r):
+                cp.wait_send()
+
+        @pl.when(jnp.logical_not(s_owner))
+        def _():
+            s_cross(r).wait_send()
+
+    for i in range(IMAGES):
+        QT[:, i * BLOCK : (i + 1) * BLOCK] = P0[EDGE + i * BLOCK : EDGE + (i + 1) * BLOCK, :].T.astype(BF16)
+    s_make(0)
+    s_make(1)
+    s_pair_add(0)
+    s_make(2)
+    s_pair_add(1)
+    s_pair_add(2)
+
+    shift1, gain1 = unpack2(ar_finish(5, "all", 4))
     k1_h = -a1_gain * gain1 * scale1 * inv_n2
     k1_0 = -a1_gain * shift1 * inv_n2 - k1_h * avg1
 
@@ -758,9 +921,15 @@
     lax.fori_loop(0, OWN, own_back_first, 0)
     ig_here[0].start()
     ig_there[0].start()
-    pair_add(2, sp, sc, sa)
-    for cp in spread_copies(2, sa, sr):
-        cp.start()
+    s_next_add(0)
+
+    def features_of(part):
+        return jnp.concatenate([half_of(F.at[0], part), half_of(F.at[1], part)], axis=1)
+
+    own_reduce = mm_tn(half_of(G1, 0), features_of(0))
+    acc_w[1] = own_reduce.reshape(2, 2, 64, 512)
+    s_next_add(1)
+    wide_give(0)
     for cp in h1x:
         cp.wait_recv()
 
@@ -770,42 +939,21 @@
         return carry
 
     lax.fori_loop(0, OWN, other_back_first, 0)
+    acc_w[1] += mm_tn(half_of(G1, 1), features_of(1)).reshape(2, 2, 64, 512)
+    pair_start(1)
     ig_here[1].start()
     ig_there[1].start()
-
-    def features_of(t):
-        left = F[0, pl.ds(2 * t, 2)].reshape(2 * ROWS, 256)
-        right = F[1, pl.ds(2 * t, 2)].reshape(2 * ROWS, 256)
-        return jnp.concatenate([left, right], axis=1)
-
-    wide_part(1, G1, features_of)
-    for cp in pair_copies(1, wp.at[1], wc.at[1]):
-        cp.start()
-
-    pair_add(1, wp.at[1], wc.at[1], wa.at[1])
-    for cp in spread_copies(1, wa.at[1], wr.at[1]):
-        cp.start()
-    sf[...] = spread_add(2, sa, sr, sh).astype(BF16)
-    cross = remote(sf, sx, g_send.at[2, 26], g_recv.at[2, 26], across)
-
-    @pl.when(jnp.logical_not(keeps))
-    def _():
-        cross.start()
-
-    wf[1] = spread_add(1, wa.at[1], wr.at[1], wh.at[1]).astype(BF16)
-    wide_give(1, 1)
-
-    def s_copies():
-        return give_copies(2, sf, sfin.at[own_sub], hi, 1)
-
-    @pl.when(keeps)
-    def _():
-        cross.wait_recv()
-        total = (sf[...].astype(F32) + sx[...].astype(F32)).astype(BF16)
-        sf[...] = total
-        sfin[own_sub] = total
-        for cp in s_copies():
-            cp.start()
+    s_quad_add(0)
+    s_next_add(2)
+    pair_add(1)
+    s_quad_add(1)
+    s_cross_add(0)
+    s_quad_add(2)
+    s_cross_add(1)
+    wide_give(1)
+    s_cross_add(2)
+    for r in range(3):
+        s_give_back(r)
 
     def own64(v):
         half = jnp.where(hi == 0, v[:, 0:128], v[:, 128:256])
@@ -828,55 +976,43 @@
         axis=0,
     )
 
-    wide_take(0, 0, eg_out)
-    wide_take(1, 1, rg_out)
-    for sub in range(n_sub):
-        q = sub * 2 + hi
-        t = lax.rem(g_lo - q + n_lo, n_lo)
-
-        @pl.when(q != g_lo)
-        def _():
-            arrived(sfin.at[sub], g_recv.at[2, 10 + 8 * hi + t])
-
-    for k in range(9):
-        sg_out[k] = sfin[:, :, 256 * k : 256 * (k + 1)].astype(F32).reshape(64, 256)
-
-    wide_close(0, 0)
-    wide_close(1, 1)
-    for cp in pair_copies(2, sp, sc) + spread_copies(2, sa, sr):
-        cp.wait_send()
-
-    @pl.when(keeps)
-    def _():
-        for cp in s_copies():
-            cp.wait_send()
-
-    @pl.when(jnp.logical_not(keeps))
-    def _():
-        cross.wait_send()
-
+    wide_take(0, eg_out)
+    for r in range(3):
+        s_take(r)
+    wide_take(1, rg_out)
+
+    wide_close(0)
+    wide_close(1)
+    for r in range(3):
+        s_close(r)
     for cp in ig_here:
         cp.wait()
     for cp in ig_there:
         cp.wait()
     for cp in res_there:
         cp.wait_recv()
-    for cp in fx + cx + w1x + pkx + w3x + h1x + [w2x_across, w2x_beside, w2x_pass]:
+    for cp in fx + cx + w1x + pkx + w3x + h1x + w2x_share + [w2x_across, w2x_beside, w2x_pass]:
         cp.wait_send()
     for kind, src, dst in ((0, h1s, h1r), (1, h2s, h2r), (2, e2s, e2r), (3, e1s, e1r)):
         for t in range(OWN):
             xcopy(kind, src, dst, t).wait_send()
-    for k, half in ((0, False), (1, False), (2, True), (3, True), (4, False), (5, False)):
-        ar_close(k, half)
+    for k, kind, rows in (
+        (0, "all", 4),
+        (1, "all", 4),
+        (2, "half", 8),
+        (3, "half", 8),
+        (4, "all", 4),
+        (5, "all", 4),
+        (6, "pix", 8),
+    ):
+        ar_close(k, kind, rows)
 
 
 def block(n_pix, n_ch, *args):
     feat, cot, mask, w1, w2, w3 = args[:6]
     rows, lanes = feat.shape
-    n_lo = min(n_pix, 8)
+    n_lo, n_sub, piece = 8, 4, 16
     n_hi = n_pix // n_lo
-    piece = 128 // n_lo
-    n_sub = n_lo // 2
     chunks = rows // ROWS
     any_space = pl.BlockSpec(memory_space=pl.ANY)
     vmem = pl.BlockSpec(memory_space=pltpu.VMEM)
@@ -890,8 +1026,8 @@
         V((4, 9, 64, 256), BF16),
         V((4, 64, 512), BF16),
         V((4, 8, 256), F32),
-        V((6, 8, 128), F32),
-        V((6, n_pix * n_ch, 8, 128), F32),
+        V((7, 8, 128), F32),
+        V((7, n_pix * n_ch, 8, 128), F32),
         V((OWN, ROWS, 256), BF16),
         V((OWN, ROWS, 256), BF16),
         V((OWN, ROWS, 256), F32),
@@ -900,7 +1036,7 @@
         V((OWN, ROWS, 256), F32),
         V((OWN * ROWS, 256), F32),
         V((FLAT + 2 * EDGE, 256), F32),
-        V((FLAT, 768), BF16),
+        V((FLAT + 2 * PAD, 768), BF16),
         V((3, FLAT, 256), BF16),
         V((IMAGES * SIDE * PAD, 256), F32),
         V((OWN * ROWS, 256), F32),
@@ -919,37 +1055,49 @@
         V((OWN, ROWS, 256), BF16),
         V((OWN, ROWS, 256), BF16),
         V((BOTH, ROWS, 256), BF16),
-        V((256, 512), F32),
-        V((256, 2304), F32),
-        V((2, 2, 2, 64, 512), BF16),
+        V((256, FLAT), BF16),
+        V((chunks, ROWS), F32),
+        V((2, 2, 2, 64, 512), F32),
         V((2, 2, 64, 512), BF16),
+        V((2, 2, 64, 512), BF16),
+        V((2, 2, n_sub, piece, 512), F32),
         V((2, 2, n_sub, piece, 512), BF16),
         V((2, n_lo, piece, 512), BF16),
         V((2, n_hi, piece, 512), BF16),
         V((2, piece, 512), BF16),
         V((2, 2, n_sub, piece, 512), BF16),
-        V((2, 2, 64, 2304), BF16),
-        V((2, 64, 2304), BF16),
-        V((2, n_sub, piece, 2304), BF16),
-        V((n_lo, piece, 2304), BF16),
-        V((n_hi, piece, 2304), BF16),
-        V((piece, 2304), BF16),
-        V((piece, 2304), BF16),
-        V((n_sub, piece, 2304), BF16),
+        V((3, 2, 2, 64, 768), F32),
+        V((3, 2, 64, 768), BF16),
+        V((3, 2, 64, 768), BF16),
+        V((3, 2, 2, 32, 768), F32),
+        V((3, 2, 32, 768), BF16),
+        V((3, 2, 32, 768), BF16),
+        V((3, 2, 2, 16, 768), F32),
+        V((3, 2, 2, 16, 768), BF16),
+        V((3, 3, 16, 768), BF16),
+        V((3, 16, 768), F32),
+        V((3, 16, 768), BF16),
+        V((3, 16, 768), BF16),
+        V((3, n_hi, 16, 768), BF16),
+        V((3, 2, 2, 16, 768), BF16),
         DMA((8,)),
         DMA((4,)),
         DMA((4,)),
-        DMA((16,)),
-        DMA((16,)),
-        DMA((6,)),
-        DMA((6,)),
+        DMA((24,)),
+        DMA((24,)),
+        DMA((7,)),
+        DMA((7,)),
         DMA((5, OWN)),
         DMA((5, OWN)),
         DMA((4,)),
         DMA((4,)),
         DMA((4,)),
-        DMA((3, 28 + n_hi)),
-        DMA((3, 28 + n_hi)),
+        DMA((2, 26)),
+        DMA((2, 26)),
+        DMA((3, 12)),
+        DMA((3, 12)),
+        DMA((5, n_hi)),
+        DMA((5, n_hi)),
     ]
     wide = jax.ShapeDtypeStruct((chunks, ROWS, lanes), BF16)
     made = pl.pallas_call(
@@ -972,7 +1120,7 @@
     )(
         feat.reshape(chunks, ROWS, lanes),
         cot.reshape(chunks, ROWS, lanes),
-        mask.reshape(chunks, ROWS),
+        mask,
         w1.T,
         w2.transpose(0, 1, 3, 2).reshape(9, 64, 256),
         w3,

time: 135 us -> 108 us (0.80)
  Pallas kernels: 132 us -> 107 us
  local copies, waits for them, and re-layouts: 1.4 us -> 0 us
    pallas_call x1, Pallas kernels: 127 us -> 102 us  [block(): pl.pallas_call(functools.partial(kernel, n_pix, n_ch), out_shape=(wide, w...]
    reshape x1 -> x0, local copies, waits for them, and re-layouts: 1.4 us -> none  [block(): mask.reshape(chunks, ROWS)]
where the time goes in v3:
time: 108 us; the launch traced here: 107 us
  Pallas kernels  107 us (99%)
    pallas_call x1, Pallas kernels, block(): pl.pallas_call(functools.partial(kernel, n_pix, n_ch), out_shape=(wide, w...  102 us
    pallas_call x1, Pallas kernels, block(): pl.pallas_call(finish, out_shape=tuple((jax.ShapeDtypeStruct(v.shape, v.d...  4.92 us

profile of v3, /device:TPU:0, one launch (start us, length us, event | category | flops | bytes accessed | tf_op | source)
XLA Modules:
  0.0 107.4 jit_solution(4433074254236253530)
XLA Ops:
  0.6 101.8 %bottleneck.1 = (bf16[28,112,256]{2,1,0:T(8,128)(2,1)}, bf16[28,112,256]{2,1,0:T(8,128)(2,1)}, f32[64,1024]{1,0:T(8,128)}, f32[9,64,256]{2,1,0:T(8,128)}, f32[64,1024]{1,0:T(8,128)}, /*index=5*/f32[8,256]{1,0:T(8,128)}) custom-call(bf16[28,112,256]{2,1,0:T(8,128)(2,1)} %bitcast.12, bf16[28,112,256]{2,1,0:T(8,128)(2,1)} %bitcast.13, s32[3136]{0:T(1024)} %mask.1, ...), custom_call_target="tpu_custom_call" | custom-call | tf_op jit(solution)/shard_map/bottleneck/pallas_call | solution.py:1103
  102.5 4.9 %outputs.1 = (bf16[28,112,256]{2,1,0:T(8,128)(2,1)}, bf16[28,112,256]{2,1,0:T(8,128)(2,1)}, f32[64,1024]{1,0:T(8,128)}, f32[9,64,256]{2,1,0:T(8,128)}, f32[64,10...) custom-call(bf16[28,112,256]{2,1,0:T(8,128)(2,1)} %get-tuple-element, ...), custom_call_target="tpu_custom_call" | custom-call | tf_op jit(solution)/shard_map/outputs/pallas_call | solution.py:1131

commit v4 on v3

--- a/solution.py
+++ b/solution.py
@@ -72,6 +72,13 @@
     sg_out,
     eg_out,
     st_out,
+    mask_v,
+    g1_v,
+    b1_v,
+    g2_v,
+    b2_v,
+    g3_v,
+    b3_v,
     F,
     C,
     V,
@@ -182,7 +189,20 @@
         local(cot.at[pl.ds(mine + part, OWN)], C.at[lo, pl.ds(OWN * s, OWN)], ld_sem.at[4 + s])
         for s, part in enumerate((part0, part1))
     ]
+    small_load = [local(mask, mask_v, ld_sem.at[7])]
+    pairs = ((g1_in, g1_v), (b1_in, b1_v), (g2_in, g2_v), (b2_in, b2_v), (g3_in, g3_v), (b3_in, b3_v))
+    small_load += [local(a, b, ld_sem.at[8 + i]) for i, (a, b) in enumerate(pairs)]
     w3_load = local(w3_in.at[:, pl.ds(pl.multiple_of(hi * 512, 512), 512)], W3.at[me_c], ld_sem.at[6])
+    barrier = pltpu.get_barrier_semaphore()
+
+    def greet(t, carry):
+        q = lax.rem(me_p * n_ch + me_c + t, n_all)
+        pl.semaphore_signal(barrier, inc=1, device_id=(q // n_ch, lax.rem(q, n_ch)), device_id_type=MESH)
+        return carry
+
+    lax.fori_loop(1, n_all, greet, 0)
+    for cp in small_load:
+        cp.start()
     w1_load.start()
     f_load[1].start()
     f_load[0].start()
@@ -191,24 +211,17 @@
     c_load[0].start()
     c_load[1].start()
 
-    barrier = pltpu.get_barrier_semaphore()
-
-    def greet(t, carry):
-        q = lax.rem(me_p * n_ch + me_c + t, n_all)
-        pl.semaphore_signal(barrier, inc=1, device_id=(q // n_ch, lax.rem(q, n_ch)), device_id_type=MESH)
-        return carry
-
-    lax.fori_loop(1, n_all, greet, 0)
-
     row_i = lax.broadcasted_iota(jnp.int32, (64, 256), 0)
     col_i = lax.broadcasted_iota(jnp.int32, (64, 256), 1)
     place = (row_i == col_i - 64 * me_c).astype(BF16)
-    narrow = jnp.concatenate([v[...].astype(F32).reshape(1, 64) for v in (g1_in, b1_in, g2_in, b2_in)] * 2, axis=0)
+    for cp in small_load:
+        cp.wait()
+    narrow = jnp.concatenate([v[...].astype(F32).reshape(1, 64) for v in (g1_v, b1_v, g2_v, b2_v)] * 2, axis=0)
     pk_rows = [mm(narrow.astype(BF16), place)[0:4]]
-    pk_rows += [v[...].astype(F32).reshape(1, 256) for v in (g3_in, b3_in)]
+    pk_rows += [v[...].astype(F32).reshape(1, 256) for v in (g3_v, b3_v)]
     pk[me_c] = jnp.concatenate(pk_rows + [jnp.zeros((2, 256), F32)], axis=0)
 
-    flat = mask[...].astype(F32).reshape(1, rows28.shape[0] * ROWS)
+    flat = mask_v[...].astype(F32).reshape(1, rows28.shape[0] * ROWS)
     for t in range(rows28.shape[0]):
         rows28[t : t + 1, :] = flat[:, t * ROWS : (t + 1) * ROWS]
     diag = lax.broadcasted_iota(jnp.int32, (ROWS, ROWS), 0) == lax.broadcasted_iota(jnp.int32, (ROWS, ROWS), 1)
@@ -241,32 +254,59 @@
         )
         for s, part in enumerate((part0, part1))
     ]
-    others = []
-    for t in range(1, n_ch):
-        q = lax.rem(me_c + t, n_ch)
-        others.append((t - 1, (me_p, q), q // 2))
+    far, near = (1 - hi) * 2 + lo, hi * 2 + 1 - lo
+
+    def columns(ref, h):
+        return ref.at[:, pl.ds(pl.multiple_of(h * 512, 512), 512)]
+
     w1x = [
-        remote(
-            w1_in.at[:, pl.ds(pl.multiple_of(h * 512, 512), 512)], W1T.at[me_c], w_send.at[t], w_recv.at[me_c], dev
-        )
-        for t, dev, h in others
+        remote(columns(w1_in, 1 - hi), W1T.at[me_c], w_send.at[0], w_recv.at[0], across),
+        remote(columns(w1_in, hi), W1T.at[me_c], w_send.at[1], w_recv.at[1], beside),
+        remote(W1T.at[far], W1T.at[far], w_send.at[2], w_recv.at[2], beside),
     ]
-    pkx = [remote(pk.at[me_c], pk.at[me_c], w_send.at[4 + t], w_recv.at[4 + me_c], dev) for t, dev, h in others]
+    pkx = [
+        remote(pk.at[me_c], pk.at[me_c], w_send.at[3], w_recv.at[3], across),
+        remote(pk.at[me_c], pk.at[me_c], w_send.at[4], w_recv.at[4], beside),
+        remote(pk.at[far], pk.at[far], w_send.at[5], w_recv.at[5], beside),
+    ]
+
+    def w2_piece(slot, q):
+        return W2T.at[
+            slot, :, pl.ds(pl.multiple_of(q // 2 * 16, 16), 16), pl.ds(pl.multiple_of(lax.rem(q, 2) * 128, 128), 128)
+        ]
+
+    def w3_piece(ref, q, first):
+        return ref.at[
+            pl.ds(pl.multiple_of(q // 2 * 16, 16), 16), pl.ds(pl.multiple_of(first + lax.rem(q, 2) * 256, 256), 256)
+        ]
+
+    w2x = [
+        remote(w2_piece(me_c, g_lo), w2_piece(me_c, g_lo), w_send.at[6], w_recv.at[6], across),
+        remote(W2T.at[me_c], W2T.at[me_c], w_send.at[7], w_recv.at[7], beside),
+        remote(W2T.at[far], W2T.at[far], w_send.at[8], w_recv.at[8], beside),
+    ]
     w3x = [
         remote(
-            w3_in.at[:, pl.ds(pl.multiple_of(h * 512, 512), 512)],
-            W3.at[me_c],
-            w_send.at[8 + t],
-            w_recv.at[8 + me_c],
-            dev,
-        )
-        for t, dev, h in others
+            w3_piece(w3_in, g_lo, (1 - hi) * 512),
+            w3_piece(W3.at[me_c], g_lo, 0),
+            w_send.at[9],
+            w_recv.at[9],
+            across,
+        ),
+        remote(columns(w3_in, hi), W3.at[me_c], w_send.at[10], w_recv.at[10], beside),
+        remote(W3.at[far], W3.at[far], w_send.at[11], w_recv.at[11], beside),
     ]
-    for cp in w1x:
-        cp.start()
+    shared = []
+    for t in range(1, n_lo):
+        to = (g_hi * n_lo + lax.rem(g_lo + t, n_lo), me_c)
+        for k, piece_of in enumerate((lambda q: w2_piece(far, q), lambda q: w3_piece(W3.at[far], q, 0))):
+            at = 12 + 8 * k + t
+            shared.append(remote(piece_of(g_lo), piece_of(g_lo), w_send.at[at], w_recv.at[at], to))
+    w1x[0].start()
+    w1x[1].start()
     fx[1].start()
     fx[0].start()
-    for cp in pkx:
+    for cp in (pkx[0], w3x[0], w2x[0], pkx[1]):
         cp.start()
 
     def arrived(dst, sem):
@@ -322,64 +362,52 @@
 
     ar_start(6, local_count, "pix")
 
-    far = (1 - hi) * 2 + lo
-
-    def w2_piece(slot, q):
-        return W2T.at[slot, :, pl.ds(pl.multiple_of(q // 2 * 16, 16), 16), pl.ds(pl.multiple_of(lax.rem(q, 2) * 128, 128), 128)]
-
-    w2x_across = remote(w2_piece(me_c, g_lo), w2_piece(me_c, g_lo), w_send.at[12], w_recv.at[12], across)
-    w2x_across.start()
-    w2x_beside = remote(W2T.at[me_c], W2T.at[me_c], w_send.at[13], w_recv.at[13], beside)
-    w2x_pass = remote(W2T.at[far], W2T.at[far], w_send.at[14], w_recv.at[14], beside)
-    w2x_share = []
-    for t in range(1, n_lo):
-        q = lax.rem(g_lo + t, n_lo)
-        w2x_share.append(
-            remote(
-                w2_piece(far, g_lo), w2_piece(far, g_lo), w_send.at[15 + t], w_recv.at[15 + t], (g_hi * n_lo + q, me_c)
-            )
-        )
-
-    for t, dev, h in others:
-        q = dev[1]
-        arrived(W1T.at[q], w_recv.at[q])
-
     w1_load.wait()
-
     f_load[1].wait()
     fx[1].wait_recv()
-    w1_all = W1T[...].reshape(256, 512)
-
-    def first(t):
-        wide = jnp.concatenate([F[0, t], F[1, t]], axis=1)
-        return mm_nt(wide, w1_all)
+    arrived(W1T.at[near], w_recv.at[1])
+
+    def wide_rows(t):
+        return jnp.concatenate([F[0, t], F[1, t]], axis=1)
 
     def xcopy(kind, src, dst, t):
         return remote(src.at[t], dst.at[t], x_send.at[kind, t], x_recv.at[kind, t], across)
 
-    def send_first(t, carry):
-        h1s[t] = first(t + OWN).astype(BF16)
-        xcopy(0, h1s, h1r, t).start()
-        return carry
-
-    lax.fori_loop(0, OWN, send_first, 0)
+    def send_first(h, kind):
+        w = W1T[pl.ds(2 * h, 2)].reshape(128, 512)
+
+        def one(t, carry):
+            h1s[h, t] = mm_nt(wide_rows(t + OWN), w).astype(BF16)
+            xcopy(kind, h1s.at[h], h1r.at[h], t).start()
+            return carry
+
+        lax.fori_loop(0, OWN, one, 0)
+
+    send_first(hi, 0)
+    arrived(W1T.at[far], w_recv.at[0])
+    w1x[2].start()
+    arrived(W1T.at[(1 - hi) * 2 + 1 - lo], w_recv.at[2])
+    send_first(1 - hi, 5)
     f_load[0].wait()
     fx[0].wait_recv()
 
+    w1_all = W1T[...].reshape(256, 512)
+
     def keep_first(t, carry):
-        H1[t] = first(t)
+        H1[t] = mm_nt(wide_rows(t), w1_all)
         return carry
 
     lax.fori_loop(0, OWN, keep_first, 0)
 
-    arrived(w2_piece(far, g_lo), w_recv.at[12])
-    for cp in w2x_share:
+    arrived(w2_piece(far, g_lo), w_recv.at[6])
+    arrived(w3_piece(W3.at[far], g_lo, 0), w_recv.at[9])
+    for cp in shared:
         cp.start()
-    w2x_beside.start()
-    cx[0].start()
-    cx[1].start()
-    for t, dev, h in others:
-        arrived(pk.at[dev[1]], w_recv.at[4 + dev[1]])
+    arrived(pk.at[far], w_recv.at[3])
+    for cp in (pkx[2], w2x[1], w3x[1], cx[0], cx[1]):
+        cp.start()
+    arrived(pk.at[near], w_recv.at[4])
+    arrived(pk.at[(1 - hi) * 2 + 1 - lo], w_recv.at[5])
     gains = pk[0] + pk[1] + pk[2] + pk[3]
     g1, b1, g2, b2 = (gains[k : k + 1] for k in range(4))
     pair0, pair1 = pk[2 * hi], pk[2 * hi + 1]
@@ -390,8 +418,9 @@
 
     def sum_first(t, carry):
         s, q = carry
-        xcopy(0, h1s, h1r, t).wait_recv()
-        h = H1[t] + h1r[t].astype(F32)
+        for kind in (0, 5):
+            xcopy(kind, h1s.at[0], h1r.at[0], t).wait_recv()
+        h = H1[t] + jnp.concatenate([h1r[0, t], h1r[1, t]], axis=1).astype(F32)
         H1[t] = h
         h1b[t] = h.astype(BF16)
         vh = spread(V[t], 256) * h
@@ -399,9 +428,13 @@
 
     s, q = lax.fori_loop(0, OWN, sum_first, (zero, zero))
     ar_start(0, pack2(fold1(s), fold1(q)), "all")
+    w3_load.wait()
     for t in range(1, n_lo):
-        arrived(w2_piece(far, lax.rem(g_lo - t + n_lo, n_lo)), w_recv.at[15 + t])
-    w2x_pass.start()
+        q = lax.rem(g_lo - t + n_lo, n_lo)
+        arrived(w2_piece(far, q), w_recv.at[12 + t])
+        arrived(w3_piece(W3.at[far], q, 0), w_recv.at[20 + t])
+    w2x[2].start()
+    w3x[2].start()
     inv_n = 1.0 / spread(ar_finish(6, "pix", 8)[0:1], 512)
     inv_n2 = inv_n[:, 0:256]
     s, q = unpack2(ar_finish(0, "all", 4))
@@ -441,10 +474,8 @@
             at = EDGE + i * 256 + c - 1
             PC[PAD + i * BLOCK : PAD + (i + 1) * BLOCK, 256 * c : 256 * (c + 1)] = P0[at : at + BLOCK, :].astype(BF16)
 
-    arrived(W2T.at[hi * 2 + 1 - lo], w_recv.at[13])
-    arrived(W2T.at[(1 - hi) * 2 + 1 - lo], w_recv.at[14])
-    for cp in w3x:
-        cp.start()
+    arrived(W2T.at[near], w_recv.at[7])
+    arrived(W2T.at[(1 - hi) * 2 + 1 - lo], w_recv.at[8])
     h1x = [remote(h1b, h1o, x_send.at[4, 0], x_recv.at[4, 0], across)]
 
     def conv(i, carry):
@@ -483,9 +514,8 @@
     a2_gain = g2 * scale2
     a2_shift = b2 - avg2 * a2_gain
 
-    w3_load.wait()
-    for t, dev, h in others:
-        arrived(W3.at[dev[1]], w_recv.at[8 + dev[1]])
+    arrived(W3.at[near], w_recv.at[10])
+    arrived(W3.at[(1 - hi) * 2 + 1 - lo], w_recv.at[11])
 
     def act_second(t, h, carry):
         s, q = carry
@@ -509,10 +539,10 @@
 
     wide_zero = jnp.zeros((8, 512), F32)
     carry = lax.fori_loop(0, OWN, own_second, (wide_zero, wide_zero))
+    for cp in h1x:
+        cp.start()
     s, q = lax.fori_loop(0, OWN, other_second, carry)
     ar_start(2, pack3(fold1(s), fold1(q)), "half")
-    for cp in h1x:
-        cp.start()
     for cp in c_load:
         cp.wait()
     for cp in cx:
@@ -881,6 +911,7 @@
 
     for i in range(IMAGES):
         QT[:, i * BLOCK : (i + 1) * BLOCK] = P0[EDGE + i * BLOCK : EDGE + (i + 1) * BLOCK, :].T.astype(BF16)
+    wide_give(0)
     s_make(0)
     s_make(1)
     s_pair_add(0)
@@ -928,8 +959,6 @@
 
     own_reduce = mm_tn(half_of(G1, 0), features_of(0))
     acc_w[1] = own_reduce.reshape(2, 2, 64, 512)
-    s_next_add(1)
-    wide_give(0)
     for cp in h1x:
         cp.wait_recv()
 
@@ -939,6 +968,7 @@
         return carry
 
     lax.fori_loop(0, OWN, other_back_first, 0)
+    s_next_add(1)
     acc_w[1] += mm_tn(half_of(G1, 1), features_of(1)).reshape(2, 2, 64, 512)
     pair_start(1)
     ig_here[1].start()
@@ -991,9 +1021,9 @@
         cp.wait()
     for cp in res_there:
         cp.wait_recv()
-    for cp in fx + cx + w1x + pkx + w3x + h1x + w2x_share + [w2x_across, w2x_beside, w2x_pass]:
+    for cp in fx + cx + w1x + pkx + w2x + w3x + shared + h1x:
         cp.wait_send()
-    for kind, src, dst in ((0, h1s, h1r), (1, h2s, h2r), (2, e2s, e2r), (3, e1s, e1r)):
+    for kind, src, dst in ((0, h1s.at[hi], h1r.at[hi]), (5, h1s.at[1 - hi], h1r.at[1 - hi]), (1, h2s, h2r), (2, e2s, e2r), (3, e1s, e1r)):
         for t in range(OWN):
             xcopy(kind, src, dst, t).wait_send()
     for k, kind, rows in (
@@ -1019,6 +1049,9 @@
     V = pltpu.VMEM
     DMA = pltpu.SemaphoreType.DMA
     scratch = [
+        V((rows,), jnp.int32),
+        *[V((64,), BF16)] * 4,
+        *[V((256,), BF16)] * 2,
         V((2, BOTH, ROWS, 256), BF16),
         V((2, BOTH, ROWS, 256), BF16),
         V((BOTH, ROWS, 128), F32),
@@ -1028,8 +1061,8 @@
         V((4, 8, 256), F32),
         V((7, 8, 128), F32),
         V((7, n_pix * n_ch, 8, 128), F32),
-        V((OWN, ROWS, 256), BF16),
-        V((OWN, ROWS, 256), BF16),
+        V((2, OWN, ROWS, 128), BF16),
+        V((2, OWN, ROWS, 128), BF16),
         V((OWN, ROWS, 256), F32),
         V((OWN, ROWS, 256), BF16),
         V((OWN, ROWS, 256), BF16),
@@ -1080,15 +1113,15 @@
         V((3, 16, 768), BF16),
         V((3, n_hi, 16, 768), BF16),
         V((3, 2, 2, 16, 768), BF16),
-        DMA((8,)),
+        DMA((14,)),
         DMA((4,)),
         DMA((4,)),
-        DMA((24,)),
-        DMA((24,)),
+        DMA((28,)),
+        DMA((28,)),
         DMA((7,)),
         DMA((7,)),
-        DMA((5, OWN)),
-        DMA((5, OWN)),
+        DMA((6, OWN)),
+        DMA((6, OWN)),
         DMA((4,)),
         DMA((4,)),
         DMA((4,)),
@@ -1099,18 +1132,18 @@
         DMA((5, n_hi)),
         DMA((5, n_hi)),
     ]
-    wide = jax.ShapeDtypeStruct((chunks, ROWS, lanes), BF16)
+    wide = V((chunks, ROWS, lanes), BF16)
     made = pl.pallas_call(
         functools.partial(kernel, n_pix, n_ch),
         out_shape=(
             wide,
             wide,
-            jax.ShapeDtypeStruct((64, 1024), F32),
-            jax.ShapeDtypeStruct((9, 64, 256), F32),
-            jax.ShapeDtypeStruct((64, 1024), F32),
-            jax.ShapeDtypeStruct((8, 256), F32),
+            V((64, 1024), F32),
+            V((9, 64, 256), F32),
+            V((64, 1024), F32),
+            V((8, 256), F32),
         ),
-        in_specs=[any_space, any_space, vmem, any_space, any_space, any_space] + [vmem] * 6,
+        in_specs=[any_space] * 12,
         out_specs=(any_space, any_space, vmem, vmem, vmem, vmem),
         scratch_shapes=scratch,
         compiler_params=pltpu.CompilerParams(
@@ -1131,11 +1164,12 @@
     return pl.pallas_call(
         finish,
         out_shape=tuple(jax.ShapeDtypeStruct(v.shape, v.dtype) for v in made[:5]) + (narrow,) * 4 + (broad,) * 2,
-        in_specs=[vmem] * 6,
+        in_specs=[any_space] * 5 + [vmem],
         out_specs=(any_space,) * 5 + (vmem,) * 6,
         scratch_shapes=[DMA((5,))],
+        compiler_params=pltpu.CompilerParams(vmem_limit_bytes=2**20),
         name="outputs",
-    )(*made)
+    )(*[pltpu.with_memory_space_constraint(v, pltpu.VMEM) for v in made])
 
 
 def finish(*refs):

time: 108 us -> 102 us (0.944)
  Pallas kernels: 107 us -> 101 us
    pallas_call x1, Pallas kernels: 102 us -> 98.5 us  [block(): pl.pallas_call(functools.partial(kernel, n_pix, n_ch), out_shape=(wide, w...]
    pallas_call x1, Pallas kernels: 4.92 us -> 2.67 us  [block(): pl.pallas_call(finish, out_shape=tuple((jax.ShapeDtypeStruct(v.shape, v.d...]
where the time goes in v4:
time: 102 us
  Pallas kernels  101 us (99%)
    pallas_call x1, Pallas kernels, block(): pl.pallas_call(functools.partial(kernel, n_pix, n_ch), out_shape=(wide, w...  98.5 us
    pallas_call x1, Pallas kernels, block(): pl.pallas_call(finish, out_shape=tuple((jax.ShapeDtypeStruct(v.shape, v.d...  2.67 us

profile of v4, /device:TPU:0, one launch (start us, length us, event | category | flops | bytes accessed | tf_op | source)
XLA Modules:
  0.0 101.9 jit_solution(15710880197047024607)
XLA Ops:
  0.6 98.5 %bottleneck.1 = (bf16[28,112,256]{2,1,0:T(8,128)(2,1)S(1)}, bf16[28,112,256]{2,1,0:T(8,128)(2,1)S(1)}, f32[64,1024]{1,0:T(8,128)S(1)}, f32[9,64,256]{2,1,0:T(8,1...) custom-call(bf16[28,112,256]{2,1,0:T(8,128)(2,1)} %bitcast.12, bf16[28,112,256]{2,1,0:T(8,128)(2,1)} %bitcast.13, ...), custom_call_target="tpu_custom_call" | custom-call | tf_op jit(solution)/shard_map/bottleneck/pallas_call | solution.py:1136
  99.2 2.7 %outputs.1 = (bf16[28,112,256]{2,1,0:T(8,128)(2,1)}, bf16[28,112,256]{2,1,0:T(8,128)(2,1)}, f32[64,1024]{1,0:T(8,128)}, f32[9,64,256]{2,1,0:T(8,128)}, f32[64,10...) custom-call(bf16[28,112,256]{2,1,0:T(8,128)(2,1)S(1)} %get-tuple-ele, ...), custom_call_target="tpu_custom_call" | custom-call | tf_op jit(solution)/shard_map/outputs/pallas_call | solution.py:1164

commit v5 on v4

--- a/solution.py
+++ b/solution.py
@@ -140,6 +140,16 @@
     xr,
     sh,
     sfin,
+    t1,
+    xb,
+    xc,
+    yb,
+    yc,
+    t2,
+    zb,
+    zc,
+    th,
+    tfin,
     ld_sem,
     fx_send,
     fx_recv,
@@ -211,35 +221,6 @@
     c_load[0].start()
     c_load[1].start()
 
-    row_i = lax.broadcasted_iota(jnp.int32, (64, 256), 0)
-    col_i = lax.broadcasted_iota(jnp.int32, (64, 256), 1)
-    place = (row_i == col_i - 64 * me_c).astype(BF16)
-    for cp in small_load:
-        cp.wait()
-    narrow = jnp.concatenate([v[...].astype(F32).reshape(1, 64) for v in (g1_v, b1_v, g2_v, b2_v)] * 2, axis=0)
-    pk_rows = [mm(narrow.astype(BF16), place)[0:4]]
-    pk_rows += [v[...].astype(F32).reshape(1, 256) for v in (g3_v, b3_v)]
-    pk[me_c] = jnp.concatenate(pk_rows + [jnp.zeros((2, 256), F32)], axis=0)
-
-    flat = mask_v[...].astype(F32).reshape(1, rows28.shape[0] * ROWS)
-    for t in range(rows28.shape[0]):
-        rows28[t : t + 1, :] = flat[:, t * ROWS : (t + 1) * ROWS]
-    diag = lax.broadcasted_iota(jnp.int32, (ROWS, ROWS), 0) == lax.broadcasted_iota(jnp.int32, (ROWS, ROWS), 1)
-    ones = jnp.ones((ROWS, 128), BF16)
-
-    def put_mask(t, carry):
-        at = mine + jnp.where(t < OWN, part0 + t, part1 + t - OWN)
-        row = rows28[pl.ds(at, 1), :]
-        V[t] = mm(jnp.where(diag, row, 0.0).astype(BF16), ones)
-        return carry
-
-    lax.fori_loop(0, BOTH, put_mask, 0)
-    lanes = jnp.broadcast_to(jnp.sum(rows28[...], axis=0, keepdims=True), (8, ROWS))
-    local_count = mm(lanes.astype(BF16), ones)
-    P0[...] = jnp.zeros_like(P0)
-    PC[0:PAD, :] = jnp.zeros((PAD, 768), BF16)
-    PC[PAD + FLAT :, :] = jnp.zeros((PAD, 768), BF16)
-    w2_load.wait()
     pl.semaphore_wait(barrier, n_all - 1)
 
     fx = [
@@ -270,9 +251,9 @@
         remote(pk.at[far], pk.at[far], w_send.at[5], w_recv.at[5], beside),
     ]
 
-    def w2_piece(slot, q):
-        return W2T.at[
-            slot, :, pl.ds(pl.multiple_of(q // 2 * 16, 16), 16), pl.ds(pl.multiple_of(lax.rem(q, 2) * 128, 128), 128)
+    def w2_piece(ref, q):
+        return ref.at[
+            :, pl.ds(pl.multiple_of(q // 2 * 16, 16), 16), pl.ds(pl.multiple_of(lax.rem(q, 2) * 128, 128), 128)
         ]
 
     def w3_piece(ref, q, first):
@@ -281,7 +262,7 @@
         ]
 
     w2x = [
-        remote(w2_piece(me_c, g_lo), w2_piece(me_c, g_lo), w_send.at[6], w_recv.at[6], across),
+        remote(w2_piece(w2_in, g_lo), w2_piece(W2T.at[me_c], g_lo), w_send.at[6], w_recv.at[6], across),
         remote(W2T.at[me_c], W2T.at[me_c], w_send.at[7], w_recv.at[7], beside),
         remote(W2T.at[far], W2T.at[far], w_send.at[8], w_recv.at[8], beside),
     ]
@@ -299,15 +280,28 @@
     shared = []
     for t in range(1, n_lo):
         to = (g_hi * n_lo + lax.rem(g_lo + t, n_lo), me_c)
-        for k, piece_of in enumerate((lambda q: w2_piece(far, q), lambda q: w3_piece(W3.at[far], q, 0))):
+        for k, piece_of in enumerate((lambda q: w2_piece(W2T.at[far], q), lambda q: w3_piece(W3.at[far], q, 0))):
             at = 12 + 8 * k + t
             shared.append(remote(piece_of(g_lo), piece_of(g_lo), w_send.at[at], w_recv.at[at], to))
     w1x[0].start()
     w1x[1].start()
     fx[1].start()
     fx[0].start()
-    for cp in (pkx[0], w3x[0], w2x[0], pkx[1]):
-        cp.start()
+    w3x[0].start()
+    w2x[0].start()
+
+    row_i = lax.broadcasted_iota(jnp.int32, (64, 256), 0)
+    col_i = lax.broadcasted_iota(jnp.int32, (64, 256), 1)
+    place = (row_i == col_i - 64 * me_c).astype(BF16)
+    for cp in small_load:
+        cp.wait()
+    narrow = jnp.concatenate([v[...].astype(F32).reshape(1, 64) for v in (g1_v, b1_v, g2_v, b2_v)] * 2, axis=0)
+    pk_rows = [mm(narrow.astype(BF16), place)[0:4]]
+    pk_rows += [v[...].astype(F32).reshape(1, 256) for v in (g3_v, b3_v)]
+    pk[me_c] = jnp.concatenate(pk_rows + [jnp.zeros((2, 256), F32)], axis=0)
+
+    pkx[0].start()
+    pkx[1].start()
 
     def arrived(dst, sem):
         local(dst, dst, sem).wait()
@@ -360,9 +354,9 @@
             jnp.concatenate([v[i : i + 1] for i in range(4, 8)], axis=1),
         )
 
-    ar_start(6, local_count, "pix")
 
     w1_load.wait()
+    w2_load.wait()
     f_load[1].wait()
     fx[1].wait_recv()
     arrived(W1T.at[near], w_recv.at[1])
@@ -386,6 +380,10 @@
     send_first(hi, 0)
     arrived(W1T.at[far], w_recv.at[0])
     w1x[2].start()
+    arrived(w3_piece(W3.at[far], g_lo, 0), w_recv.at[9])
+    arrived(w2_piece(W2T.at[far], g_lo), w_recv.at[6])
+    for cp in shared:
+        cp.start()
     arrived(W1T.at[(1 - hi) * 2 + 1 - lo], w_recv.at[2])
     send_first(1 - hi, 5)
     f_load[0].wait()
@@ -399,10 +397,26 @@
 
     lax.fori_loop(0, OWN, keep_first, 0)
 
-    arrived(w2_piece(far, g_lo), w_recv.at[6])
-    arrived(w3_piece(W3.at[far], g_lo, 0), w_recv.at[9])
-    for cp in shared:
-        cp.start()
+    flat = mask_v[...].astype(F32).reshape(1, rows28.shape[0] * ROWS)
+    for t in range(rows28.shape[0]):
+        rows28[t : t + 1, :] = flat[:, t * ROWS : (t + 1) * ROWS]
+    diag = lax.broadcasted_iota(jnp.int32, (ROWS, ROWS), 0) == lax.broadcasted_iota(jnp.int32, (ROWS, ROWS), 1)
+    ones = jnp.ones((ROWS, 128), BF16)
+
+    def put_mask(t, carry):
+        at = mine + jnp.where(t < OWN, part0 + t, part1 + t - OWN)
+        row = rows28[pl.ds(at, 1), :]
+        V[t] = mm(jnp.where(diag, row, 0.0).astype(BF16), ones)
+        return carry
+
+    lax.fori_loop(0, BOTH, put_mask, 0)
+    lanes = jnp.broadcast_to(jnp.sum(rows28[...], axis=0, keepdims=True), (8, ROWS))
+    local_count = mm(lanes.astype(BF16), ones)
+    P0[...] = jnp.zeros_like(P0)
+    PC[0:PAD, :] = jnp.zeros((PAD, 768), BF16)
+    PC[PAD + FLAT :, :] = jnp.zeros((PAD, 768), BF16)
+    ar_start(6, local_count, "pix")
+
     arrived(pk.at[far], w_recv.at[3])
     for cp in (pkx[2], w2x[1], w3x[1], cx[0], cx[1]):
         cp.start()
@@ -431,7 +445,7 @@
     w3_load.wait()
     for t in range(1, n_lo):
         q = lax.rem(g_lo - t + n_lo, n_lo)
-        arrived(w2_piece(far, q), w_recv.at[12 + t])
+        arrived(w2_piece(W2T.at[far], q), w_recv.at[12 + t])
         arrived(w3_piece(W3.at[far], q, 0), w_recv.at[20 + t])
     w2x[2].start()
     w3x[2].start()
@@ -498,14 +512,16 @@
         for t in range(first, last):
             xcopy(kind, src, dst, t).start()
 
-    early = 2
-    lax.fori_loop(0, 2, conv, 0)
-    from_padded(H2, (0, 1))
-    carry = lax.fori_loop(0, 3, sum_second, (zero, zero))
-    start_all(1, h2s, h2r, 0, early)
-    lax.fori_loop(2, IMAGES, conv, 0)
-    from_padded(H2, (2, 3))
-    s, q = lax.fori_loop(3, OWN, sum_second, carry)
+    early = 3
+    whole = [(i + 1) * SIDE * SIDE // ROWS for i in range(IMAGES)]
+    carry, done = (zero, zero), 0
+    for i, now in enumerate(whole):
+        conv(i, 0)
+        from_padded(H2, (i,))
+        carry = lax.fori_loop(done, now, sum_second, carry)
+        start_all(1, h2s, h2r, min(done, early), min(now, early))
+        done = now
+    s, q = carry
     ar_start(1, pack2(fold1(s), fold1(q)), "all")
     start_all(1, h2s, h2r, early, OWN)
     s, q = unpack2(ar_finish(1, "all", 4))
@@ -712,6 +728,64 @@
             else:
                 cp.start()
 
+    e_spot = wfin.at[0, hi, own_sub]
+    e_cross = remote(wf.at[0], e_spot, g_send.at[0, 10], g_recv.at[0, 10], across)
+
+    def e_share(h, at):
+        spot = wfin.at[0, h, own_sub]
+        return [
+            remote(
+                spot, spot, g_send.at[0, at + t], g_recv.at[0, at + t], (g_hi * n_lo + lax.rem(g_lo + t, n_lo), me_c)
+            )
+            for t in range(1, n_lo)
+        ]
+
+    def e_first():
+        wf[0] = spread_add(0).astype(BF16)
+
+        @pl.when(jnp.logical_not(keeps))
+        def _():
+            e_cross.start()
+
+        @pl.when(keeps)
+        def _():
+            wfin[0, hi, own_sub] = wf[0]
+            for cp in e_share(hi, 10):
+                cp.start()
+
+    def e_second():
+        @pl.when(keeps)
+        def _():
+            arrived(wfin.at[0, 1 - hi, own_sub], g_recv.at[0, 10])
+            for cp in e_share(1 - hi, 17):
+                cp.start()
+
+    def e_take(out):
+        for sub in range(n_sub):
+            q = sub * 2 + hi
+            t = lax.rem(g_lo - q + n_lo, n_lo)
+
+            @pl.when(q != g_lo)
+            def _():
+                arrived(wfin.at[0, hi, sub], g_recv.at[0, 10 + t])
+                arrived(wfin.at[0, 1 - hi, sub], g_recv.at[0, 17 + t])
+
+        for h in range(2):
+            out[:, 512 * h : 512 * (h + 1)] = wfin[0, h].astype(F32).reshape(64, 512)
+
+    def e_close():
+        for cp in pair_copies(0) + spread_copies(0):
+            cp.wait_send()
+
+        @pl.when(jnp.logical_not(keeps))
+        def _():
+            e_cross.wait_send()
+
+        @pl.when(keeps)
+        def _():
+            for cp in e_share(hi, 10) + e_share(1 - hi, 17):
+                cp.wait_send()
+
     def wide_take(k, out):
         for sub in range(n_sub):
             q = sub * 2 + hi
@@ -757,6 +831,7 @@
         return carry
 
     lax.fori_loop(0, OWN, back_second, 0)
+    e_first()
     to_padded()
     for i in range(IMAGES):
         for c in range(3):
@@ -781,13 +856,14 @@
         e1s[t] = e.astype(BF16)
         return s + fold8(e), q + fold8(e * (H1[t] - avg1))
 
-    lax.fori_loop(0, 2, conv_back, 0)
-    from_padded(comp, (0, 1))
-    carry = lax.fori_loop(0, 3, sum_back_first, (zero, zero))
-    start_all(3, e1s, e1r, 0, early)
-    lax.fori_loop(2, IMAGES, conv_back, 0)
-    from_padded(comp, (2, 3))
-    s, q = lax.fori_loop(3, OWN, sum_back_first, carry)
+    carry, done = (zero, zero), 0
+    for i, now in enumerate(whole):
+        conv_back(i, 0)
+        from_padded(comp, (i,))
+        carry = lax.fori_loop(done, now, sum_back_first, carry)
+        start_all(3, e1s, e1r, min(done, early), min(now, early))
+        done = now
+    s, q = carry
     ar_start(5, pack2(fold1(s), fold1(q * scale1)), "all")
     start_all(3, e1s, e1r, early, OWN)
 
@@ -799,42 +875,6 @@
         return [
             remote(sp.at[r, h], sc.at[r, h], s_send.at[r, h], s_recv.at[r, h], beside) for h in range(2)
         ]
-
-    def s_next(r):
-        return remote(ys.at[r], yr.at[r], s_send.at[r, 2], s_recv.at[r, 2], next_group)
-
-    def s_quad(r):
-        copies = []
-        for t in range(1, 4):
-            q = lax.rem(quad + t, 4)
-            copies.append(
-                remote(
-                    zs.at[r, lax.rem(q, 2), q // 2],
-                    zr.at[r, t - 1],
-                    s_send.at[r, 2 + t],
-                    s_recv.at[r, 2 + t],
-                    (g_hi * n_lo + q * 2 + bit, me_c),
-                )
-            )
-        return copies
-
-    def s_cross(r):
-        return remote(xs.at[r], xr.at[r], s_send.at[r, 6], s_recv.at[r, 6], across)
-
-    def s_give(r):
-        copies = []
-        for t in range(1, 4):
-            q = lax.rem(quad + t, 4)
-            spot = sfin.at[r, bit, quad // 2]
-            copies.append(
-                remote(
-                    spot, spot, s_send.at[r, 6 + t], s_recv.at[r, 7 + quad // 2], (g_hi * n_lo + q * 2 + bit, me_c)
-                )
-            )
-        return copies
-
-    def s_back(r):
-        return remote(sfin.at[r, bit], sfin.at[r, bit], s_send.at[r, 10], s_recv.at[r, 10], next_group)
 
     def s_make(r):
         taps = mm(QT[...], PC[PAD * r : PAD * r + FLAT, :])
@@ -848,76 +888,187 @@
         for h, cp in enumerate(s_pair(r)):
             cp.wait_recv()
             s1[r, h] = (acc_s[r, h, lo] + sc[r, h].astype(F32)).reshape(2, 32, 768)
-            ys[r, h] = s1[r, h, 1 - bit].astype(BF16)
-        s_next(r).start()
-
-    def s_next_add(r):
-        s_next(r).wait_recv()
+
+    def group_at(q):
+        return (g_hi * n_lo + q * 2 + bit, me_c)
+
+    y_next = remote(ys, yr, s_send.at[0, 2], s_recv.at[0, 2], next_group)
+    y_cross = remote(xs, xr, s_send.at[0, 6], s_recv.at[0, 6], across)
+
+    def y_quad():
+        copies = []
+        for t in range(1, 4):
+            q = lax.rem(quad + t, 4)
+            copies.append(
+                remote(zs.at[lax.rem(q, 2), q // 2], zr.at[t - 1], s_send.at[0, 2 + t], s_recv.at[0, 2 + t], group_at(q))
+            )
+        return copies
+
+    def y_give():
+        copies = []
+        spot = sfin.at[bit, quad // 2]
+        for t in range(1, 4):
+            to = group_at(lax.rem(quad + t, 4))
+            copies.append(remote(spot, spot, s_send.at[0, 6 + t], s_recv.at[0, 7 + quad // 2], to))
+        return copies
+
+    y_back = remote(sfin.at[bit], sfin.at[bit], s_send.at[0, 10], s_recv.at[0, 10], next_group)
+
+    def y_start():
         for h in range(2):
-            s2[r, h] = (s1[r, h, bit] + yr[r, h].astype(F32)).reshape(2, 16, 768)
-            zs[r, h] = s2[r, h].astype(BF16)
-        for cp in s_quad(r):
+            zs[h] = s1[0, h].astype(BF16)
+        for cp in y_quad():
             cp.start()
 
-    def s_quad_add(r):
-        for cp in s_quad(r):
+    def y_quad_add():
+        for cp in y_quad():
             cp.wait_recv()
-        total = s2[r, lax.rem(quad, 2), quad // 2]
+        total = s1[0, lax.rem(quad, 2), quad // 2]
         for t in range(3):
-            total = total + zr[r, t].astype(F32)
-        s3[r] = total
-        xs[r] = total.astype(BF16)
+            total = total + zr[t].astype(F32)
+        s2[...] = total.reshape(2, 16, 768)
+        ys[...] = s2[1 - bit].astype(BF16)
+        y_next.start()
+
+    def y_next_add():
+        y_next.wait_recv()
+        total = s2[bit] + yr[...].astype(F32)
+        s3[...] = total
+        xs[...] = total.astype(BF16)
 
         @pl.when(jnp.logical_not(s_owner))
         def _():
-            s_cross(r).start()
-
-    def s_cross_add(r):
+            y_cross.start()
+
+    def y_cross_add():
         @pl.when(s_owner)
         def _():
-            s_cross(r).wait_recv()
-            total = s3[r] + xr[r].astype(F32)
-            sfin[r, bit, quad // 2] = over_groups(total, sh.at[r], (h_send.at[2 + r], h_recv.at[2 + r])).astype(BF16)
-            for cp in s_give(r):
+            y_cross.wait_recv()
+            total = s3[...] + xr[...].astype(F32)
+            sfin[bit, quad // 2] = over_groups(total, sh, (h_send.at[2], h_recv.at[2])).astype(BF16)
+            for cp in y_give():
                 cp.start()
 
-    def s_give_back(r):
+    def y_give_back():
         for part in range(2):
 
             @pl.when(quad != 2 * part + hi)
             def _():
-                arrived(sfin.at[r, bit, part], s_recv.at[r, 7 + part])
-
-        s_back(r).start()
-
-    def s_take(r):
-        arrived(sfin.at[r, 1 - bit], s_recv.at[r, 10])
-        rows = sfin[r].astype(F32).reshape(64, 768)
-        for c in range(3):
-            sg_out[3 * r + c] = rows[:, 256 * c : 256 * (c + 1)]
-
-    def s_close(r):
-        for cp in s_pair(r) + [s_next(r)] + s_quad(r) + [s_back(r)]:
+                arrived(sfin.at[bit, part], s_recv.at[0, 7 + part])
+
+        y_back.start()
+
+    def y_take():
+        arrived(sfin.at[1 - bit], s_recv.at[0, 10])
+        for b in range(2):
+            for h in range(2):
+                rows = sfin[b, h].astype(F32)
+                for c in range(3):
+                    sg_out[c, 32 * h + 16 * b : 32 * h + 16 * (b + 1), :] = rows[:, 256 * c : 256 * (c + 1)]
+
+    def y_close():
+        for cp in s_pair(0) + [y_next] + y_quad() + [y_back]:
             cp.wait_send()
 
         @pl.when(s_owner)
         def _():
-            for cp in s_give(r):
+            for cp in y_give():
                 cp.wait_send()
 
         @pl.when(jnp.logical_not(s_owner))
         def _():
-            s_cross(r).wait_send()
+            y_cross.wait_send()
+
+    def x_cross(r):
+        return remote(yb.at[r], yc.at[r], s_send.at[r, 6], s_recv.at[r, 6], across)
+
+    def x_next(r):
+        return remote(xb.at[r], xc.at[r], s_send.at[r, 2], s_recv.at[r, 2], next_group)
+
+    def x_quad(r):
+        copies = []
+        for t in range(1, 4):
+            q = lax.rem(quad + t, 4)
+            copies.append(
+                remote(
+                    zb.at[r, q // 2, lax.rem(q, 2)], zc.at[r, t - 1], s_send.at[r, 2 + t], s_recv.at[r, 2 + t], group_at(q)
+                )
+            )
+        return copies
+
+    def x_give(r):
+        copies = []
+        spot = tfin.at[r, bit, quad // 2, lax.rem(quad, 2)]
+        for t in range(1, 4):
+            to = group_at(lax.rem(quad + t, 4))
+            copies.append(remote(spot, spot, s_send.at[r, 6 + t], s_recv.at[r, 6 + t], to))
+        return copies
+
+    def x_back(r):
+        return remote(tfin.at[r, bit], tfin.at[r, bit], s_send.at[r, 10], s_recv.at[r, 10], next_group)
+
+    def x_start(r):
+        for h in range(2):
+            xb[r, h] = s1[r, h, 1 - bit].astype(BF16)
+        x_next(r).start()
+
+    def x_next_add(r):
+        x_next(r).wait_recv()
+        for h in range(2):
+            t1[r, h] = s1[r, h, bit] + xc[r, h].astype(F32)
+        yb[r] = t1[r, 1 - hi].astype(BF16)
+        x_cross(r).start()
+
+    def x_cross_add(r):
+        x_cross(r).wait_recv()
+        total = t1[r, hi] + yc[r].astype(F32)
+        for h in range(2):
+            for w in range(2):
+                part = total[16 * h : 16 * (h + 1), 384 * w : 384 * (w + 1)]
+                t2[r, h, w] = part
+                zb[r, h, w] = part.astype(BF16)
+        for cp in x_quad(r):
+            cp.start()
+
+    def x_quad_add(r):
+        for cp in x_quad(r):
+            cp.wait_recv()
+        total = t2[r, quad // 2, lax.rem(quad, 2)]
+        for t in range(3):
+            total = total + zc[r, t].astype(F32)
+        total = over_groups(total, th.at[r], (h_send.at[2 + r], h_recv.at[2 + r]))
+        tfin[r, bit, quad // 2, lax.rem(quad, 2)] = total.astype(BF16)
+        for cp in x_give(r):
+            cp.start()
+
+    def x_give_back(r):
+        for cp in x_give(r):
+            cp.wait_recv()
+        x_back(r).start()
+
+    def x_take(r):
+        arrived(tfin.at[r, 1 - bit], s_recv.at[r, 10])
+        halves = [tfin[r, :, :, w].astype(F32).reshape(64, 384) for w in range(2)]
+        sg_out[3 * r] = halves[0][:, 0:256]
+        sg_out[3 * r + 1] = jnp.concatenate([halves[0][:, 256:384], halves[1][:, 0:128]], axis=1)
+        sg_out[3 * r + 2] = halves[1][:, 128:384]
+
+    def x_close(r):
+        for cp in s_pair(r) + [x_cross(r), x_next(r)] + x_quad(r) + x_give(r) + [x_back(r)]:
+            cp.wait_send()
 
     for i in range(IMAGES):
         QT[:, i * BLOCK : (i + 1) * BLOCK] = P0[EDGE + i * BLOCK : EDGE + (i + 1) * BLOCK, :].T.astype(BF16)
-    wide_give(0)
     s_make(0)
     s_make(1)
     s_pair_add(0)
+    y_start()
     s_make(2)
     s_pair_add(1)
+    x_start(1)
     s_pair_add(2)
+    x_start(2)
+    e_second()
 
     shift1, gain1 = unpack2(ar_finish(5, "all", 4))
     k1_h = -a1_gain * gain1 * scale1 * inv_n2
@@ -952,7 +1103,6 @@
     lax.fori_loop(0, OWN, own_back_first, 0)
     ig_here[0].start()
     ig_there[0].start()
-    s_next_add(0)
 
     def features_of(part):
         return jnp.concatenate([half_of(F.at[0], part), half_of(F.at[1], part)], axis=1)
@@ -968,22 +1118,24 @@
         return carry
 
     lax.fori_loop(0, OWN, other_back_first, 0)
-    s_next_add(1)
     acc_w[1] += mm_tn(half_of(G1, 1), features_of(1)).reshape(2, 2, 64, 512)
     pair_start(1)
     ig_here[1].start()
     ig_there[1].start()
-    s_quad_add(0)
-    s_next_add(2)
+    x_next_add(1)
+    x_next_add(2)
     pair_add(1)
-    s_quad_add(1)
-    s_cross_add(0)
-    s_quad_add(2)
-    s_cross_add(1)
+    y_quad_add()
+    x_cross_add(1)
+    y_next_add()
+    x_cross_add(2)
+    x_quad_add(1)
+    y_cross_add()
     wide_give(1)
-    s_cross_add(2)
-    for r in range(3):
-        s_give_back(r)
+    x_quad_add(2)
+    x_give_back(1)
+    y_give_back()
+    x_give_back(2)
 
     def own64(v):
         half = jnp.where(hi == 0, v[:, 0:128], v[:, 128:256])
@@ -1006,15 +1158,17 @@
         axis=0,
     )
 
-    wide_take(0, eg_out)
-    for r in range(3):
-        s_take(r)
+    e_take(eg_out)
+    x_take(1)
+    y_take()
     wide_take(1, rg_out)
-
-    wide_close(0)
+    x_take(2)
+
+    e_close()
     wide_close(1)
-    for r in range(3):
-        s_close(r)
+    y_close()
+    x_close(1)
+    x_close(2)
     for cp in ig_here:
         cp.wait()
     for cp in ig_there:
@@ -1103,16 +1257,26 @@
         V((3, 2, 64, 768), BF16),
         V((3, 2, 64, 768), BF16),
         V((3, 2, 2, 32, 768), F32),
+        V((16, 768), BF16),
+        V((16, 768), BF16),
+        V((2, 16, 768), F32),
+        V((2, 2, 32, 768), BF16),
+        V((3, 32, 768), BF16),
+        V((16, 768), F32),
+        V((16, 768), BF16),
+        V((16, 768), BF16),
+        V((n_hi, 16, 768), BF16),
+        V((2, 2, 16, 768), BF16),
+        V((3, 2, 32, 768), F32),
         V((3, 2, 32, 768), BF16),
         V((3, 2, 32, 768), BF16),
-        V((3, 2, 2, 16, 768), F32),
-        V((3, 2, 2, 16, 768), BF16),
-        V((3, 3, 16, 768), BF16),
-        V((3, 16, 768), F32),
-        V((3, 16, 768), BF16),
-        V((3, 16, 768), BF16),
-        V((3, n_hi, 16, 768), BF16),
-        V((3, 2, 2, 16, 768), BF16),
+        V((3, 32, 768), BF16),
+        V((3, 32, 768), BF16),
+        V((3, 2, 2, 16, 384), F32),
+        V((3, 2, 2, 16, 384), BF16),
+        V((3, 3, 16, 384), BF16),
+        V((3, n_hi, 16, 384), BF16),
+        V((3, 2, 2, 2, 16, 384), BF16),
         DMA((14,)),
         DMA((4,)),
         DMA((4,)),
@@ -1166,7 +1330,7 @@
         out_shape=tuple(jax.ShapeDtypeStruct(v.shape, v.dtype) for v in made[:5]) + (narrow,) * 4 + (broad,) * 2,
         in_specs=[any_space] * 5 + [vmem],
         out_specs=(any_space,) * 5 + (vmem,) * 6,
-        scratch_shapes=[DMA((5,))],
+        scratch_shapes=[DMA((20,))],
         compiler_params=pltpu.CompilerParams(vmem_limit_bytes=2**20),
         name="outputs",
     )(*[pltpu.with_memory_space_constraint(v, pltpu.VMEM) for v in made])
@@ -1174,7 +1338,13 @@
 
 def finish(*refs):
     made, stats, outs, small, sems = refs[:5], refs[5], refs[6:11], refs[11:17], refs[17]
-    copies = [pltpu.make_async_copy(a, b, sems.at[i]) for i, (a, b) in enumerate(zip(made, outs))]
+    copies = []
+    for a, b in zip(made, outs):
+        parts = 4 if a.shape[0] % 4 == 0 else 3
+        rows = a.shape[0] // parts
+        for k in range(parts):
+            at = pl.ds(k * rows, rows)
+            copies.append(pltpu.make_async_copy(a.at[at], b.at[at], sems.at[len(copies)]))
     for cp in copies:
         cp.start()
     for i, out in enumerate(small):

time: 102 us -> 98.3 us (0.964)
  Pallas kernels: 101 us -> 97.4 us
    pallas_call x1, Pallas kernels: 98.5 us -> 94.7 us  [block(): pl.pallas_call(functools.partial(kernel, n_pix, n_ch), out_shape=(wide, w...]
where the time goes in v5:
time: 98.3 us; the launch traced here: 98.1 us
  Pallas kernels  97.4 us (99%)
    pallas_call x1, Pallas kernels, block(): pl.pallas_call(functools.partial(kernel, n_pix, n_ch), out_shape=(wide, w...  94.7 us
    pallas_call x1, Pallas kernels, block(): pl.pallas_call(finish, out_shape=tuple((jax.ShapeDtypeStruct(v.shape, v.d...  2.79 us

profile of v5, /device:TPU:0, one launch (start us, length us, event | category | flops | bytes accessed | tf_op | source)
XLA Modules:
  0.0 98.1 jit_solution(8744390699601113317)
XLA Ops:
  0.6 94.7 %bottleneck.1 = (bf16[28,112,256]{2,1,0:T(8,128)(2,1)S(1)}, bf16[28,112,256]{2,1,0:T(8,128)(2,1)S(1)}, f32[64,1024]{1,0:T(8,128)S(1)}, f32[9,64,256]{2,1,0:T(8,1...) custom-call(bf16[28,112,256]{2,1,0:T(8,128)(2,1)} %bitcast.12, bf16[28,112,256]{2,1,0:T(8,128)(2,1)} %bitcast.13, ...), custom_call_target="tpu_custom_call" | custom-call | tf_op jit(solution)/shard_map/bottleneck/pallas_call | solution.py:1300
  95.3 2.8 %outputs.1 = (bf16[28,112,256]{2,1,0:T(8,128)(2,1)}, bf16[28,112,256]{2,1,0:T(8,128)(2,1)}, f32[64,1024]{1,0:T(8,128)}, f32[9,64,256]{2,1,0:T(8,128)}, f32[64,10...) custom-call(bf16[28,112,256]{2,1,0:T(8,128)(2,1)S(1)} %get-tuple-ele, ...), custom_call_target="tpu_custom_call" | custom-call | tf_op jit(solution)/shard_map/outputs/pallas_call | solution.py:1328

commit v6 on v4

v6 whole, which is shorter than its diff:
```python
import functools

import jax
import jax.numpy as jnp
from jax import lax
from jax.experimental import pallas as pl
from jax.experimental.pallas import tpu as pltpu
from jax.sharding import PartitionSpec as P

SIDE = 14
EPS = 1e-05
MESH = pl.DeviceIdType.MESH
F32 = jnp.float32
BF16 = jnp.bfloat16

ROWS = 112
OWN = 7
BOTH = 14
IMAGES = 4
PAD = 16
FLAT = IMAGES * PAD * PAD
EDGE = 8
BLOCK = PAD * PAD


def mm(a, b):
    return jnp.dot(a, b, preferred_element_type=F32)


def mm_nt(a, b):
    return lax.dot_general(a, b, (((1,), (1,)), ((), ())), preferred_element_type=F32)


def mm_tn(a, b):
    return lax.dot_general(a, b, (((0,), (0,)), ((), ())), preferred_element_type=F32)


def logistic(v):
    return 0.5 * jnp.tanh(0.5 * v) + 0.5


def fold8(v):
    return jnp.sum(v.reshape(v.shape[0] // 8, 8, v.shape[1]), axis=0)


def fold1(v):
    return jnp.sum(v, axis=0, keepdims=True)


def spread(v, lanes):
    return jnp.concatenate([v] * (lanes // 128), axis=1)


def kernel(
    n_pix,
    n_ch,
    feat,
    cot,
    mask,
    w1_in,
    w2_in,
    w3_in,
    g1_in,
    b1_in,
    g2_in,
    b2_in,
    g3_in,
    b3_in,
    res_out,
    ig_out,
    rg_out,
    sg_out,
    eg_out,
    st_out,
    mask_v,
    g1_v,
    b1_v,
    g2_v,
    b2_v,
    g3_v,
    b3_v,
    F,
    C,
    V,
    W1T,
    W2T,
    W3,
    W3X,
    pk,
    sbuf,
    rbuf,
    h1s,
    h1r,
    H1,
    h1b,
    h1o,
    D1,
    comp,
    P0,
    PC,
    Q,
    padded,
    H2,
    h2s,
    h2r,
    A2,
    D2,
    D2b,
    D2h,
    H3,
    GS,
    RES,
    G3,
    kb,
    kr,
    E2,
    e2s,
    e2r,
    E1,
    e1s,
    e1r,
    G1,
    QT,
    rows28,
    acc_w,
    wp,
    wc,
    wa,
    wb,
    wr,
    wq,
    wu,
    wh,
    wf,
    wfin,
    acc_s,
    sp,
    sc,
    s1,
    sb,
    sr,
    st,
    sz,
    sq,
    sx,
    sh,
    sfin,
    ld_sem,
    fx_send,
    fx_recv,
    w_send,
    w_recv,
    ar_send,
    ar_recv,
    x_send,
    x_recv,
    o_send,
    o_recv,
    g_send,
    g_recv,
    s_send,
    s_recv,
    h_send,
    h_recv,
):
    me_p, me_c = lax.axis_index("pix"), lax.axis_index("ch")
    hi, lo = me_c // 2, lax.rem(me_c, 2)
    n_lo = 8
    n_hi = n_pix // n_lo
    g_hi, g_lo = me_p // n_lo, lax.rem(me_p, n_lo)
    across = (me_p, (1 - hi) * 2 + lo)
    beside = (me_p, hi * 2 + 1 - lo)
    n_all = n_pix * n_ch

    def remote(src, dst, send, recv, device):
        return pltpu.make_async_remote_copy(
            src_ref=src, dst_ref=dst, send_sem=send, recv_sem=recv, device_id=device, device_id_type=MESH
        )

    def local(src, dst, sem):
        return pltpu.make_async_copy(src, dst, sem)

    mine, theirs = lo * BOTH, (1 - lo) * BOTH
    part0, part1 = hi * OWN, (1 - hi) * OWN

    def columns(ref, h):
        return ref.at[:, pl.ds(pl.multiple_of(h * 512, 512), 512)]

    def arrived(dst, sem):
        local(dst, dst, sem).wait()

    w1_load = local(columns(w1_in, hi), W1T.at[me_c], ld_sem.at[0])
    w2_load = local(w2_in, W2T.at[me_c], ld_sem.at[1])
    halves = ((0, part0), (1, part1))
    f_load = [
        local(feat.at[pl.ds(mine + part, OWN)], F.at[lo, pl.ds(OWN * s, OWN)], ld_sem.at[2 + s]) for s, part in halves
    ]
    c_load = [
        local(cot.at[pl.ds(mine + part, OWN)], C.at[lo, pl.ds(OWN * s, OWN)], ld_sem.at[4]) for s, part in halves
    ]
    w3_load = [
        local(columns(w3_in, hi), W3.at[me_c], ld_sem.at[5]),
        local(columns(w3_in, 1 - hi), W3X.at[me_c], ld_sem.at[5]),
    ]
    small_load = [local(mask, mask_v, ld_sem.at[6])]
    pairs = ((g1_in, g1_v), (b1_in, b1_v), (g2_in, g2_v), (b2_in, b2_v), (g3_in, g3_v), (b3_in, b3_v))
    small_load += [local(a, b, ld_sem.at[7 + i]) for i, (a, b) in enumerate(pairs)]

    barrier = pltpu.get_barrier_semaphore()

    def greet(t, carry):
        q = lax.rem(me_p * n_ch + me_c + t, n_all)
        pl.semaphore_signal(barrier, inc=1, device_id=(q // n_ch, lax.rem(q, n_ch)), device_id_type=MESH)
        return carry

    lax.fori_loop(1, n_all, greet, 0)
    for cp in small_load:
        cp.start()
    w1_load.start()
    f_load[1].start()
    f_load[0].start()
    w2_load.start()
    for cp in w3_load + c_load:
        cp.start()

    pl.semaphore_wait(barrier, n_all - 1)

    fx = [
        remote(feat.at[pl.ds(theirs + part, OWN)], F.at[lo, pl.ds(OWN * s, OWN)], fx_send.at[0], fx_recv.at[s], beside)
        for s, part in halves
    ]
    cx = [
        remote(cot.at[pl.ds(theirs + part, OWN)], C.at[lo, pl.ds(OWN * s, OWN)], fx_send.at[1], fx_recv.at[2], beside)
        for s, part in halves
    ]
    far, near, last_one = (1 - hi) * 2 + lo, hi * 2 + 1 - lo, (1 - hi) * 2 + 1 - lo

    quad, top = lax.rem(g_lo, 4), g_lo // 4
    low, high = lax.rem(quad, 2), quad // 2
    next_group = (g_hi * n_lo + top * 4 + high * 2 + 1 - low, me_c)

    w1x = [
        remote(columns(w1_in, 1 - hi), W1T.at[me_c], w_send.at[0], w_recv.at[1], across),
        remote(columns(w1_in, hi), W1T.at[me_c], w_send.at[0], w_recv.at[0], beside),
        remote(W1T.at[far], W1T.at[far], w_send.at[0], w_recv.at[3], beside),
    ]
    pkx = [
        remote(pk.at[me_c], pk.at[me_c], w_send.at[5], w_recv.at[4], across),
        remote(pk.at[me_c], pk.at[me_c], w_send.at[5], w_recv.at[5], beside),
        remote(pk.at[far], pk.at[far], w_send.at[5], w_recv.at[5], beside),
    ]

    def w2_piece(ref, q):
        return ref.at[
            :, pl.ds(pl.multiple_of(q // 2 * 16, 16), 16), pl.ds(pl.multiple_of(lax.rem(q, 2) * 128, 128), 128)
        ]

    def w3_piece(ref, q, first):
        return ref.at[
            pl.ds(pl.multiple_of(q // 2 * 16, 16), 16), pl.ds(pl.multiple_of(first + lax.rem(q, 2) * 256, 256), 256)
        ]

    w2x = [
        remote(w2_piece(w2_in, g_lo), w2_piece(W2T.at[me_c], g_lo), w_send.at[3], w_recv.at[6], across),
        remote(W2T.at[me_c], W2T.at[me_c], w_send.at[1], w_recv.at[8], beside),
        remote(W2T.at[far], W2T.at[far], w_send.at[1], w_recv.at[9], beside),
    ]
    w3x = [
        remote(w3_piece(w3_in, g_lo, (1 - hi) * 512), w3_piece(W3.at[me_c], g_lo, 0), w_send.at[4], w_recv.at[10], across),
        remote(columns(w3_in, hi), W3.at[me_c], w_send.at[2], w_recv.at[12], beside),
        remote(W3.at[far], W3.at[far], w_send.at[2], w_recv.at[13], beside),
    ]
    w3y = [
        remote(w3_piece(w3_in, g_lo, hi * 512), w3_piece(W3X.at[me_c], g_lo, 0), w_send.at[4], w_recv.at[14], across),
        remote(columns(w3_in, 1 - hi), W3X.at[me_c], w_send.at[2], w_recv.at[16], beside),
        remote(W3X.at[far], W3X.at[far], w_send.at[2], w_recv.at[17], beside),
    ]
    shared, shared_y = [], []
    for t in range(1, n_lo):
        to = (g_hi * n_lo + lax.rem(g_lo + t, n_lo), me_c)
        for spot, sent, got, group in (
            (w2_piece(W2T.at[far], g_lo), 3, 7, shared),
            (w3_piece(W3.at[far], g_lo, 0), 4, 11, shared),
            (w3_piece(W3X.at[far], g_lo, 0), 4, 15, shared_y),
        ):
            group.append(remote(spot, spot, w_send.at[sent], w_recv.at[got], to))
    w1x[0].start()
    w1x[1].start()
    fx[1].start()
    fx[0].start()
    w3x[0].start()
    w2x[0].start()

    row_i = lax.broadcasted_iota(jnp.int32, (64, 256), 0)
    col_i = lax.broadcasted_iota(jnp.int32, (64, 256), 1)
    place = (row_i == col_i - 64 * me_c).astype(BF16)
    for cp in small_load:
        cp.wait()
    narrow = jnp.concatenate([v[...].astype(F32).reshape(1, 64) for v in (g1_v, b1_v, g2_v, b2_v)] * 2, axis=0)
    pk_rows = [mm(narrow.astype(BF16), place)[0:4]]
    pk_rows += [v[...].astype(F32).reshape(1, 256) for v in (g3_v, b3_v)]
    pk[me_c] = jnp.concatenate(pk_rows + [jnp.zeros((2, 256), F32)], axis=0)

    pkx[1].start()

    def ar_group(kind):
        if kind == "all":
            return n_all, me_p * n_ch + me_c, lambda q: (q // n_ch, lax.rem(q, n_ch))
        if kind == "half":
            return n_pix * 2, me_p * 2 + lo, lambda q: (q // 2, hi * 2 + lax.rem(q, 2))
        return n_pix, me_p, lambda q: (q, me_c)

    def ar_start(k, val, kind):
        n, me, device = ar_group(kind)
        rows = val.shape[0]
        sbuf[k, 0:rows] = val
        rbuf[k, me, 0:rows] = val

        def send(t, carry):
            to = device(lax.rem(me + t, n))
            cut = pl.ds(0, rows)
            remote(sbuf.at[k, cut], rbuf.at[k, me, cut], ar_send.at[k], ar_recv.at[k], to).start()
            return carry

        lax.fori_loop(1, n, send, 0)

    def ar_finish(k, kind, rows):
        n = ar_group(kind)[0]
        arrived(rbuf.at[k, pl.ds(0, n - 1), pl.ds(0, rows)], ar_recv.at[k])
        return jnp.sum(rbuf[k, 0:n, 0:rows], axis=0)

    def ar_close(k, kind, rows):
        n = ar_group(kind)[0]
        arrived(rbuf.at[k, pl.ds(0, n - 1), pl.ds(0, rows)], ar_send.at[k])

    def pack2(a, b):
        return jnp.concatenate([a[:, 0:128], a[:, 128:256], b[:, 0:128], b[:, 128:256]], axis=0)

    def unpack2(v):
        return (
            jnp.concatenate([v[0:1], v[1:2]], axis=1),
            jnp.concatenate([v[2:3], v[3:4]], axis=1),
        )

    def pack3(a, b):
        return jnp.concatenate([a[:, 128 * i : 128 * (i + 1)] for i in range(4)] + [b[:, 128 * i : 128 * (i + 1)] for i in range(4)], axis=0)

    def unpack3(v):
        return (
            jnp.concatenate([v[i : i + 1] for i in range(4)], axis=1),
            jnp.concatenate([v[i : i + 1] for i in range(4, 8)], axis=1),
        )


    w1_load.wait()
    w2_load.wait()
    f_load[1].wait()
    fx[1].wait_recv()
    arrived(W1T.at[near], w_recv.at[0])

    def wide_rows(t):
        return jnp.concatenate([F[0, t], F[1, t]], axis=1)

    def xcopy(kind, src, dst, t):
        got = (0, 8 + t, 15 + jnp.where(t < 2, 0, 1), 17, None, 1 + t)[kind]
        return remote(src.at[t], dst.at[t], x_send.at[kind], x_recv.at[got], across)

    def send_first(h, kind):
        w = W1T[pl.ds(2 * h, 2)].reshape(128, 512)

        def one(t, carry):
            h1s[h, t] = mm_nt(wide_rows(t + OWN), w).astype(BF16)
            xcopy(kind, h1s.at[h], h1r.at[h], t).start()
            return carry

        lax.fori_loop(0, OWN, one, 0)

    send_first(hi, 0)
    arrived(W1T.at[far], w_recv.at[1])
    w1x[2].start()
    arrived(w3_piece(W3.at[far], g_lo, 0), w_recv.at[10])
    arrived(w2_piece(W2T.at[far], g_lo), w_recv.at[6])
    for cp in shared:
        cp.start()

    flat = mask_v[...].astype(F32).reshape(1, rows28.shape[0] * ROWS)
    for t in range(rows28.shape[0]):
        rows28[t : t + 1, :] = flat[:, t * ROWS : (t + 1) * ROWS]
    diag = lax.broadcasted_iota(jnp.int32, (ROWS, ROWS), 0) == lax.broadcasted_iota(jnp.int32, (ROWS, ROWS), 1)
    ones = jnp.ones((ROWS, 128), BF16)

    lanes = jnp.broadcast_to(jnp.sum(rows28[...], axis=0, keepdims=True), (8, ROWS))
    local_count = mm(lanes.astype(BF16), ones)
    P0[...] = jnp.zeros_like(P0)
    PC[0:PAD, :] = jnp.zeros((PAD, 768), BF16)
    PC[PAD + FLAT :, :] = jnp.zeros((PAD, 768), BF16)
    ar_start(6, local_count, "pix")

    arrived(W1T.at[last_one], w_recv.at[3])
    send_first(1 - hi, 5)
    pkx[0].start()
    f_load[0].wait()
    fx[0].wait_recv()

    w1_all = W1T[...].reshape(256, 512)

    def keep_first(t, carry):
        H1[t] = mm_nt(wide_rows(t), w1_all)
        return carry

    lax.fori_loop(0, OWN, keep_first, 0)

    def put_mask(t, carry):
        at = mine + jnp.where(t < OWN, part0 + t, part1 + t - OWN)
        row = rows28[pl.ds(at, 1), :]
        V[t] = mm(jnp.where(diag, row, 0.0).astype(BF16), ones)
        return carry

    lax.fori_loop(0, BOTH, put_mask, 0)

    for cp in (w2x[1], w3x[1], cx[0], cx[1]):
        cp.start()

    zero = jnp.zeros((8, 256), F32)

    def sum_first(t, carry):
        s, q = carry
        xcopy(5, h1s.at[0], h1r.at[0], t).wait_recv()
        h = H1[t] + jnp.concatenate([h1r[0, t], h1r[1, t]], axis=1).astype(F32)
        H1[t] = h
        h1b[t] = h.astype(BF16)
        vh = spread(V[t], 256) * h
        return s + fold8(vh), q + fold8(vh * h)

    arrived(h1r.at[0], x_recv.at[0])
    s, q = lax.fori_loop(0, OWN, sum_first, (zero, zero))
    ar_start(0, pack2(fold1(s), fold1(q)), "all")
    arrived(pk.at[far], w_recv.at[4])
    pkx[2].start()
    arrived(W3.at[pl.ds(0, 2)], ld_sem.at[5])
    arrived(G3.at[pl.ds(0, 9), :, pl.ds(0, 128)], w_recv.at[7])
    arrived(A2.at[0], w_recv.at[11])
    w2x[2].start()
    w3x[2].start()
    arrived(pk.at[pl.ds(0, 2)], w_recv.at[5])
    gains = pk[0] + pk[1] + pk[2] + pk[3]
    g1, b1, g2, b2 = (gains[k : k + 1] for k in range(4))
    pair0, pair1 = pk[2 * hi], pk[2 * hi + 1]
    g3 = jnp.concatenate([pair0[4:5], pair1[4:5]], axis=1)
    b3 = jnp.concatenate([pair0[5:6], pair1[5:6]], axis=1)
    inv_n = 1.0 / spread(ar_finish(6, "pix", 8)[0:1], 512)
    inv_n2 = inv_n[:, 0:256]
    s, q = unpack2(ar_finish(0, "all", 4))
    w3y[0].start()
    avg1 = s * inv_n2
    scale1 = lax.rsqrt(q * inv_n2 - avg1 * avg1 + EPS)
    a1_gain = g1 * scale1
    a1_shift = b1 - avg1 * a1_gain

    def act_first(t, carry):
        v = spread(V[t], 256)
        aff = v * (H1[t] * a1_gain + a1_shift)
        sig = logistic(aff)
        act = aff * sig
        comp[pl.ds(pl.multiple_of(t * ROWS, 16), ROWS), :] = act
        D1[t] = v * (sig + act * (1.0 - sig))
        return carry

    def to_padded(images):
        for i in images:
            for y in range(SIDE):
                at = EDGE + (i * PAD + y + 1) * PAD
                P0[at : at + SIDE, :] = comp[(i * SIDE + y) * SIDE : (i * SIDE + y + 1) * SIDE, :]

    def from_padded(dst, image, first, last):
        for y in range(first, last):
            at = (image * PAD + y + 1) * PAD
            dst[(image * SIDE + y) * SIDE : (image * SIDE + y + 1) * SIDE, :] = padded[at : at + SIDE, :]

    def columns_forward(images):
        for i in images:
            for c in range(3):
                at = EDGE + i * BLOCK + c - 1
                PC[PAD + i * BLOCK : PAD + (i + 1) * BLOCK, 256 * c : 256 * (c + 1)] = P0[at : at + BLOCK, :].astype(BF16)

    lax.fori_loop(0, 2, act_first, 0)
    to_padded((0,))
    columns_forward((0,))

    arrived(W2T.at[near], w_recv.at[8])
    arrived(W2T.at[last_one], w_recv.at[9])
    h1x = [remote(h1b, h1o, x_send.at[4], x_recv.at[18], across)]

    def conv(first, rows):
        taps = [PC[PAD * r + first : PAD * r + first + rows, :] for r in range(3)]
        weights = [W2T[:, k].reshape(256, 256) for k in range(9)]
        padded[first : first + rows, :] = mm_nt(jnp.concatenate(taps, axis=1), jnp.concatenate(weights, axis=1))

    def sum_second(t, carry):
        s, q = carry
        h = H2[pl.ds(pl.multiple_of(t * ROWS, 16), ROWS), :]
        h2s[t] = h.astype(BF16)
        vh = spread(V[t], 256) * h
        return s + fold8(vh), q + fold8(vh * h)

    def start_all(kind, src, dst, first, last):
        for t in range(first, last):
            xcopy(kind, src, dst, t).start()

    early = 3
    pieces = (
        (PAD, 8 * PAD, ((0, 0, 8),), 1),
        (9 * PAD, 2 * BLOCK - 10 * PAD, ((0, 8, SIDE), (1, 0, SIDE)), 3),
        (2 * BLOCK + PAD, 2 * BLOCK - 2 * PAD, ((2, 0, SIDE), (3, 0, SIDE)), OWN),
    )
    carry, done = (zero, zero), 0
    for first, rows, images, now in pieces:
        conv(first, rows)
        for image, y0, y1 in images:
            from_padded(H2, image, y0, y1)
        carry = lax.fori_loop(done, now, sum_second, carry)
        start_all(1, h2s, h2r, min(done, early), min(now, early))
        if done == 0:
            lax.fori_loop(2, OWN, act_first, 0)
            to_padded((1, 2, 3))
            columns_forward((1, 2, 3))
        done = now
    s, q = carry
    ar_start(1, pack2(fold1(s), fold1(q)), "all")
    start_all(1, h2s, h2r, early, OWN)
    s, q = unpack2(ar_finish(1, "all", 4))
    avg2 = s * inv_n2
    scale2 = lax.rsqrt(q * inv_n2 - avg2 * avg2 + EPS)
    a2_gain = g2 * scale2
    a2_shift = b2 - avg2 * a2_gain

    arrived(w3_piece(W3X.at[far], g_lo, 0), w_recv.at[14])
    for cp in shared_y:
        cp.start()
    w3y[1].start()
    arrived(W3.at[near], w_recv.at[12])
    arrived(W3.at[last_one], w_recv.at[13])

    def act_second(t, h, carry):
        s, q, d, e = carry
        v = spread(V[t], 256)
        aff = v * (h * a2_gain + a2_shift)
        sig = logistic(aff)
        act = aff * sig
        slope = v * (sig + act * (1.0 - sig))
        far_slope = slope * (h - avg2)
        D2[t] = slope
        D2b[t] = slope.astype(BF16)
        D2h[t] = far_slope.astype(BF16)
        act = act.astype(BF16)
        A2[t] = act
        h3 = mm(act, W3[...].reshape(256, 512))
        H3[t] = h3
        return s + fold8(h3), q + fold8(h3 * h3), d + fold8(slope), e + fold8(far_slope)

    def own_second(t, carry):
        return act_second(t, H2[pl.ds(pl.multiple_of(t * ROWS, 16), ROWS), :], carry)

    def other_second(t, carry):
        xcopy(1, h2s, h2r, t).wait_recv()
        return act_second(t + OWN, h2r[t].astype(F32), carry)

    wide_zero = jnp.zeros((8, 512), F32)
    carry = lax.fori_loop(0, OWN, own_second, (wide_zero, wide_zero, zero, zero))
    for cp in h1x:
        cp.start()
    s, q, slopes, far_slopes = lax.fori_loop(0, OWN, other_second, carry)
    ar_start(2, pack3(fold1(s), fold1(q)), "half")
    arrived(C.at[lo], ld_sem.at[4])
    arrived(C.at[1 - lo], fx_recv.at[2])
    def half_of(ref, part):
        return ref[OWN * part : OWN * (part + 1)].reshape(OWN * ROWS, ref.shape[2])

    cross_d = mm_tn(half_of(A2, 0), half_of(D2b, 0)) + mm_tn(half_of(A2, 1), half_of(D2b, 1))
    cross_h = mm_tn(half_of(A2, 0), half_of(D2h, 0)) + mm_tn(half_of(A2, 1), half_of(D2h, 1))
    slopes, far_slopes = fold1(slopes), fold1(far_slopes)
    arrived(A2.at[0], w_recv.at[15])
    w3y[2].start()

    s, q = unpack3(ar_finish(2, "half", 8))
    avg3 = s * inv_n
    scale3 = lax.rsqrt(q * inv_n - avg3 * avg3 + EPS)
    a3_gain = g3 * scale3
    a3_shift = b3 - avg3 * a3_gain

    def put_out(ref, t, out):
        first, second = out[:, 0:256].astype(BF16), out[:, 256:512].astype(BF16)
        ref[mine + jnp.where(t < OWN, part0 + t, part1 + t - OWN)] = jnp.where(lo == 0, first, second)
        RES[t] = jnp.where(lo == 0, second, first)

    def last(t, carry):
        s, q = carry
        v = spread(V[t], 512)
        h3 = H3[t]
        wide = jnp.concatenate([F[0, t], F[1, t]], axis=1).astype(F32)
        total = v * (h3 * a3_gain + a3_shift) + wide
        sig = logistic(total)
        out = total * sig
        put_out(res_out, t, out)
        given = jnp.concatenate([C[0, t], C[1, t]], axis=1).astype(F32)
        gs = given * (sig + out * (1.0 - sig))
        GS[t] = gs
        vg = v * gs
        return s + fold8(vg), q + fold8(vg * (h3 - avg3))

    def product(t, h, carry):
        s, q = carry
        given = (spread(V[t], 512) * (a3_gain * GS[t])).astype(BF16)
        e = mm_nt(given, W3[...].reshape(256, 512)) * D2[t]
        return e, (s + fold8(e), q + fold8(e * (h - avg2)))

    def other_product(t, carry):
        e, carry = product(t + OWN, h2r[t].astype(F32), carry)
        e2s[t] = e.astype(BF16)
        return carry

    def last_and_product(t, carry):
        sums = last(t + OWN, carry[0])
        prods = other_product(t, carry[1])
        xcopy(2, e2s, e2r, t).start()
        return sums, prods

    def own_product(t, carry):
        e, carry = product(t, H2[pl.ds(pl.multiple_of(t * ROWS, 16), ROWS), :], carry)
        E2[t] = e
        return carry

    sums, prods = lax.fori_loop(0, 3, last_and_product, ((wide_zero, wide_zero), (zero, zero)))
    sums = lax.fori_loop(OWN + 3, BOTH, last, sums)
    s, q = lax.fori_loop(0, OWN, last, sums)
    ar_start(3, pack3(fold1(s), fold1(q * scale3)), "half")
    prods = lax.fori_loop(3, OWN, other_product, prods)
    start_all(2, e2s, e2r, 3, 4)
    prods = lax.fori_loop(0, OWN, own_product, prods)
    def beside_out(ref, k):
        return [
            remote(RES.at[pl.ds(OWN * s, OWN)], ref.at[pl.ds(mine + part, OWN)], o_send.at[k], o_recv.at[k], beside)
            for s, part in halves
        ]

    res_there, ig_there = beside_out(res_out, 0), beside_out(ig_out, 1)
    shift3, gain3 = unpack3(ar_finish(3, "half", 8))
    k3_h = -a3_gain * gain3 * scale3 * inv_n
    k3_0 = -a3_gain * shift3 * inv_n - k3_h * avg3

    def low_high(v):
        high = v.astype(BF16)
        return high, (v - high.astype(F32)).astype(BF16)

    def corrections(by_h, by_0, weights):
        flat = weights[...].reshape(256, 512)
        high, low = low_high(flat.astype(F32) * by_h)
        square = mm_nt(high, flat) + mm_nt(low, flat)
        high, low = low_high(by_0)
        rows = mm_nt(jnp.concatenate([high.astype(F32), low.astype(F32)] * 4, axis=0).astype(BF16), flat)
        return square, rows[0:1] + rows[1:2]

    kb[...] = jnp.concatenate([k3_h, k3_0, jnp.zeros((6, 512), F32)], axis=0)
    kx = remote(kb, kr, w_send.at[6], w_recv.at[18], across)
    kx.start()
    start_all(2, e2s, e2r, 4, 5)
    square, line = corrections(k3_h, k3_0, W3)
    s = fold1(prods[0]) + fold1(square * cross_d) + line * slopes
    q = fold1(prods[1]) + fold1(square * cross_h) + line * far_slopes
    ar_start(4, pack2(s, q * scale2), "all")
    start_all(2, e2s, e2r, 5, OWN)
    for cp in res_there:
        cp.start()

    def back_third(t, carry):
        v = spread(V[t], 512)
        G3[t] = (v * (a3_gain * GS[t] + k3_h * H3[t] + k3_0)).astype(BF16)
        return carry

    lax.fori_loop(0, BOTH, back_third, 0)

    def group_at(t, up=False):
        return (g_hi * n_lo + (1 - top if up else top) * 4 + lax.rem(quad + t, 4), me_c)

    def over_groups(total, level, sems):
        if n_hi == 1:
            return total
        level[g_hi] = total.astype(BF16)

        def swap(t):
            q = lax.rem(g_hi + t, n_hi)
            return remote(level.at[g_hi], level.at[g_hi], sems[0].at[t], sems[1].at[t], (q * n_lo + g_lo, me_c))

        for t in range(1, n_hi):
            swap(t).start()
        for t in range(1, n_hi):
            swap(t).wait()
        total = level[0].astype(F32)
        for t in range(1, n_hi):
            total = total + level[t].astype(F32)
        return total

    def pair_copies(k):
        return [remote(wp.at[k, h], wc.at[k, h], g_send.at[k], g_recv.at[k, 0], beside) for h in range(2)]

    def four_copies(k):
        return [
            remote(wb.at[k, lax.rem(quad + t, 4)], wr.at[k, quad], g_send.at[k], g_recv.at[k, 1], group_at(t))
            for t in range(1, 4)
        ]

    def swap_copy(k):
        return remote(wq.at[k], wu.at[k], g_send.at[k], g_recv.at[k, 2], group_at(0, True))

    def give_copies(k):
        spot = wfin.at[k, hi, quad]
        copies = []
        for t in range(4):
            group, place = group_at(t)
            if t > 0:
                copies.append(remote(wf.at[k, hi], spot, g_send.at[k], g_recv.at[k, 3], (group, place)))
            copies.append(
                remote(wf.at[k, 1 - hi], spot, g_send.at[k], g_recv.at[k, 3], (group, (1 - hi) * 2 + lo))
            )
        return copies

    def pair_start(k):
        for h in range(2):
            wp[k, h] = acc_w[k, h, 1 - lo].astype(BF16)
        for cp in pair_copies(k):
            cp.start()

    def pair_add(k):
        arrived(wc.at[k], g_recv.at[k, 0])
        for h in range(2):
            both = (acc_w[k, h, lo] + wc[k, h].astype(F32)).reshape(4, 16, 512)
            wa[k, h] = both
            for q in range(4):
                wb[k, q, h] = both[q].astype(BF16)
        for cp in four_copies(k):
            cp.start()

    def four_add(k):
        arrived(wr.at[k, pl.ds(0, 3)], g_recv.at[k, 1])
        total = wa[k, :, quad]
        for t in range(1, 4):
            total = total + wr[k, lax.rem(quad + t, 4)].astype(F32)
        wq[k] = total.astype(BF16)
        swap_copy(k).start()

    def swap_add(k):
        arrived(wu.at[k], g_recv.at[k, 2])
        total = over_groups(wq[k].astype(F32) + wu[k].astype(F32), wh.at[k], (h_send.at[k], h_recv.at[k]))
        wf[k] = total.astype(BF16)
        wfin[k, hi, quad] = wf[k, hi]
        for cp in give_copies(k):
            cp.start()

    def wide_take(k, out):
        arrived(A2.at[pl.ds(0, 2)], g_recv.at[k, 3])
        for h in range(2):
            out[:, 512 * h : 512 * (h + 1)] = wfin[k, h].astype(F32).reshape(64, 512)

    def wide_close(k):
        arrived(Q.at[0, pl.ds(0, 736)], g_send.at[k])

    acc_w[0] = (mm_tn(half_of(A2, 0), half_of(G3, 0)) + mm_tn(half_of(A2, 1), half_of(G3, 1))).reshape(2, 2, 64, 512)
    pair_start(0)
    arrived(kr, w_recv.at[18])
    arrived(W3X.at[near], w_recv.at[16])
    arrived(W3X.at[last_one], w_recv.at[17])
    square_x, line_x = corrections(kr[0:1], kr[1:2], W3X)
    square_both = jnp.concatenate(low_high(square + square_x), axis=1)
    line = line + line_x

    def correct(t, carry):
        both = mm(A2[t], square_both)
        E2[t] += D2[t] * (both[:, 0:256] + both[:, 256:512] + line)
        return carry

    lax.fori_loop(0, OWN, correct, 0)
    pair_add(0)

    shift2, gain2 = unpack2(ar_finish(4, "all", 4))
    k2_h = -a2_gain * gain2 * scale2 * inv_n2
    k2_0 = -a2_gain * shift2 * inv_n2 - k2_h * avg2

    def s_pair(r):
        return [remote(sp.at[r, h], sc.at[r, h], s_send.at[r], s_recv.at[r, 0], beside) for h in range(2)]

    def s_four(r):
        copies = []
        for t in range(1, 4):
            q = lax.rem(quad + t, 4)
            copies.append(
                remote(
                    sb.at[r, lax.rem(q, 2), q // 2], sr.at[r, low, high], s_send.at[r], s_recv.at[r, 1], group_at(t)
                )
            )
        return copies

    def s_low(r):
        return remote(sb.at[r, 1 - low], sr.at[r, 0], s_send.at[r], s_recv.at[r, 1], next_group)

    def s_high(r):
        to = (g_hi * n_lo + top * 4 + (1 - high) * 2 + low, me_c)
        return remote(sr.at[r, 1, 0], sz.at[r], s_send.at[r], s_recv.at[r, 2], to)

    def s_swap(r):
        up = group_at(0, True)[0]
        aside = (1 - hi) * 2 + lo
        return [
            remote(sq.at[r, 1 - hi], sx.at[r, 0], s_send.at[r], s_recv.at[r, 3], (me_p, aside)),
            remote(sq.at[r, hi], sx.at[r, 1], s_send.at[r], s_recv.at[r, 3], (up, me_c)),
            remote(sq.at[r, 1 - hi], sx.at[r, 2], s_send.at[r], s_recv.at[r, 3], (up, aside)),
        ]

    def s_give(r):
        spot = sfin.at[r, quad]
        return [remote(spot, spot, s_send.at[r], s_recv.at[r, 4], group_at(t)) for t in range(1, 4)]

    def s_make(r):
        taps = mm(QT[...], PC[PAD * r : PAD * r + FLAT, :])
        acc_s[r] = taps.reshape(2, 2, 64, 768)
        for h in range(2):
            sp[r, h] = acc_s[r, h, 1 - lo].astype(BF16)
        for cp in s_pair(r):
            cp.start()

    def s_pair_add(r):
        arrived(sc.at[r], s_recv.at[r, 0])
        for h in range(2):
            both = (acc_s[r, h, lo] + sc[r, h].astype(F32)).reshape(4, 16, 768)
            s1[r, h] = both
            for q in range(4):
                sb[r, q % 2, q // 2, h] = both[q].astype(BF16)
        for cp in s_four(r) if r == 2 else [s_low(r)]:
            cp.start()

    def s_low_add(r):
        arrived(sr.at[r, 0], s_recv.at[r, 1])
        for z in range(2):
            st[r, z] = s1[r, :, 2 * z + low] + sr[r, 0, z].astype(F32)
        sr[r, 1, 0] = st[r, 1 - high].astype(BF16)
        s_high(r).start()

    def s_four_add(r):
        if r == 2:
            arrived(PC.at[pl.ds(0, 96)], s_recv.at[r, 1])
            total = s1[r, :, quad]
            for t in range(1, 4):
                q = lax.rem(quad + t, 4)
                total = total + sr[r, lax.rem(q, 2), q // 2].astype(F32)
        else:
            arrived(sz.at[r], s_recv.at[r, 2])
            total = st[r, high] + sz[r].astype(F32)
        sq[r] = total.astype(BF16)
        for cp in s_swap(r):
            cp.start()

    def s_swap_add(r):
        arrived(sx.at[r], s_recv.at[r, 3])
        here = sq[r, hi].astype(F32) + sx[r, 0].astype(F32)
        there = sx[r, 1].astype(F32) + sx[r, 2].astype(F32)
        total = over_groups(here + there, sh.at[r], (h_send.at[2 + r], h_recv.at[2 + r]))
        sfin[r, quad] = total.astype(BF16)
        for cp in s_give(r):
            cp.start()

    def s_take(r):
        arrived(sfin.at[r, pl.ds(0, 3)], s_recv.at[r, 4])
        rows = sfin[r].astype(F32).reshape(64, 768)
        for c in range(3):
            sg_out[3 * r + c] = rows[:, 256 * c : 256 * (c + 1)]

    def s_close(r):
        arrived(PC.at[pl.ds(0, 320)], s_send.at[r])

    def back_second(t, carry):
        at = pl.ds(pl.multiple_of(t * ROWS, 16), ROWS)
        e = E2[t] + e2r[t].astype(F32)
        comp[at, :] = spread(V[t], 256) * (a2_gain * e + k2_h * H2[at, :] + k2_0)
        return carry

    def columns_back(images):
        for i in images:
            for c in range(3):
                at = EDGE + i * BLOCK - (c - 1)
                Q[c, i * BLOCK : (i + 1) * BLOCK, :] = P0[at : at + BLOCK, :].astype(BF16)

    def conv_back(first, rows):
        taps = []
        for r in range(3):
            at = first + PAD * (1 - r)
            taps += [Q[c, at : at + rows, :] for c in range(3)]
        weights = [W2T[:, k].reshape(256, 256) for k in range(9)]
        padded[first : first + rows, :] = mm(jnp.concatenate(taps, axis=1), jnp.concatenate(weights, axis=0))

    arrived(e2r.at[pl.ds(0, 2)], x_recv.at[15])
    lax.fori_loop(0, 2, back_second, 0)
    to_padded((0,))
    columns_back((0,))

    def sum_back_first(t, carry):
        s, q = carry
        e = comp[pl.ds(pl.multiple_of(t * ROWS, 16), ROWS), :] * D1[t]
        E1[t] = e
        e1s[t] = e.astype(BF16)
        return s + fold8(e), q + fold8(e * (H1[t] - avg1))

    carry, done = (zero, zero), 0
    for first, rows, images, now in pieces:
        if done == 3:
            for i in range(IMAGES):
                QT[:, i * BLOCK : (i + 1) * BLOCK] = P0[EDGE + i * BLOCK : EDGE + (i + 1) * BLOCK, :].T.astype(BF16)
            s_make(0)
        conv_back(first, rows)
        for image, y0, y1 in images:
            from_padded(comp, image, y0, y1)
        carry = lax.fori_loop(done, now, sum_back_first, carry)
        start_all(3, e1s, e1r, min(done, early), min(now, early))
        if done == 0:
            arrived(e2r.at[pl.ds(2, OWN - 2)], x_recv.at[16])
            lax.fori_loop(2, OWN, back_second, 0)
            to_padded((1, 2, 3))
            columns_back((1, 2, 3))
        done = now
    s, q = carry
    ar_start(5, pack2(fold1(s), fold1(q * scale1)), "all")
    start_all(3, e1s, e1r, early, OWN)
    four_add(0)

    s_pair_add(0)
    s_make(1)
    s_make(2)
    s_pair_add(1)
    s_pair_add(2)

    shift1, gain1 = unpack2(ar_finish(5, "all", 4))
    k1_h = -a1_gain * gain1 * scale1 * inv_n2
    k1_0 = -a1_gain * shift1 * inv_n2 - k1_h * avg1

    def back_first(t, e, h):
        G1[t] = (spread(V[t], 256) * (a1_gain * e + k1_h * h + k1_0)).astype(BF16)

    def input_term(t, carry):
        out = mm(G1[t], W1T[...].reshape(256, 512)) + GS[t]
        put_out(ig_out, t, out)
        return carry

    arrived(RES, o_send.at[0])

    def own_back_first(t, carry):
        back_first(t, E1[t], H1[t])
        return carry

    def features_of(part):
        return jnp.concatenate([half_of(F.at[0], part), half_of(F.at[1], part)], axis=1)

    lax.fori_loop(0, OWN, own_back_first, 0)
    own_reduce = mm_tn(half_of(G1, 0), features_of(0))
    acc_w[1] = own_reduce.reshape(2, 2, 64, 512)
    s_low_add(0)
    swap_add(0)
    lax.fori_loop(0, OWN, input_term, 0)
    ig_there[0].start()
    s_low_add(1)
    for cp in h1x:
        cp.wait_recv()

    def other_back_first(t, carry):
        back_first(t + OWN, e1r[t].astype(F32), h1o[t].astype(F32))
        return carry

    arrived(e1r, x_recv.at[17])
    lax.fori_loop(0, OWN, other_back_first, 0)
    acc_w[1] += mm_tn(half_of(G1, 1), features_of(1)).reshape(2, 2, 64, 512)
    pair_start(1)
    s_four_add(0)
    lax.fori_loop(OWN, BOTH, input_term, 0)
    ig_there[1].start()
    pair_add(1)
    s_four_add(1)
    s_four_add(2)
    s_swap_add(0)
    four_add(1)
    s_swap_add(1)
    s_swap_add(2)
    swap_add(1)

    def own64(v):
        half = jnp.where(hi == 0, v[:, 0:128], v[:, 128:256])
        swapped = jnp.concatenate([half[:, 64:128], half[:, 0:64]], axis=1)
        return jnp.concatenate([jnp.where(lo == 0, half, swapped), jnp.zeros((1, 128), F32)], axis=1)

    def own256(v):
        return jnp.where(lo == 0, v[:, 0:256], v[:, 256:512])

    st_out[...] = jnp.concatenate(
        [
            own64(gain1),
            own64(shift1),
            own64(gain2),
            own64(shift2),
            own256(gain3),
            own256(shift3),
            jnp.zeros((2, 256), F32),
        ],
        axis=0,
    )

    wide_take(0, eg_out)
    for r in range(3):
        s_take(r)
    wide_take(1, rg_out)

    wide_close(0)
    wide_close(1)
    for r in range(3):
        s_close(r)
    arrived(RES, o_send.at[1])
    for k, ref in enumerate((res_out, ig_out)):
        arrived(ref.at[pl.ds(theirs, BOTH)], o_recv.at[k])
    arrived(F.at[0], fx_send.at[0])
    arrived(C.at[0], fx_send.at[1])
    for k, ref in enumerate((W1T.at[pl.ds(0, 3)], W2T.at[pl.ds(0, 2)], W3, W2T.at[0], W3.at[pl.ds(0, 2)], pk.at[pl.ds(0, 3)], kb)):
        arrived(ref, w_send.at[k])
    for k, ref in enumerate((h1s.at[0], h2s, e2s, e1s, h1b, h1s.at[1])):
        arrived(ref, x_send.at[k])
    for k, kind, rows in (
        (0, "all", 4),
        (1, "all", 4),
        (2, "half", 8),
        (3, "half", 8),
        (4, "all", 4),
        (5, "all", 4),
        (6, "pix", 8),
    ):
        ar_close(k, kind, rows)


def block(n_pix, n_ch, *args):
    feat, cot, mask, w1, w2, w3 = args[:6]
    rows, lanes = feat.shape
    n_lo = 8
    n_hi = n_pix // n_lo
    chunks = rows // ROWS
    any_space = pl.BlockSpec(memory_space=pl.ANY)
    vmem = pl.BlockSpec(memory_space=pltpu.VMEM)
    V = pltpu.VMEM
    DMA = pltpu.SemaphoreType.DMA
    scratch = [
        V((rows,), jnp.int32),
        *[V((64,), BF16)] * 4,
        *[V((256,), BF16)] * 2,
        V((2, BOTH, ROWS, 256), BF16),
        V((2, BOTH, ROWS, 256), BF16),
        V((BOTH, ROWS, 128), F32),
        V((4, 64, 512), BF16),
        V((4, 9, 64, 256), BF16),
        V((4, 64, 512), BF16),
        V((4, 64, 512), BF16),
        V((4, 8, 256), F32),
        V((7, 8, 128), F32),
        V((7, n_pix * n_ch, 8, 128), F32),
        V((2, OWN, ROWS, 128), BF16),
        V((2, OWN, ROWS, 128), BF16),
        V((OWN, ROWS, 256), F32),
        V((OWN, ROWS, 256), BF16),
        V((OWN, ROWS, 256), BF16),
        V((OWN, ROWS, 256), F32),
        V((OWN * ROWS, 256), F32),
        V((FLAT + 2 * EDGE, 256), F32),
        V((FLAT + 2 * PAD, 768), BF16),
        V((3, FLAT, 256), BF16),
        V((FLAT, 256), F32),
        V((OWN * ROWS, 256), F32),
        V((OWN, ROWS, 256), BF16),
        V((OWN, ROWS, 256), BF16),
        V((BOTH, ROWS, 256), BF16),
        V((BOTH, ROWS, 256), F32),
        V((BOTH, ROWS, 256), BF16),
        V((BOTH, ROWS, 256), BF16),
        V((BOTH, ROWS, 512), F32),
        V((BOTH, ROWS, 512), F32),
        V((BOTH, ROWS, 256), BF16),
        V((BOTH, ROWS, 512), BF16),
        V((8, 512), F32),
        V((8, 512), F32),
        V((OWN, ROWS, 256), F32),
        V((OWN, ROWS, 256), BF16),
        V((OWN, ROWS, 256), BF16),
        V((OWN, ROWS, 256), F32),
        V((OWN, ROWS, 256), BF16),
        V((OWN, ROWS, 256), BF16),
        V((BOTH, ROWS, 256), BF16),
        V((256, FLAT), BF16),
        V((chunks, ROWS), F32),
        V((2, 2, 2, 64, 512), F32),
        V((2, 2, 64, 512), BF16),
        V((2, 2, 64, 512), BF16),
        V((2, 2, 4, 16, 512), F32),
        V((2, 4, 2, 16, 512), BF16),
        V((2, 4, 2, 16, 512), BF16),
        V((2, 2, 16, 512), BF16),
        V((2, 2, 16, 512), BF16),
        V((2, n_hi, 2, 16, 512), BF16),
        V((2, 2, 16, 512), BF16),
        V((2, 2, 4, 16, 512), BF16),
        V((3, 2, 2, 64, 768), F32),
        V((3, 2, 64, 768), BF16),
        V((3, 2, 64, 768), BF16),
        V((3, 2, 4, 16, 768), F32),
        V((3, 2, 2, 2, 16, 768), BF16),
        V((3, 2, 2, 2, 16, 768), BF16),
        V((2, 2, 2, 16, 768), F32),
        V((2, 2, 16, 768), BF16),
        V((3, 2, 16, 768), BF16),
        V((3, 3, 16, 768), BF16),
        V((3, n_hi, 16, 768), BF16),
        V((3, 4, 16, 768), BF16),
        DMA((13,)),
        DMA((2,)),
        DMA((3,)),
        DMA((7,)),
        DMA((19,)),
        DMA((7,)),
        DMA((7,)),
        DMA((6,)),
        DMA((19,)),
        DMA((2,)),
        DMA((2,)),
        DMA((2,)),
        DMA((2, 4)),
        DMA((3,)),
        DMA((3, 5)),
        DMA((5, n_hi) if n_hi > 1 else (1, 1)),
        DMA((5, n_hi) if n_hi > 1 else (1, 1)),
    ]
    wide = V((chunks, ROWS, lanes), BF16)
    made = pl.pallas_call(
        functools.partial(kernel, n_pix, n_ch),
        out_shape=(
            wide,
            wide,
            V((64, 1024), F32),
            V((9, 64, 256), F32),
            V((64, 1024), F32),
            V((8, 256), F32),
        ),
        in_specs=[any_space] * 12,
        out_specs=(vmem,) * 6,
        scratch_shapes=scratch,
        compiler_params=pltpu.CompilerParams(
            collective_id=0, has_side_effects=True, vmem_limit_bytes=56 * 2**20
        ),
        name="bottleneck",
    )(
        feat.reshape(chunks, ROWS, lanes),
        cot.reshape(chunks, ROWS, lanes),
        mask,
        w1.T,
        w2.transpose(0, 1, 3, 2).reshape(9, 64, 256),
        w3,
        *args[6:],
    )
    narrow = jax.ShapeDtypeStruct((64,), F32)
    broad = jax.ShapeDtypeStruct((256,), F32)
    return pl.pallas_call(
        finish,
        out_shape=tuple(jax.ShapeDtypeStruct(v.shape, v.dtype) for v in made[:5]) + (narrow,) * 4 + (broad,) * 2,
        in_specs=[any_space] * 5 + [vmem],
        out_specs=(any_space,) * 5 + (vmem,) * 6,
        scratch_shapes=[DMA((20,))],
        compiler_params=pltpu.CompilerParams(vmem_limit_bytes=2**20),
        name="outputs",
    )(*[pltpu.with_memory_space_constraint(v, pltpu.VMEM) for v in made])


def finish(*refs):
    made, stats, outs, small, sems = refs[:5], refs[5], refs[6:11], refs[11:17], refs[17]
    copies = []
    for a, b in zip(made, outs):
        parts = 4 if a.shape[0] % 4 == 0 else 3
        rows = a.shape[0] // parts
        for k in range(parts):
            at = pl.ds(k * rows, rows)
            copies.append(pltpu.make_async_copy(a.at[at], b.at[at], sems.at[len(copies)]))
    for cp in copies:
        cp.start()
    for i, out in enumerate(small):
        out[...] = stats[i : i + 1, 0 : out.shape[0]].reshape(out.shape)
    for cp in copies:
        cp.wait()


def solution(mesh):
    n_pix, n_ch = mesh.shape["pix"], mesh.shape["ch"]

    def body(feat, mask, w1, w2, w3, g1, b1, g2, b2, g3, b3, cot):
        made = block(n_pix, n_ch, feat, cot, mask, w1, w2, w3, g1, b1, g2, b2, g3, b3)
        res, ig, rg, sg, eg = made[:5]
        return (
            res.reshape(feat.shape),
            ig.reshape(feat.shape),
            rg.T,
            sg.reshape(3, 3, 64, 256).transpose(0, 1, 3, 2),
            eg,
        ) + tuple(made[5:])

    wide = P("pix", "ch")
    return jax.shard_map(
        body,
        mesh=mesh,
        in_specs=(wide, P("pix"), P(None, "ch"), P(None, None, None, "ch"), P("ch", None)) + (P("ch"),) * 6 + (wide,),
        out_specs=(wide, wide, P(None, "ch"), P(None, None, None, "ch"), P("ch", None)) + (P("ch"),) * 6,
        check_vma=False,
    )
```

time: 102 us -> 87.8 us (0.86)
  Pallas kernels: 101 us -> 87 us
    pallas_call x1, Pallas kernels: 98.5 us -> 84.2 us  [block(): pl.pallas_call(functools.partial(kernel, n_pix, n_ch), out_shape=(wide, w...]
where the time goes in v6:
time: 87.8 us; the launch traced here: 87.6 us
  Pallas kernels  87 us (99%)
    pallas_call x1, Pallas kernels, block(): pl.pallas_call(functools.partial(kernel, n_pix, n_ch), out_shape=(wide, w...  84.2 us
    pallas_call x1, Pallas kernels, block(): pl.pallas_call(finish, out_shape=tuple((jax.ShapeDtypeStruct(v.shape, v.d...  2.79 us

profile of v6, /device:TPU:0, one launch (start us, length us, event | category | flops | bytes accessed | tf_op | source)
XLA Modules:
  0.0 87.6 jit_solution(2008833759245099573)
XLA Ops:
  0.6 84.2 %bottleneck.1 = (bf16[28,112,256]{2,1,0:T(8,128)(2,1)S(1)}, bf16[28,112,256]{2,1,0:T(8,128)(2,1)S(1)}, f32[64,1024]{1,0:T(8,128)S(1)}, f32[9,64,256]{2,1,0:T(8,1...) custom-call(bf16[28,112,256]{2,1,0:T(8,128)(2,1)} %bitcast.12, bf16[28,112,256]{2,1,0:T(8,128)(2,1)} %bitcast.13, ...), custom_call_target="tpu_custom_call" | custom-call | tf_op jit(solution)/shard_map/bottleneck/pallas_call | solution.py:1141
  84.8 2.8 %outputs.1 = (bf16[28,112,256]{2,1,0:T(8,128)(2,1)}, bf16[28,112,256]{2,1,0:T(8,128)(2,1)}, f32[64,1024]{1,0:T(8,128)}, f32[9,64,256]{2,1,0:T(8,128)}, f32[64,10...) custom-call(bf16[28,112,256]{2,1,0:T(8,128)(2,1)S(1)} %get-tuple-ele, ...), custom_call_target="tpu_custom_call" | custom-call | tf_op jit(solution)/shard_map/outputs/pallas_call | solution.py:1169

commit v7 on v6

--- a/solution.py
+++ b/solution.py
@@ -208,12 +208,25 @@
 
     barrier = pltpu.get_barrier_semaphore()
 
+    few = n_pix <= 8
+    pix_at = [me_p] + [lax.rem(me_p + i, n_pix) for i in range(1, n_pix)] if few else []
+    ch_at = [me_c] + [lax.rem(me_c + i, n_ch) for i in range(1, n_ch)]
+    place_beside = hi * 2 + 1 - lo
+
+    def everybody(kind):
+        places = {"all": ch_at, "half": [me_c, place_beside], "pix": [me_c]}[kind]
+        return [(p, c) for i, p in enumerate(pix_at) for j, c in enumerate(places) if i + j > 0]
+
     def greet(t, carry):
         q = lax.rem(me_p * n_ch + me_c + t, n_all)
         pl.semaphore_signal(barrier, inc=1, device_id=(q // n_ch, lax.rem(q, n_ch)), device_id_type=MESH)
         return carry
 
-    lax.fori_loop(1, n_all, greet, 0)
+    if few:
+        for device in everybody("all"):
+            pl.semaphore_signal(barrier, inc=1, device_id=device, device_id_type=MESH)
+    else:
+        lax.fori_loop(1, n_all, greet, 0)
     for cp in small_load:
         cp.start()
     w1_load.start()
@@ -275,15 +288,23 @@
         remote(columns(w3_in, 1 - hi), W3X.at[me_c], w_send.at[2], w_recv.at[16], beside),
         remote(W3X.at[far], W3X.at[far], w_send.at[2], w_recv.at[17], beside),
     ]
-    shared, shared_y = [], []
-    for t in range(1, n_lo):
-        to = (g_hi * n_lo + lax.rem(g_lo + t, n_lo), me_c)
-        for spot, sent, got, group in (
-            (w2_piece(W2T.at[far], g_lo), 3, 7, shared),
-            (w3_piece(W3.at[far], g_lo, 0), 4, 11, shared),
-            (w3_piece(W3X.at[far], g_lo, 0), 4, 15, shared_y),
-        ):
-            group.append(remote(spot, spot, w_send.at[sent], w_recv.at[got], to))
+    flip = (1 - top) * 4 + quad
+    to_flip, to_four = (g_hi * n_lo + flip, me_c), []
+    for t in range(1, 4):
+        to_four.append((g_hi * n_lo + top * 4 + lax.rem(quad + t, 4), me_c))
+
+    def pass_pieces(piece_of, sent, got):
+        one = [remote(piece_of(g_lo), piece_of(g_lo), w_send.at[sent], w_recv.at[got], to_flip)]
+        two = [
+            remote(piece_of(q), piece_of(q), w_send.at[sent], w_recv.at[18 + got // 4], to)
+            for to in to_four
+            for q in (g_lo, flip)
+        ]
+        return one, two
+
+    w2_flip, w2_four = pass_pieces(lambda q: w2_piece(W2T.at[far], q), 3, 7)
+    w3_flip, w3_four = pass_pieces(lambda q: w3_piece(W3.at[far], q, 0), 4, 11)
+    w3y_flip, w3y_four = pass_pieces(lambda q: w3_piece(W3X.at[far], q, 0), 4, 15)
     w1x[0].start()
     w1x[1].start()
     fx[1].start()
@@ -316,13 +337,20 @@
         sbuf[k, 0:rows] = val
         rbuf[k, me, 0:rows] = val
 
-        def send(t, carry):
-            to = device(lax.rem(me + t, n))
-            cut = pl.ds(0, rows)
+        cut = pl.ds(0, rows)
+
+        def send(to):
             remote(sbuf.at[k, cut], rbuf.at[k, me, cut], ar_send.at[k], ar_recv.at[k], to).start()
+
+        def send_next(t, carry):
+            send(device(lax.rem(me + t, n)))
             return carry
 
-        lax.fori_loop(1, n, send, 0)
+        if few:
+            for to in everybody(kind):
+                send(to)
+        else:
+            lax.fori_loop(1, n, send_next, 0)
 
     def ar_finish(k, kind, rows):
         n = ar_group(kind)[0]
@@ -380,7 +408,7 @@
     w1x[2].start()
     arrived(w3_piece(W3.at[far], g_lo, 0), w_recv.at[10])
     arrived(w2_piece(W2T.at[far], g_lo), w_recv.at[6])
-    for cp in shared:
+    for cp in w2_flip + w3_flip:
         cp.start()
 
     flat = mask_v[...].astype(F32).reshape(1, rows28.shape[0] * ROWS)
@@ -409,6 +437,10 @@
         return carry
 
     lax.fori_loop(0, OWN, keep_first, 0)
+    arrived(w2_piece(W2T.at[far], flip), w_recv.at[7])
+    arrived(w3_piece(W3.at[far], flip, 0), w_recv.at[11])
+    for cp in w2_four + w3_four:
+        cp.start()
 
     def put_mask(t, carry):
         at = mine + jnp.where(t < OWN, part0 + t, part1 + t - OWN)
@@ -438,8 +470,8 @@
     arrived(pk.at[far], w_recv.at[4])
     pkx[2].start()
     arrived(W3.at[pl.ds(0, 2)], ld_sem.at[5])
-    arrived(G3.at[pl.ds(0, 9), :, pl.ds(0, 128)], w_recv.at[7])
-    arrived(A2.at[0], w_recv.at[11])
+    arrived(G3.at[pl.ds(0, 9), pl.ds(0, 96), pl.ds(0, 128)], w_recv.at[19])
+    arrived(A2.at[0, pl.ds(0, 96)], w_recv.at[20])
     w2x[2].start()
     w3x[2].start()
     arrived(pk.at[pl.ds(0, 2)], w_recv.at[5])
@@ -528,14 +560,16 @@
     s, q = carry
     ar_start(1, pack2(fold1(s), fold1(q)), "all")
     start_all(1, h2s, h2r, early, OWN)
+    arrived(w3_piece(W3X.at[far], g_lo, 0), w_recv.at[14])
+    w3y_flip[0].start()
     s, q = unpack2(ar_finish(1, "all", 4))
     avg2 = s * inv_n2
     scale2 = lax.rsqrt(q * inv_n2 - avg2 * avg2 + EPS)
     a2_gain = g2 * scale2
     a2_shift = b2 - avg2 * a2_gain
 
-    arrived(w3_piece(W3X.at[far], g_lo, 0), w_recv.at[14])
-    for cp in shared_y:
+    arrived(w3_piece(W3X.at[far], flip, 0), w_recv.at[15])
+    for cp in w3y_four:
         cp.start()
     w3y[1].start()
     arrived(W3.at[near], w_recv.at[12])
@@ -579,7 +613,7 @@
     cross_d = mm_tn(half_of(A2, 0), half_of(D2b, 0)) + mm_tn(half_of(A2, 1), half_of(D2b, 1))
     cross_h = mm_tn(half_of(A2, 0), half_of(D2h, 0)) + mm_tn(half_of(A2, 1), half_of(D2h, 1))
     slopes, far_slopes = fold1(slopes), fold1(far_slopes)
-    arrived(A2.at[0], w_recv.at[15])
+    arrived(A2.at[0, pl.ds(0, 96)], w_recv.at[21])
     w3y[2].start()
 
     s, q = unpack3(ar_finish(2, "half", 8))
@@ -635,7 +669,7 @@
     s, q = lax.fori_loop(0, OWN, last, sums)
     ar_start(3, pack3(fold1(s), fold1(q * scale3)), "half")
     prods = lax.fori_loop(3, OWN, other_product, prods)
-    start_all(2, e2s, e2r, 3, 4)
+    start_all(2, e2s, e2r, 3, 5)
     prods = lax.fori_loop(0, OWN, own_product, prods)
     def beside_out(ref, k):
         return [
@@ -663,7 +697,6 @@
     kb[...] = jnp.concatenate([k3_h, k3_0, jnp.zeros((6, 512), F32)], axis=0)
     kx = remote(kb, kr, w_send.at[6], w_recv.at[18], across)
     kx.start()
-    start_all(2, e2s, e2r, 4, 5)
     square, line = corrections(k3_h, k3_0, W3)
     s = fold1(prods[0]) + fold1(square * cross_d) + line * slopes
     q = fold1(prods[1]) + fold1(square * cross_h) + line * far_slopes
@@ -834,7 +867,7 @@
             s1[r, h] = both
             for q in range(4):
                 sb[r, q % 2, q // 2, h] = both[q].astype(BF16)
-        for cp in s_four(r) if r == 2 else [s_low(r)]:
+        for cp in s_four(r) if r in (0, 1, 2) else [s_low(r)]:
             cp.start()
 
     def s_low_add(r):
@@ -845,7 +878,7 @@
         s_high(r).start()
 
     def s_four_add(r):
-        if r == 2:
+        if r in (0, 1, 2):
             arrived(PC.at[pl.ds(0, 96)], s_recv.at[r, 1])
             total = s1[r, :, quad]
             for t in range(1, 4):
@@ -960,11 +993,9 @@
     lax.fori_loop(0, OWN, own_back_first, 0)
     own_reduce = mm_tn(half_of(G1, 0), features_of(0))
     acc_w[1] = own_reduce.reshape(2, 2, 64, 512)
-    s_low_add(0)
     swap_add(0)
     lax.fori_loop(0, OWN, input_term, 0)
     ig_there[0].start()
-    s_low_add(1)
     for cp in h1x:
         cp.wait_recv()
 
@@ -1123,7 +1154,7 @@
         DMA((2,)),
         DMA((3,)),
         DMA((7,)),
-        DMA((19,)),
+        DMA((22,)),
         DMA((7,)),
         DMA((7,)),
         DMA((6,)),

time: 87.8 us -> 86.6 us (0.986)
  Pallas kernels: 87 us -> 85.8 us
    pallas_call x1, Pallas kernels: 84.2 us -> 83 us  [block(): pl.pallas_call(functools.partial(kernel, n_pix, n_ch), out_shape=(wide, w...]
where the time goes in v7:
time: 86.6 us; the launch traced here: 86.4 us
  Pallas kernels  85.8 us (99%)
    pallas_call x1, Pallas kernels, block(): pl.pallas_call(functools.partial(kernel, n_pix, n_ch), out_shape=(wide, w...  83 us
    pallas_call x1, Pallas kernels, block(): pl.pallas_call(finish, out_shape=tuple((jax.ShapeDtypeStruct(v.shape, v.d...  2.79 us

profile of v7, /device:TPU:0, one launch (start us, length us, event | category | flops | bytes accessed | tf_op | source)
XLA Modules:
  0.0 86.4 jit_solution(3773789721341270865)
XLA Ops:
  0.6 83.0 %bottleneck.1 = (bf16[28,112,256]{2,1,0:T(8,128)(2,1)S(1)}, bf16[28,112,256]{2,1,0:T(8,128)(2,1)S(1)}, f32[64,1024]{1,0:T(8,128)S(1)}, f32[9,64,256]{2,1,0:T(8,1...) custom-call(bf16[28,112,256]{2,1,0:T(8,128)(2,1)} %bitcast.12, bf16[28,112,256]{2,1,0:T(8,128)(2,1)} %bitcast.13, ...), custom_call_target="tpu_custom_call" | custom-call | tf_op jit(solution)/shard_map/bottleneck/pallas_call | solution.py:1172
  83.7 2.8 %outputs.1 = (bf16[28,112,256]{2,1,0:T(8,128)(2,1)}, bf16[28,112,256]{2,1,0:T(8,128)(2,1)}, f32[64,1024]{1,0:T(8,128)}, f32[9,64,256]{2,1,0:T(8,128)}, f32[64,10...) custom-call(bf16[28,112,256]{2,1,0:T(8,128)(2,1)S(1)} %get-tuple-ele, ...), custom_call_target="tpu_custom_call" | custom-call | tf_op jit(solution)/shard_map/outputs/pallas_call | solution.py:1200

commit v8 on v7

--- a/solution.py
+++ b/solution.py
@@ -35,8 +35,11 @@
     return lax.dot_general(a, b, (((0,), (0,)), ((), ())), preferred_element_type=F32)
 
 
-def logistic(v):
-    return 0.5 * jnp.tanh(0.5 * v) + 0.5
+def silu_and_slope(half):
+    t = jnp.tanh(half)
+    up = 1.0 + t
+    out = half * up
+    return out, up + out * (1.0 - t)
 
 
 def fold8(v):
@@ -89,6 +92,7 @@
     pk,
     sbuf,
     rbuf,
+    pbuf,
     h1s,
     h1r,
     H1,
@@ -152,6 +156,8 @@
     w_recv,
     ar_send,
     ar_recv,
+    pair_send,
+    pair_recv,
     x_send,
     x_recv,
     o_send,
@@ -214,7 +220,7 @@
     place_beside = hi * 2 + 1 - lo
 
     def everybody(kind):
-        places = {"all": ch_at, "half": [me_c, place_beside], "pix": [me_c]}[kind]
+        places = {"all": ch_at, "half": [me_c, place_beside], "pix": [me_c], "core": [me_c, (1 - hi) * 2 + lo]}[kind]
         return [(p, c) for i, p in enumerate(pix_at) for j, c in enumerate(places) if i + j > 0]
 
     def greet(t, carry):
@@ -329,6 +335,8 @@
             return n_all, me_p * n_ch + me_c, lambda q: (q // n_ch, lax.rem(q, n_ch))
         if kind == "half":
             return n_pix * 2, me_p * 2 + lo, lambda q: (q // 2, hi * 2 + lax.rem(q, 2))
+        if kind == "core":
+            return n_pix * 2, me_p * 2 + hi, lambda q: (q // 2, lax.rem(q, 2) * 2 + lo)
         return n_pix, me_p, lambda q: (q, me_c)
 
     def ar_start(k, val, kind):
@@ -352,6 +360,13 @@
         else:
             lax.fori_loop(1, n, send_next, 0)
 
+    def pair_first(k, val):
+        pbuf[k, 0] = val
+        swap = remote(pbuf.at[k, 0], pbuf.at[k, 1], pair_send.at[k], pair_recv.at[k], beside)
+        swap.start()
+        swap.wait()
+        return pbuf[k, 0] + pbuf[k, 1]
+
     def ar_finish(k, kind, rows):
         n = ar_group(kind)[0]
         arrived(rbuf.at[k, pl.ds(0, n - 1), pl.ds(0, rows)], ar_recv.at[k])
@@ -390,7 +405,14 @@
         return jnp.concatenate([F[0, t], F[1, t]], axis=1)
 
     def xcopy(kind, src, dst, t):
-        got = (0, 8 + t, 15 + jnp.where(t < 2, 0, 1), 17, None, 1 + t)[kind]
+        got = (
+            0,
+            3 + jnp.where(t < 3, 0, jnp.where(t < 5, 1, 2)),
+            6 + jnp.where(t < 2, 0, 1),
+            8 + jnp.where(t < 4, 0, 1),
+            None,
+            1 + jnp.where(t < 5, 0, 1),
+        )[kind]
         return remote(src.at[t], dst.at[t], x_send.at[kind], x_recv.at[got], across)
 
     def send_first(h, kind):
@@ -457,7 +479,6 @@
 
     def sum_first(t, carry):
         s, q = carry
-        xcopy(5, h1s.at[0], h1r.at[0], t).wait_recv()
         h = H1[t] + jnp.concatenate([h1r[0, t], h1r[1, t]], axis=1).astype(F32)
         H1[t] = h
         h1b[t] = h.astype(BF16)
@@ -465,7 +486,10 @@
         return s + fold8(vh), q + fold8(vh * h)
 
     arrived(h1r.at[0], x_recv.at[0])
-    s, q = lax.fori_loop(0, OWN, sum_first, (zero, zero))
+    arrived(h1r.at[0, pl.ds(0, 5)], x_recv.at[1])
+    carry = lax.fori_loop(0, 5, sum_first, (zero, zero))
+    arrived(h1r.at[0, pl.ds(5, OWN - 5)], x_recv.at[2])
+    s, q = lax.fori_loop(5, OWN, sum_first, carry)
     ar_start(0, pack2(fold1(s), fold1(q)), "all")
     arrived(pk.at[far], w_recv.at[4])
     pkx[2].start()
@@ -491,11 +515,9 @@
 
     def act_first(t, carry):
         v = spread(V[t], 256)
-        aff = v * (H1[t] * a1_gain + a1_shift)
-        sig = logistic(aff)
-        act = aff * sig
+        act, slope = silu_and_slope(v * (H1[t] * (0.5 * a1_gain) + 0.5 * a1_shift))
         comp[pl.ds(pl.multiple_of(t * ROWS, 16), ROWS), :] = act
-        D1[t] = v * (sig + act * (1.0 - sig))
+        D1[t] = spread(0.5 * V[t], 256) * slope
         return carry
 
     def to_padded(images):
@@ -521,7 +543,7 @@
 
     arrived(W2T.at[near], w_recv.at[8])
     arrived(W2T.at[last_one], w_recv.at[9])
-    h1x = [remote(h1b, h1o, x_send.at[4], x_recv.at[18], across)]
+    h1x = [remote(h1b, h1o, x_send.at[4], x_recv.at[10], across)]
 
     def conv(first, rows):
         taps = [PC[PAD * r + first : PAD * r + first + rows, :] for r in range(3)]
@@ -558,11 +580,11 @@
             columns_forward((1, 2, 3))
         done = now
     s, q = carry
-    ar_start(1, pack2(fold1(s), fold1(q)), "all")
+    ar_start(1, pair_first(0, pack2(fold1(s), fold1(q))), "core")
     start_all(1, h2s, h2r, early, OWN)
     arrived(w3_piece(W3X.at[far], g_lo, 0), w_recv.at[14])
     w3y_flip[0].start()
-    s, q = unpack2(ar_finish(1, "all", 4))
+    s, q = unpack2(ar_finish(1, "core", 4))
     avg2 = s * inv_n2
     scale2 = lax.rsqrt(q * inv_n2 - avg2 * avg2 + EPS)
     a2_gain = g2 * scale2
@@ -578,10 +600,8 @@
     def act_second(t, h, carry):
         s, q, d, e = carry
         v = spread(V[t], 256)
-        aff = v * (h * a2_gain + a2_shift)
-        sig = logistic(aff)
-        act = aff * sig
-        slope = v * (sig + act * (1.0 - sig))
+        act, slope = silu_and_slope(v * (h * (0.5 * a2_gain) + 0.5 * a2_shift))
+        slope = spread(0.5 * V[t], 256) * slope
         far_slope = slope * (h - avg2)
         D2[t] = slope
         D2b[t] = slope.astype(BF16)
@@ -596,14 +616,16 @@
         return act_second(t, H2[pl.ds(pl.multiple_of(t * ROWS, 16), ROWS), :], carry)
 
     def other_second(t, carry):
-        xcopy(1, h2s, h2r, t).wait_recv()
         return act_second(t + OWN, h2r[t].astype(F32), carry)
 
     wide_zero = jnp.zeros((8, 512), F32)
     carry = lax.fori_loop(0, OWN, own_second, (wide_zero, wide_zero, zero, zero))
     for cp in h1x:
         cp.start()
-    s, q, slopes, far_slopes = lax.fori_loop(0, OWN, other_second, carry)
+    for k, (first, last) in enumerate(((0, 3), (3, 5), (5, OWN))):
+        arrived(h2r.at[pl.ds(first, last - first)], x_recv.at[3 + k])
+        carry = lax.fori_loop(first, last, other_second, carry)
+    s, q, slopes, far_slopes = carry
     ar_start(2, pack3(fold1(s), fold1(q)), "half")
     arrived(C.at[lo], ld_sem.at[4])
     arrived(C.at[1 - lo], fx_recv.at[2])
@@ -621,6 +643,7 @@
     scale3 = lax.rsqrt(q * inv_n - avg3 * avg3 + EPS)
     a3_gain = g3 * scale3
     a3_shift = b3 - avg3 * a3_gain
+    half_gain, half_shift = 0.5 * a3_gain, 0.5 * a3_shift
 
     def put_out(ref, t, out):
         first, second = out[:, 0:256].astype(BF16), out[:, 256:512].astype(BF16)
@@ -632,19 +655,16 @@
         v = spread(V[t], 512)
         h3 = H3[t]
         wide = jnp.concatenate([F[0, t], F[1, t]], axis=1).astype(F32)
-        total = v * (h3 * a3_gain + a3_shift) + wide
-        sig = logistic(total)
-        out = total * sig
+        out, slope = silu_and_slope(v * (h3 * half_gain + half_shift) + 0.5 * wide)
         put_out(res_out, t, out)
         given = jnp.concatenate([C[0, t], C[1, t]], axis=1).astype(F32)
-        gs = given * (sig + out * (1.0 - sig))
+        gs = given * slope
         GS[t] = gs
-        vg = v * gs
-        return s + fold8(vg), q + fold8(vg * (h3 - avg3))
+        return s + fold8(v * gs), q + fold8(gs * h3)
 
     def product(t, h, carry):
         s, q = carry
-        given = (spread(V[t], 512) * (a3_gain * GS[t])).astype(BF16)
+        given = (spread(V[t], 512) * (half_gain * GS[t])).astype(BF16)
         e = mm_nt(given, W3[...].reshape(256, 512)) * D2[t]
         return e, (s + fold8(e), q + fold8(e * (h - avg2)))
 
@@ -667,7 +687,8 @@
     sums, prods = lax.fori_loop(0, 3, last_and_product, ((wide_zero, wide_zero), (zero, zero)))
     sums = lax.fori_loop(OWN + 3, BOTH, last, sums)
     s, q = lax.fori_loop(0, OWN, last, sums)
-    ar_start(3, pack3(fold1(s), fold1(q * scale3)), "half")
+    s, q = 0.5 * fold1(s), 0.5 * fold1(q)
+    ar_start(3, pack3(s, (q - avg3 * s) * scale3), "half")
     prods = lax.fori_loop(3, OWN, other_product, prods)
     start_all(2, e2s, e2r, 3, 5)
     prods = lax.fori_loop(0, OWN, own_product, prods)
@@ -707,7 +728,7 @@
 
     def back_third(t, carry):
         v = spread(V[t], 512)
-        G3[t] = (v * (a3_gain * GS[t] + k3_h * H3[t] + k3_0)).astype(BF16)
+        G3[t] = (v * (half_gain * GS[t] + k3_h * H3[t] + k3_0)).astype(BF16)
         return carry
 
     lax.fori_loop(0, BOTH, back_third, 0)
@@ -929,7 +950,7 @@
         weights = [W2T[:, k].reshape(256, 256) for k in range(9)]
         padded[first : first + rows, :] = mm(jnp.concatenate(taps, axis=1), jnp.concatenate(weights, axis=0))
 
-    arrived(e2r.at[pl.ds(0, 2)], x_recv.at[15])
+    arrived(e2r.at[pl.ds(0, 2)], x_recv.at[6])
     lax.fori_loop(0, 2, back_second, 0)
     to_padded((0,))
     columns_back((0,))
@@ -953,7 +974,7 @@
         carry = lax.fori_loop(done, now, sum_back_first, carry)
         start_all(3, e1s, e1r, min(done, early), min(now, early))
         if done == 0:
-            arrived(e2r.at[pl.ds(2, OWN - 2)], x_recv.at[16])
+            arrived(e2r.at[pl.ds(2, OWN - 2)], x_recv.at[7])
             lax.fori_loop(2, OWN, back_second, 0)
             to_padded((1, 2, 3))
             columns_back((1, 2, 3))
@@ -977,7 +998,7 @@
         G1[t] = (spread(V[t], 256) * (a1_gain * e + k1_h * h + k1_0)).astype(BF16)
 
     def input_term(t, carry):
-        out = mm(G1[t], W1T[...].reshape(256, 512)) + GS[t]
+        out = mm(G1[t], W1T[...].reshape(256, 512)) + 0.5 * GS[t]
         put_out(ig_out, t, out)
         return carry
 
@@ -987,12 +1008,12 @@
         back_first(t, E1[t], H1[t])
         return carry
 
-    def features_of(part):
-        return jnp.concatenate([half_of(F.at[0], part), half_of(F.at[1], part)], axis=1)
+    def reduce_rows(first, chunks):
+        parts = [v[first : first + chunks].reshape(chunks * ROWS, 256) for v in (G1, F.at[0], F.at[1])]
+        return mm_tn(parts[0], jnp.concatenate(parts[1:], axis=1)).reshape(2, 2, 64, 512)
 
     lax.fori_loop(0, OWN, own_back_first, 0)
-    own_reduce = mm_tn(half_of(G1, 0), features_of(0))
-    acc_w[1] = own_reduce.reshape(2, 2, 64, 512)
+    acc_w[1] = reduce_rows(0, OWN)
     swap_add(0)
     lax.fori_loop(0, OWN, input_term, 0)
     ig_there[0].start()
@@ -1003,9 +1024,10 @@
         back_first(t + OWN, e1r[t].astype(F32), h1o[t].astype(F32))
         return carry
 
-    arrived(e1r, x_recv.at[17])
+    arrived(e1r.at[pl.ds(0, 4)], x_recv.at[8])
+    arrived(e1r.at[pl.ds(4, OWN - 4)], x_recv.at[9])
     lax.fori_loop(0, OWN, other_back_first, 0)
-    acc_w[1] += mm_tn(half_of(G1, 1), features_of(1)).reshape(2, 2, 64, 512)
+    acc_w[1] += reduce_rows(OWN, OWN)
     pair_start(1)
     s_four_add(0)
     lax.fori_loop(OWN, BOTH, input_term, 0)
@@ -1060,7 +1082,7 @@
         arrived(ref, x_send.at[k])
     for k, kind, rows in (
         (0, "all", 4),
-        (1, "all", 4),
+        (1, "core", 4),
         (2, "half", 8),
         (3, "half", 8),
         (4, "all", 4),
@@ -1094,6 +1116,7 @@
         V((4, 8, 256), F32),
         V((7, 8, 128), F32),
         V((7, n_pix * n_ch, 8, 128), F32),
+        V((2, 2, 4, 128), F32),
         V((2, OWN, ROWS, 128), BF16),
         V((2, OWN, ROWS, 128), BF16),
         V((OWN, ROWS, 256), F32),
@@ -1157,8 +1180,10 @@
         DMA((22,)),
         DMA((7,)),
         DMA((7,)),
+        DMA((2,)),
+        DMA((2,)),
         DMA((6,)),
-        DMA((19,)),
+        DMA((11,)),
         DMA((2,)),
         DMA((2,)),
         DMA((2,)),
@@ -1200,27 +1225,26 @@
     return pl.pallas_call(
         finish,
         out_shape=tuple(jax.ShapeDtypeStruct(v.shape, v.dtype) for v in made[:5]) + (narrow,) * 4 + (broad,) * 2,
-        in_specs=[any_space] * 5 + [vmem],
-        out_specs=(any_space,) * 5 + (vmem,) * 6,
-        scratch_shapes=[DMA((20,))],
+        in_specs=[any_space] * 6,
+        out_specs=(any_space,) * 11,
+        scratch_shapes=[V((8, 256), F32)] + [V(v.shape, F32) for v in (narrow,) * 4 + (broad,) * 2] + [DMA((12,))],
         compiler_params=pltpu.CompilerParams(vmem_limit_bytes=2**20),
         name="outputs",
     )(*[pltpu.with_memory_space_constraint(v, pltpu.VMEM) for v in made])
 
 
 def finish(*refs):
-    made, stats, outs, small, sems = refs[:5], refs[5], refs[6:11], refs[11:17], refs[17]
-    copies = []
-    for a, b in zip(made, outs):
-        parts = 4 if a.shape[0] % 4 == 0 else 3
-        rows = a.shape[0] // parts
-        for k in range(parts):
-            at = pl.ds(k * rows, rows)
-            copies.append(pltpu.make_async_copy(a.at[at], b.at[at], sems.at[len(copies)]))
+    made, outs, stats, small, sems = refs[:6], refs[6:17], refs[17], refs[18:24], refs[24]
+    copies = [pltpu.make_async_copy(a, b, sems.at[i]) for i, (a, b) in enumerate(zip(made[:5], outs[:5]))]
+    got = pltpu.make_async_copy(made[5], stats, sems.at[5])
+    got.start()
     for cp in copies:
         cp.start()
-    for i, out in enumerate(small):
-        out[...] = stats[i : i + 1, 0 : out.shape[0]].reshape(out.shape)
+    got.wait()
+    for i, (one, out) in enumerate(zip(small, outs[5:])):
+        one[...] = stats[i : i + 1, 0 : one.shape[0]].reshape(one.shape)
+        copies.append(pltpu.make_async_copy(one, out, sems.at[6 + i]))
+        copies[-1].start()
     for cp in copies:
         cp.wait()
 

time: 86.6 us -> 85.7 us (0.990)
  Pallas kernels: 85.8 us -> 84.9 us
where the time goes in v8:
time: 85.7 us; the launch traced here: 85.5 us
  Pallas kernels  84.9 us (99%)
    pallas_call x1, Pallas kernels, block(): pl.pallas_call(functools.partial(kernel, n_pix, n_ch), out_shape=(wide, w...  82.7 us
    pallas_call x1, Pallas kernels, block(): pl.pallas_call(finish, out_shape=tuple((jax.ShapeDtypeStruct(v.shape, v.d...  2.17 us

profile of v8, /device:TPU:0, one launch (start us, length us, event | category | flops | bytes accessed | tf_op | source)
XLA Modules:
  0.0 85.5 jit_solution(4484043346325128405)
XLA Ops:
  0.6 82.7 %bottleneck.1 = (bf16[28,112,256]{2,1,0:T(8,128)(2,1)S(1)}, bf16[28,112,256]{2,1,0:T(8,128)(2,1)S(1)}, f32[64,1024]{1,0:T(8,128)S(1)}, f32[9,64,256]{2,1,0:T(8,1...) custom-call(bf16[28,112,256]{2,1,0:T(8,128)(2,1)} %bitcast.12, bf16[28,112,256]{2,1,0:T(8,128)(2,1)} %bitcast.13, ...), custom_call_target="tpu_custom_call" | custom-call | tf_op jit(solution)/shard_map/bottleneck/pallas_call | solution.py:1197
  83.4 2.2 %outputs.1 = (bf16[28,112,256]{2,1,0:T(8,128)(2,1)}, bf16[28,112,256]{2,1,0:T(8,128)(2,1)}, f32[64,1024]{1,0:T(8,128)}, f32[9,64,256]{2,1,0:T(8,128)}, f32[64,10...) custom-call(bf16[28,112,256]{2,1,0:T(8,128)(2,1)S(1)} %get-tuple-ele, ...), custom_call_target="tpu_custom_call" | custom-call | tf_op jit(solution)/shard_map/outputs/pallas_call | solution.py:1225

commit v9 on v8

--- a/solution.py
+++ b/solution.py
@@ -754,69 +754,88 @@
             total = total + level[t].astype(F32)
         return total
 
+    def lanes_of(k):
+        return pl.ds(0, 512 if k == 0 else 256)
+
     def pair_copies(k):
-        return [remote(wp.at[k, h], wc.at[k, h], g_send.at[k], g_recv.at[k, 0], beside) for h in range(2)]
+        at = lanes_of(k)
+        return [remote(wp.at[k, h, :, at], wc.at[k, h, :, at], g_send.at[k], g_recv.at[k, 0], beside) for h in range(2)]
 
     def four_copies(k):
         return [
-            remote(wb.at[k, lax.rem(quad + t, 4)], wr.at[k, quad], g_send.at[k], g_recv.at[k, 1], group_at(t))
+            remote(
+                wb.at[k, lax.rem(quad + t, 4), :, :, lanes_of(k)],
+                wr.at[k, quad, :, :, lanes_of(k)],
+                g_send.at[k],
+                g_recv.at[k, 1],
+                group_at(t),
+            )
             for t in range(1, 4)
         ]
 
     def swap_copy(k):
-        return remote(wq.at[k], wu.at[k], g_send.at[k], g_recv.at[k, 2], group_at(0, True))
+        at = lanes_of(k)
+        return remote(wq.at[k, :, :, at], wu.at[k, :, :, at], g_send.at[k], g_recv.at[k, 2], group_at(0, True))
 
     def give_copies(k):
-        spot = wfin.at[k, hi, quad]
+        at = lanes_of(k)
+        spot = wfin.at[k, hi, quad, :, at]
         copies = []
         for t in range(4):
             group, place = group_at(t)
             if t > 0:
-                copies.append(remote(wf.at[k, hi], spot, g_send.at[k], g_recv.at[k, 3], (group, place)))
+                copies.append(remote(wf.at[k, hi, :, at], spot, g_send.at[k], g_recv.at[k, 3], (group, place)))
             copies.append(
-                remote(wf.at[k, 1 - hi], spot, g_send.at[k], g_recv.at[k, 3], (group, (1 - hi) * 2 + lo))
+                remote(wf.at[k, 1 - hi, :, at], spot, g_send.at[k], g_recv.at[k, 3], (group, (1 - hi) * 2 + lo))
             )
         return copies
 
     def pair_start(k):
+        width = 512 if k == 0 else 256
         for h in range(2):
-            wp[k, h] = acc_w[k, h, 1 - lo].astype(BF16)
+            wp[k, h, :, 0:width] = acc_w[k, h, 1 - lo, :, 0:width].astype(BF16)
         for cp in pair_copies(k):
             cp.start()
 
     def pair_add(k):
-        arrived(wc.at[k], g_recv.at[k, 0])
+        width = 512 if k == 0 else 256
+        arrived(wc.at[k, :, :, lanes_of(k)], g_recv.at[k, 0])
         for h in range(2):
-            both = (acc_w[k, h, lo] + wc[k, h].astype(F32)).reshape(4, 16, 512)
-            wa[k, h] = both
+            both = acc_w[k, h, lo, :, 0:width] + wc[k, h, :, 0:width].astype(F32)
+            both = both.reshape(4, 16, width)
+            wa[k, h, :, :, 0:width] = both
             for q in range(4):
-                wb[k, q, h] = both[q].astype(BF16)
+                wb[k, q, h, :, 0:width] = both[q].astype(BF16)
         for cp in four_copies(k):
             cp.start()
 
     def four_add(k):
-        arrived(wr.at[k, pl.ds(0, 3)], g_recv.at[k, 1])
-        total = wa[k, :, quad]
+        width = 512 if k == 0 else 256
+        arrived(wr.at[k, pl.ds(0, 3), :, :, lanes_of(k)], g_recv.at[k, 1])
+        total = wa[k, :, quad, :, 0:width]
         for t in range(1, 4):
-            total = total + wr[k, lax.rem(quad + t, 4)].astype(F32)
-        wq[k] = total.astype(BF16)
+            total = total + wr[k, lax.rem(quad + t, 4), :, :, 0:width].astype(F32)
+        wq[k, :, :, 0:width] = total.astype(BF16)
         swap_copy(k).start()
 
     def swap_add(k):
-        arrived(wu.at[k], g_recv.at[k, 2])
-        total = over_groups(wq[k].astype(F32) + wu[k].astype(F32), wh.at[k], (h_send.at[k], h_recv.at[k]))
-        wf[k] = total.astype(BF16)
-        wfin[k, hi, quad] = wf[k, hi]
+        width = 512 if k == 0 else 256
+        arrived(wu.at[k, :, :, lanes_of(k)], g_recv.at[k, 2])
+        total = wq[k, :, :, 0:width].astype(F32) + wu[k, :, :, 0:width].astype(F32)
+        total = over_groups(total, wh.at[k, :, :, :, lanes_of(k)], (h_send.at[k], h_recv.at[k])).astype(BF16)
+        wf[k, :, :, 0:width] = total
+        wfin[k, hi, quad, :, 0:width] = wf[k, hi, :, 0:width]
         for cp in give_copies(k):
             cp.start()
 
     def wide_take(k, out):
-        arrived(A2.at[pl.ds(0, 2)], g_recv.at[k, 3])
+        arrived(A2.at[pl.ds(0, 2)] if k == 0 else A2.at[0], g_recv.at[k, 3])
+        width, first = (512, 0) if k == 0 else (256, 256 * (k - 1))
         for h in range(2):
-            out[:, 512 * h : 512 * (h + 1)] = wfin[k, h].astype(F32).reshape(64, 512)
+            out[:, 512 * h + first : 512 * h + first + width] = wfin[k, h, :, :, 0:width].astype(F32).reshape(64, width)
 
     def wide_close(k):
-        arrived(Q.at[0, pl.ds(0, 736)], g_send.at[k])
+        arrived(Q.at[0, pl.ds(0, 736 if k == 0 else 368)], g_send.at[k])
 
     acc_w[0] = (mm_tn(half_of(A2, 0), half_of(G3, 0)) + mm_tn(half_of(A2, 1), half_of(G3, 1))).reshape(2, 2, 64, 512)
     pair_start(0)
@@ -916,7 +935,7 @@
         arrived(sx.at[r], s_recv.at[r, 3])
         here = sq[r, hi].astype(F32) + sx[r, 0].astype(F32)
         there = sx[r, 1].astype(F32) + sx[r, 2].astype(F32)
-        total = over_groups(here + there, sh.at[r], (h_send.at[2 + r], h_recv.at[2 + r]))
+        total = over_groups(here + there, sh.at[r], (h_send.at[3 + r], h_recv.at[3 + r]))
         sfin[r, quad] = total.astype(BF16)
         for cp in s_give(r):
             cp.start()
@@ -1008,12 +1027,14 @@
         back_first(t, E1[t], H1[t])
         return carry
 
-    def reduce_rows(first, chunks):
-        parts = [v[first : first + chunks].reshape(chunks * ROWS, 256) for v in (G1, F.at[0], F.at[1])]
-        return mm_tn(parts[0], jnp.concatenate(parts[1:], axis=1)).reshape(2, 2, 64, 512)
+    def reduce_rows(first, chunks, w):
+        left = G1[first : first + chunks].reshape(chunks * ROWS, 256)
+        right = F[w, first : first + chunks].reshape(chunks * ROWS, 256)
+        return mm_tn(left, right).reshape(2, 2, 64, 256)
 
     lax.fori_loop(0, OWN, own_back_first, 0)
-    acc_w[1] = reduce_rows(0, OWN)
+    for w in range(2):
+        acc_w[1 + w, :, :, :, 0:256] = reduce_rows(0, OWN, w)
     swap_add(0)
     lax.fori_loop(0, OWN, input_term, 0)
     ig_there[0].start()
@@ -1027,19 +1048,23 @@
     arrived(e1r.at[pl.ds(0, 4)], x_recv.at[8])
     arrived(e1r.at[pl.ds(4, OWN - 4)], x_recv.at[9])
     lax.fori_loop(0, OWN, other_back_first, 0)
-    acc_w[1] += reduce_rows(OWN, OWN)
-    pair_start(1)
+    for w in range(2):
+        acc_w[1 + w, :, :, :, 0:256] += reduce_rows(OWN, OWN, w)
+        pair_start(1 + w)
     s_four_add(0)
     lax.fori_loop(OWN, BOTH, input_term, 0)
     ig_there[1].start()
     pair_add(1)
+    pair_add(2)
     s_four_add(1)
     s_four_add(2)
     s_swap_add(0)
     four_add(1)
+    four_add(2)
     s_swap_add(1)
     s_swap_add(2)
     swap_add(1)
+    swap_add(2)
 
     def own64(v):
         half = jnp.where(hi == 0, v[:, 0:128], v[:, 128:256])
@@ -1066,9 +1091,11 @@
     for r in range(3):
         s_take(r)
     wide_take(1, rg_out)
+    wide_take(2, rg_out)
 
     wide_close(0)
     wide_close(1)
+    wide_close(2)
     for r in range(3):
         s_close(r)
     arrived(RES, o_send.at[1])
@@ -1150,17 +1177,17 @@
         V((BOTH, ROWS, 256), BF16),
         V((256, FLAT), BF16),
         V((chunks, ROWS), F32),
-        V((2, 2, 2, 64, 512), F32),
-        V((2, 2, 64, 512), BF16),
-        V((2, 2, 64, 512), BF16),
-        V((2, 2, 4, 16, 512), F32),
-        V((2, 4, 2, 16, 512), BF16),
-        V((2, 4, 2, 16, 512), BF16),
-        V((2, 2, 16, 512), BF16),
-        V((2, 2, 16, 512), BF16),
-        V((2, n_hi, 2, 16, 512), BF16),
-        V((2, 2, 16, 512), BF16),
-        V((2, 2, 4, 16, 512), BF16),
+        V((3, 2, 2, 64, 512), F32),
+        V((3, 2, 64, 512), BF16),
+        V((3, 2, 64, 512), BF16),
+        V((3, 2, 4, 16, 512), F32),
+        V((3, 4, 2, 16, 512), BF16),
+        V((3, 4, 2, 16, 512), BF16),
+        V((3, 2, 16, 512), BF16),
+        V((3, 2, 16, 512), BF16),
+        V((3, n_hi, 2, 16, 512), BF16),
+        V((3, 2, 16, 512), BF16),
+        V((3, 2, 4, 16, 512), BF16),
         V((3, 2, 2, 64, 768), F32),
         V((3, 2, 64, 768), BF16),
         V((3, 2, 64, 768), BF16),
@@ -1186,12 +1213,12 @@
         DMA((11,)),
         DMA((2,)),
         DMA((2,)),
-        DMA((2,)),
-        DMA((2, 4)),
+        DMA((3,)),
+        DMA((3, 4)),
         DMA((3,)),
         DMA((3, 5)),
-        DMA((5, n_hi) if n_hi > 1 else (1, 1)),
-        DMA((5, n_hi) if n_hi > 1 else (1, 1)),
+        DMA((6, n_hi) if n_hi > 1 else (1, 1)),
+        DMA((6, n_hi) if n_hi > 1 else (1, 1)),
     ]
     wide = V((chunks, ROWS, lanes), BF16)
     made = pl.pallas_call(

time: 85.7 us -> 85.4 us (level)
  no operation moved by 1% of the time
where the time goes in v9:
time: 85.4 us; the launch traced here: 85.2 us
  Pallas kernels  84.6 us (99%)
    pallas_call x1, Pallas kernels, block(): pl.pallas_call(functools.partial(kernel, n_pix, n_ch), out_shape=(wide, w...  82.4 us
    pallas_call x1, Pallas kernels, block(): pl.pallas_call(finish, out_shape=tuple((jax.ShapeDtypeStruct(v.shape, v.d...  2.17 us

profile of v9, /device:TPU:0, one launch (start us, length us, event | category | flops | bytes accessed | tf_op | source)
XLA Modules:
  0.0 85.2 jit_solution(8010714734859922236)
XLA Ops:
  0.6 82.4 %bottleneck.1 = (bf16[28,112,256]{2,1,0:T(8,128)(2,1)S(1)}, bf16[28,112,256]{2,1,0:T(8,128)(2,1)S(1)}, f32[64,1024]{1,0:T(8,128)S(1)}, f32[9,64,256]{2,1,0:T(8,1...) custom-call(bf16[28,112,256]{2,1,0:T(8,128)(2,1)} %bitcast.12, bf16[28,112,256]{2,1,0:T(8,128)(2,1)} %bitcast.13, ...), custom_call_target="tpu_custom_call" | custom-call | tf_op jit(solution)/shard_map/bottleneck/pallas_call | solution.py:1224
  83.1 2.2 %outputs.1 = (bf16[28,112,256]{2,1,0:T(8,128)(2,1)}, bf16[28,112,256]{2,1,0:T(8,128)(2,1)}, f32[64,1024]{1,0:T(8,128)}, f32[9,64,256]{2,1,0:T(8,128)}, f32[64,10...) custom-call(bf16[28,112,256]{2,1,0:T(8,128)(2,1)S(1)} %get-tuple-ele, ...), custom_call_target="tpu_custom_call" | custom-call | tf_op jit(solution)/shard_map/outputs/pallas_call | solution.py:1252

commit v10 on v9

--- a/solution.py
+++ b/solution.py
@@ -249,7 +249,7 @@
         for s, part in halves
     ]
     cx = [
-        remote(cot.at[pl.ds(theirs + part, OWN)], C.at[lo, pl.ds(OWN * s, OWN)], fx_send.at[1], fx_recv.at[2], beside)
+        remote(cot.at[pl.ds(theirs + part, OWN)], C.at[lo, pl.ds(OWN * s, OWN)], fx_send.at[0], fx_recv.at[2], beside)
         for s, part in halves
     ]
     far, near, last_one = (1 - hi) * 2 + lo, hi * 2 + 1 - lo, (1 - hi) * 2 + 1 - lo
@@ -413,7 +413,7 @@
             None,
             1 + jnp.where(t < 5, 0, 1),
         )[kind]
-        return remote(src.at[t], dst.at[t], x_send.at[kind], x_recv.at[got], across)
+        return remote(src.at[t], dst.at[t], x_send.at[0], x_recv.at[got], across)
 
     def send_first(h, kind):
         w = W1T[pl.ds(2 * h, 2)].reshape(128, 512)
@@ -543,7 +543,7 @@
 
     arrived(W2T.at[near], w_recv.at[8])
     arrived(W2T.at[last_one], w_recv.at[9])
-    h1x = [remote(h1b, h1o, x_send.at[4], x_recv.at[10], across)]
+    h1x = [remote(h1b, h1o, x_send.at[1], x_recv.at[10], across)]
 
     def conv(first, rows):
         taps = [PC[PAD * r + first : PAD * r + first + rows, :] for r in range(3)]
@@ -859,7 +859,7 @@
     k2_0 = -a2_gain * shift2 * inv_n2 - k2_h * avg2
 
     def s_pair(r):
-        return [remote(sp.at[r, h], sc.at[r, h], s_send.at[r], s_recv.at[r, 0], beside) for h in range(2)]
+        return [remote(sp.at[r, h], sc.at[r, h], s_send.at[0], s_recv.at[r, 0], beside) for h in range(2)]
 
     def s_four(r):
         copies = []
@@ -867,30 +867,30 @@
             q = lax.rem(quad + t, 4)
             copies.append(
                 remote(
-                    sb.at[r, lax.rem(q, 2), q // 2], sr.at[r, low, high], s_send.at[r], s_recv.at[r, 1], group_at(t)
+                    sb.at[r, lax.rem(q, 2), q // 2], sr.at[r, low, high], s_send.at[0], s_recv.at[r, 1], group_at(t)
                 )
             )
         return copies
 
     def s_low(r):
-        return remote(sb.at[r, 1 - low], sr.at[r, 0], s_send.at[r], s_recv.at[r, 1], next_group)
+        return remote(sb.at[r, 1 - low], sr.at[r, 0], s_send.at[0], s_recv.at[r, 1], next_group)
 
     def s_high(r):
         to = (g_hi * n_lo + top * 4 + (1 - high) * 2 + low, me_c)
-        return remote(sr.at[r, 1, 0], sz.at[r], s_send.at[r], s_recv.at[r, 2], to)
+        return remote(sr.at[r, 1, 0], sz.at[r], s_send.at[0], s_recv.at[r, 2], to)
 
     def s_swap(r):
         up = group_at(0, True)[0]
         aside = (1 - hi) * 2 + lo
         return [
-            remote(sq.at[r, 1 - hi], sx.at[r, 0], s_send.at[r], s_recv.at[r, 3], (me_p, aside)),
-            remote(sq.at[r, hi], sx.at[r, 1], s_send.at[r], s_recv.at[r, 3], (up, me_c)),
-            remote(sq.at[r, 1 - hi], sx.at[r, 2], s_send.at[r], s_recv.at[r, 3], (up, aside)),
+            remote(sq.at[r, 1 - hi], sx.at[r, 0], s_send.at[0], s_recv.at[r, 3], (me_p, aside)),
+            remote(sq.at[r, hi], sx.at[r, 1], s_send.at[0], s_recv.at[r, 3], (up, me_c)),
+            remote(sq.at[r, 1 - hi], sx.at[r, 2], s_send.at[0], s_recv.at[r, 3], (up, aside)),
         ]
 
     def s_give(r):
         spot = sfin.at[r, quad]
-        return [remote(spot, spot, s_send.at[r], s_recv.at[r, 4], group_at(t)) for t in range(1, 4)]
+        return [remote(spot, spot, s_send.at[0], s_recv.at[r, 4], group_at(t)) for t in range(1, 4)]
 
     def s_make(r):
         taps = mm(QT[...], PC[PAD * r : PAD * r + FLAT, :])
@@ -946,8 +946,8 @@
         for c in range(3):
             sg_out[3 * r + c] = rows[:, 256 * c : 256 * (c + 1)]
 
-    def s_close(r):
-        arrived(PC.at[pl.ds(0, 320)], s_send.at[r])
+    def s_close():
+        arrived(PC.at[pl.ds(0, 960)], s_send.at[0])
 
     def back_second(t, carry):
         at = pl.ds(pl.multiple_of(t * ROWS, 16), ROWS)
@@ -1096,17 +1096,15 @@
     wide_close(0)
     wide_close(1)
     wide_close(2)
-    for r in range(3):
-        s_close(r)
+    s_close()
     arrived(RES, o_send.at[1])
     for k, ref in enumerate((res_out, ig_out)):
         arrived(ref.at[pl.ds(theirs, BOTH)], o_recv.at[k])
-    arrived(F.at[0], fx_send.at[0])
-    arrived(C.at[0], fx_send.at[1])
+    arrived(F, fx_send.at[0])
     for k, ref in enumerate((W1T.at[pl.ds(0, 3)], W2T.at[pl.ds(0, 2)], W3, W2T.at[0], W3.at[pl.ds(0, 2)], pk.at[pl.ds(0, 3)], kb)):
         arrived(ref, w_send.at[k])
-    for k, ref in enumerate((h1s.at[0], h2s, e2s, e1s, h1b, h1s.at[1])):
-        arrived(ref, x_send.at[k])
+    arrived(F, x_send.at[0])
+    arrived(h1b, x_send.at[1])
     for k, kind, rows in (
         (0, "all", 4),
         (1, "core", 4),
@@ -1201,21 +1199,21 @@
         V((3, n_hi, 16, 768), BF16),
         V((3, 4, 16, 768), BF16),
         DMA((13,)),
-        DMA((2,)),
+        DMA((1,)),
         DMA((3,)),
         DMA((7,)),
         DMA((22,)),
         DMA((7,)),
         DMA((7,)),
+        DMA((1,)),
+        DMA((1,)),
         DMA((2,)),
-        DMA((2,)),
-        DMA((6,)),
         DMA((11,)),
         DMA((2,)),
         DMA((2,)),
         DMA((3,)),
         DMA((3, 4)),
-        DMA((3,)),
+        DMA((1,)),
         DMA((3, 5)),
         DMA((6, n_hi) if n_hi > 1 else (1, 1)),
         DMA((6, n_hi) if n_hi > 1 else (1, 1)),

time: 85.4 us -> 85.3 us (level)
  no operation moved by 1% of the time
where the time goes in v10:
time: 85.3 us; the launch traced here: 85.2 us
  Pallas kernels  84.5 us (99%)
    pallas_call x1, Pallas kernels, block(): pl.pallas_call(functools.partial(kernel, n_pix, n_ch), out_shape=(wide, w...  82.3 us
    pallas_call x1, Pallas kernels, block(): pl.pallas_call(finish, out_shape=tuple((jax.ShapeDtypeStruct(v.shape, v.d...  2.17 us

profile of v10, /device:TPU:0, one launch (start us, length us, event | category | flops | bytes accessed | tf_op | source)
XLA Modules:
  0.0 85.2 jit_solution(13166610913214709388)
XLA Ops:
  0.6 82.3 %bottleneck.1 = (bf16[28,112,256]{2,1,0:T(8,128)(2,1)S(1)}, bf16[28,112,256]{2,1,0:T(8,128)(2,1)S(1)}, f32[64,1024]{1,0:T(8,128)S(1)}, f32[9,64,256]{2,1,0:T(8,1...) custom-call(bf16[28,112,256]{2,1,0:T(8,128)(2,1)} %bitcast.12, bf16[28,112,256]{2,1,0:T(8,128)(2,1)} %bitcast.13, ...), custom_call_target="tpu_custom_call" | custom-call | tf_op jit(solution)/shard_map/bottleneck/pallas_call | solution.py:1222
  83.0 2.2 %outputs.1 = (bf16[28,112,256]{2,1,0:T(8,128)(2,1)}, bf16[28,112,256]{2,1,0:T(8,128)(2,1)}, f32[64,1024]{1,0:T(8,128)}, f32[9,64,256]{2,1,0:T(8,128)}, f32[64,10...) custom-call(bf16[28,112,256]{2,1,0:T(8,128)(2,1)S(1)} %get-tuple-ele, ...), custom_call_target="tpu_custom_call" | custom-call | tf_op jit(solution)/shard_map/outputs/pallas_call | solution.py:1250
